TPU v7x, 32 devices: a whole 2x2x4 slice. The times are simulated.
32 devices in a mesh: gy: 8 (over z, y), gz: 4 (over x, core).
Axes of the slice: x: 2, y: 2, z: 4, core: 2. Of those that a mesh axis runs over, the one named last changes fastest.
Arguments:
- image: float32 [16, 128, 2048], P(None, 'gy', 'gz'), may hold values from -6 to 6
- seeds: int32 [16, 128, 2048], P(None, 'gy', 'gz'), may hold values from 0 to 2, as said below
Outputs:
- potentials: float32 [2, 16, 128, 2048], P(None, None, 'gy', 'gz')
Inputs may be any that keep to these rules, and one draw needn't show every extreme that they name: Every voxel is unlabeled, pore or grain; about a fifth of the voxels are seeds.
All inputs are finite; a program needn't handle non-finite values.
Results may differ from a plain program's by a relative error of at most 0.0001.
Values sent between devices are 32-bit elements; how exact they have to be, the bound alone decides.
No kernel may reach another device: no remote copies, remote signals or barrier semaphores. Data moves between devices by JAX's collectives and lax.ppermute only.
A program may use at most 64 MiB of HBM per device.

v0:
```python
import math

import jax
import jax.numpy as jnp
from jax import lax
from jax.sharding import PartitionSpec as P

ITERS = 4


edge_beta = 60.0
edge_floor = 0.05


def padded(array, sides, width):
    for axis, dim in sides:
        peers, length = (lax.axis_size(axis), array.shape[dim])
        up = [(i, (i + 1) % peers) for i in range(peers - 1)]
        down = [(j, i) for i, j in up]
        last = lax.slice_in_dim(array, length - width, length, axis=dim)
        initial = lax.slice_in_dim(array, 0, width, axis=dim)
        before = lax.ppermute(last, axis, up)
        after = lax.ppermute(initial, axis, down)
        array = jnp.concatenate([before, array, after], axis=dim)
    return array


def gauss_taps():
    raw = [math.exp(-0.5 * k * k) for k in range(-2, 3)]
    total = sum(raw)
    return [value / total for value in raw]


def valid_smooth(field, axis):
    taps = gauss_taps()
    length = field.shape[axis] - 4
    result = taps[0] * lax.slice_in_dim(field, 0, length, axis=axis)
    for k in range(1, 5):
        result = result + taps[k] * lax.slice_in_dim(field, k, k + length, axis=axis)
    return result


def depth_smooth(field):
    return valid_smooth(jnp.pad(field, ((2, 2), (0, 0), (0, 0))), 0)


def edge_weights(step, first, total, count):
    places = first - 1 + jnp.arange(count, dtype=jnp.int32)
    inside = (places >= 0) & (places <= total - 2)
    return (inside, edge_floor + jnp.exp(-edge_beta * step * step))


def inner_local(left, right):
    return jnp.sum(left * right, axis=(1, 2, 3))


def paired_global(resid, precond, image_pre):
    return lax.psum((inner_local(resid, precond), inner_local(image_pre, precond)), ("gy", "gz"))


def on_device(image, seeds):
    rows = image.shape[1]
    cols = image.shape[2]
    wide = padded(image, (("gy", 1), ("gz", 2)), 2)
    smooth_core = valid_smooth(valid_smooth(depth_smooth(wide), 1), 2)
    smooth_full = padded(smooth_core, (("gy", 1), ("gz", 2)), 1)
    core = smooth_full[:, 1:-1, 1:-1]
    depth_step = core[1:] - core[:-1]
    w_depth = jnp.pad(
        edge_floor + jnp.exp(-edge_beta * depth_step * depth_step), ((0, 1), (0, 0), (0, 0))
    )
    w_depth_back = jnp.pad(w_depth, ((1, 0), (0, 0), (0, 0)))[:-1]
    row_field = smooth_full[:, :, 1:-1]
    row_step = row_field[:, 1:, :] - row_field[:, :-1, :]
    row_inside, row_raw = edge_weights(
        row_step, lax.axis_index("gy") * rows, rows * lax.axis_size("gy"), rows + 1
    )
    w_rows = jnp.where(row_inside[None, :, None], row_raw, 0.0)
    col_field = smooth_full[:, 1:-1, :]
    col_step = col_field[:, :, 1:] - col_field[:, :, :-1]
    col_inside, col_raw = edge_weights(
        col_step, lax.axis_index("gz") * cols, cols * lax.axis_size("gz"), cols + 1
    )
    w_cols = jnp.where(col_inside[None, None, :], col_raw, 0.0)
    w_row_up = w_rows[:, 1:, :]
    w_row_down = w_rows[:, :-1, :]
    w_col_up = w_cols[:, :, 1:]
    w_col_down = w_cols[:, :, :-1]
    degree = w_depth + w_depth_back + w_row_up + w_row_down + w_col_up + w_col_down

    def neighbours(fields):
        framed = padded(fields, (("gy", 2), ("gz", 3)), 1)
        middle = framed[:, :, 1:-1, 1:-1]
        deep_pad = jnp.pad(middle, ((0, 0), (1, 1), (0, 0), (0, 0)))
        total = w_depth * deep_pad[:, 2:] + w_depth_back * deep_pad[:, :-2]
        total = total + w_row_up * framed[:, :, 2:, 1:-1] + w_row_down * framed[:, :, :-2, 1:-1]
        total = total + w_col_up * framed[:, :, 1:-1, 2:] + w_col_down * framed[:, :, 1:-1, :-2]
        return total

    free = (seeds == 0).astype(jnp.float32)
    marks = jnp.stack([(seeds == 1).astype(jnp.float32), (seeds == 2).astype(jnp.float32)])

    def operate(fields):
        return free * (degree * fields - neighbours(free * fields)) + (1.0 - free) * fields

    rhs = free * neighbours(marks)
    diag = free * degree + (1.0 - free)
    solution = jnp.zeros_like(rhs)
    resid = rhs
    precond = resid / diag
    image_pre = operate(precond)
    rz_now, curve = paired_global(resid, precond, image_pre)
    alpha = rz_now / curve
    direction = precond
    along = image_pre
    for step in range(ITERS):
        solution = solution + alpha[:, None, None, None] * direction
        resid = resid - alpha[:, None, None, None] * along
        if step + 1 < ITERS:
            precond = resid / diag
            image_pre = operate(precond)
            rz_next, curve = paired_global(resid, precond, image_pre)
            ratio = rz_next / rz_now
            alpha = rz_next / (curve - ratio * rz_next / alpha)
            direction = precond + ratio[:, None, None, None] * direction
            along = image_pre + ratio[:, None, None, None] * along
            rz_now = rz_next
    return solution + marks


def solution(mesh):
    return jax.shard_map(
        on_device,
        mesh=mesh,
        in_specs=(P(None, "gy", "gz"), P(None, "gy", "gz")),
        out_specs=P(None, None, "gy", "gz"),
        check_vma=False,
    )
```

profile of v0, /device:TPU:0, one launch (start us, length us, event | category | flops | bytes accessed | tf_op | source)
XLA Modules:
  0.0 325.2 jit_solution(13741433576189150765)
XLA Ops:
  1.1 4.9 %collective-permute-start = (f32[16,2,512]{2,1,0:T(2,128)S(1)}, f32[16,2,512]{2,1,0:T(2,128)S(1)}, u32[]{:S(2)}, u32[]{:S(2)}) collective-permute-start(f32[16,2,512]{2,1,0:T(2,128)S(1)} %get-tuple-element.75), channel_id=1, source_target_pairs={{0,4},{4,8},{8,12},{12,16},{16,20},{20,24},{24,28},{1,5},{5,9},{9,... | collective-permute-start | bytes 196616 | tf_op jit(solution)/shard_map/ppermute | solution.py:22
  8.9 4.7 %collective-permute-start.7 = (f32[2,16,1,512]{3,2,1,0:T(1,128)S(1)}, f32[2,16,1,512]{3,2,1,0:T(1,128)S(1)}, u32[]{:S(2)}, u32[]{:S(2)}) collective-permute-start(f32[2,16,1,512]{3,2,1,0:T(1,128)S(1)} %get-tuple-element.60), channel_id=1, source_target_pairs={{0,4},{4,8},{8,12},{12,16},{16,20},{20,24},{24,28},{1,5},{5,9},{9,... | collective-permute-start | bytes 196616 | tf_op jit(solution)/shard_map/ppermute | solution.py:22
  21.7 4.0 %collective-permute-start.11 = (f32[2,16,18,1]{3,2,1,0:T(8,128)S(1)}, f32[2,16,18,1]{3,2,1,0:T(8,128)S(1)}, u32[]{:S(2)}, u32[]{:S(2)}) collective-permute-start(f32[2,16,18,1]{3,2,1,0:T(8,128)S(1)} %get-tuple-element.51), channel_id=1, source_target_pairs={{0,1},{1,2},{2,3},{4,5},{5,6},{6,7},{8,9},{9,10},{10,11},{12,13},{... | collective-permute-start | bytes 6920 | tf_op jit(solution)/shard_map/ppermute | solution.py:22
  28.5 5.0 %collective-permute-start.5 = (f32[16,1,512]{2,1,0:T(1,128)S(1)}, f32[16,1,512]{2,1,0:T(1,128)S(1)}, u32[]{:S(2)}, u32[]{:S(2)}) collective-permute-start(f32[16,1,512]{2,1,0:T(1,128)S(1)} %get-tuple-element.73), channel_id=1, source_target_pairs={{0,4},{4,8},{8,12},{12,16},{16,20},{20,24},{24,28},{1,5},{5,9},{9,... | collective-permute-start | bytes 98312 | tf_op jit(solution)/shard_map/ppermute | solution.py:22
  35.0 5.1 %collective-permute-done.4 = f32[16,1,512]{2,1,0:T(1,128)S(1)} collective-permute-done((f32[16,1,512]{2,1,0:T(1,128)S(1)}, f32[16,1,512]{2,1,0:T(1,128)S(1)}, u32[]{:S(2)}, u32[]{:S(2)}) %collective-permute-start.4) | collective-permute-done | bytes 32800 | tf_op jit(solution)/shard_map/ppermute | solution.py:23
  41.6 3.1 collective-permute-start.9
  49.3 4.9 %collective-permute-start.13 = (f32[2,16,1,512]{3,2,1,0:T(1,128)S(1)}, f32[2,16,1,512]{3,2,1,0:T(1,128)S(1)}, u32[]{:S(2)}, u32[]{:S(2)}) collective-permute-start(f32[2,16,1,512]{3,2,1,0:T(1,128)S(1)} %get-tuple-element.58), channel_id=1, source_target_pairs={{0,4},{4,8},{8,12},{12,16},{16,20},{20,24},{24,28},{1,5},{5,9},{9,... | collective-permute-start | bytes 196616 | tf_op jit(solution)/shard_map/ppermute | solution.py:22
  56.0 4.3 %collective-permute-done.12 = f32[2,16,1,512]{3,2,1,0:T(1,128)S(1)} collective-permute-done((f32[2,16,1,512]{3,2,1,0:T(1,128)S(1)}, f32[2,16,1,512]{3,2,1,0:T(1,128)S(1)}, u32[]{:S(2)}, u32[]{:S(2)}) %collective-permute-start.12) | collective-permute-done | bytes 65568 | tf_op jit(solution)/shard_map/ppermute | solution.py:23
  61.9 4.4 %collective-permute-start.15 = (f32[2,16,18,1]{3,2,1,0:T(8,128)S(1)}, f32[2,16,18,1]{3,2,1,0:T(8,128)S(1)}, u32[]{:S(2)}, u32[]{:S(2)}) collective-permute-start(f32[2,16,18,1]{3,2,1,0:T(8,128)S(1)} %get-tuple-element.49), channel_id=1, source_target_pairs={{0,1},{1,2},{2,3},{4,5},{5,6},{6,7},{8,9},{9,10},{10,11},{12,13},{... | collective-permute-start | bytes 6920 | tf_op jit(solution)/shard_map/ppermute | solution.py:22
  67.6 3.1 multiply_reduce_fusion.5
  70.7 48.0 %all-reduce.11 = (f32[2]{0:T(128)S(1)}, f32[2]{0:T(128)S(1)}) all-reduce(f32[2]{0:T(128)S(1)} %get-tuple-element.10, f32[2]{0:T(128)S(1)} %get-tuple-element.9), channel_id=1, replica_groups=mesh['gy'=8,'gz'=4] {'gy','gz'}, use_global_device_ids=true, to_apply=%region_1.2 | all-reduce | flops 4 | bytes 32 | tf_op jit(solution)/shard_map/psum | solution.py:58
  121.0 4.4 %collective-permute-start.17 = (f32[2,16,1,512]{3,2,1,0:T(1,128)S(1)}, f32[2,16,1,512]{3,2,1,0:T(1,128)S(1)}, u32[]{:S(2)}, u32[]{:S(2)}) collective-permute-start(f32[2,16,1,512]{3,2,1,0:T(1,128)S(1)} %get-tuple-element.56), channel_id=1, source_target_pairs={{0,4},{4,8},{8,12},{12,16},{16,20},{20,24},{24,28},{1,5},{5,9},{9,... | collective-permute-start | bytes 196616 | tf_op jit(solution)/shard_map/ppermute | solution.py:22
  127.3 4.3 %collective-permute-done.16 = f32[2,16,1,512]{3,2,1,0:T(1,128)S(1)} collective-permute-done((f32[2,16,1,512]{3,2,1,0:T(1,128)S(1)}, f32[2,16,1,512]{3,2,1,0:T(1,128)S(1)}, u32[]{:S(2)}, u32[]{:S(2)}) %collective-permute-start.16) | collective-permute-done | bytes 65568 | tf_op jit(solution)/shard_map/ppermute | solution.py:23
  133.1 3.1 collective-permute-start.19
  137.5 3.1 multiply_reduce_fusion.3
  140.6 45.6 %all-reduce.10 = (f32[2]{0:T(128)S(1)}, f32[2]{0:T(128)S(1)}) all-reduce(f32[2]{0:T(128)S(1)} %get-tuple-element.8, f32[2]{0:T(128)S(1)} %get-tuple-element.7), channel_id=1, replica_groups=mesh['gy'=8,'gz'=4] {'gy','gz'}, use_global_device_ids=true, to_apply=%region_5.6 | all-reduce | flops 4 | bytes 32 | tf_op jit(solution)/shard_map/psum | solution.py:58
  188.9 4.4 %collective-permute-start.21 = (f32[2,16,1,512]{3,2,1,0:T(1,128)S(1)}, f32[2,16,1,512]{3,2,1,0:T(1,128)S(1)}, u32[]{:S(2)}, u32[]{:S(2)}) collective-permute-start(f32[2,16,1,512]{3,2,1,0:T(1,128)S(1)} %get-tuple-element.54), channel_id=1, source_target_pairs={{0,4},{4,8},{8,12},{12,16},{16,20},{20,24},{24,28},{1,5},{5,9},{9,... | collective-permute-start | bytes 196616 | tf_op jit(solution)/shard_map/ppermute | solution.py:22
  195.9 3.7 %collective-permute-done.20 = f32[2,16,1,512]{3,2,1,0:T(1,128)S(1)} collective-permute-done((f32[2,16,1,512]{3,2,1,0:T(1,128)S(1)}, f32[2,16,1,512]{3,2,1,0:T(1,128)S(1)}, u32[]{:S(2)}, u32[]{:S(2)}) %collective-permute-start.20) | collective-permute-done | bytes 65568 | tf_op jit(solution)/shard_map/ppermute | solution.py:23
  205.5 3.1 multiply_reduce_fusion.1
  208.6 45.4 %all-reduce.9 = (f32[2]{0:T(128)S(1)}, f32[2]{0:T(128)S(1)}) all-reduce(f32[2]{0:T(128)S(1)} %get-tuple-element.6, f32[2]{0:T(128)S(1)} %get-tuple-element.5), channel_id=1, replica_groups=mesh['gy'=8,'gz'=4] {'gy','gz'}, use_global_device_ids=true, to_apply=%region_9.10 | all-reduce | flops 4 | bytes 32 | tf_op jit(solution)/shard_map/psum | solution.py:58
  257.2 4.2 %collective-permute-start.25 = (f32[2,16,1,512]{3,2,1,0:T(1,128)S(1)}, f32[2,16,1,512]{3,2,1,0:T(1,128)S(1)}, u32[]{:S(2)}, u32[]{:S(2)}) collective-permute-start(f32[2,16,1,512]{3,2,1,0:T(1,128)S(1)} %get-tuple-element.52), channel_id=1, source_target_pairs={{0,4},{4,8},{8,12},{12,16},{16,20},{20,24},{24,28},{1,5},{5,9},{9,... | collective-permute-start | bytes 196616 | tf_op jit(solution)/shard_map/ppermute | solution.py:22
  263.8 3.7 %collective-permute-done.24 = f32[2,16,1,512]{3,2,1,0:T(1,128)S(1)} collective-permute-done((f32[2,16,1,512]{3,2,1,0:T(1,128)S(1)}, f32[2,16,1,512]{3,2,1,0:T(1,128)S(1)}, u32[]{:S(2)}, u32[]{:S(2)}) %collective-permute-start.24) | collective-permute-done | bytes 65568 | tf_op jit(solution)/shard_map/ppermute | solution.py:23
  275.9 45.4 %all-reduce.8 = (f32[2]{0:T(128)S(1)}, f32[2]{0:T(128)S(1)}) all-reduce(f32[2]{0:T(128)S(1)} %multiply_reduce_fusion, f32[2]{0:T(128)S(1)} %fusion.69), channel_id=1, replica_groups=mesh['gy'=8,'gz'=4] {'gy','gz'}, use_global_device_ids=true, to_apply=%region_13.14 | all-reduce | flops 4 | bytes 32 | tf_op jit(solution)/shard_map/psum | solution.py:58
  321.3 3.9 %add_add_fusion = f32[2,16,16,512]{3,2,1,0:T(8,128)} fusion(f32[2]{0:T(128)S(1)} %get-tuple-element.20, f32[2]{0:T(128)S(1)} %get-tuple-element.19, f32[2]{0:T(128)S(1)} %get-tuple-element.25, f32[2]{0:T(128)S(1)} %get-tuple-element.23, f32[2]{0:T(128)S(1)} %get-tuple-element.31, f32[2]{0:T(128)S(1)} %get-tuple-element.29, f32[2]{0:T(128)S(1)} %div.58, ...), kind=kLoop, calls=%fused_computation.124 | loop fusion | flops 5242880 | bytes 6029368 | tf_op jit(solution)/shard_map/add | solution.py:128
  (139 shorter events, 58.8 us)
Async XLA Ops:
  1.1 14.8 %collective-permute-start = (f32[16,2,512]{2,1,0:T(2,128)S(1)}, f32[16,2,512]{2,1,0:T(2,128)S(1)}, u32[]{:S(2)}, u32[]{:S(2)}) collective-permute-start(f32[16,2,512]{2,1,0:T(2,128)S(1)} %get-tuple-element.75), channel_id=1, source_target_pairs={{0,4},{4,8},{8,12},{12,16},{16,20},{20,24},{24,28},{1,5},{5,9},{9,... | collective-permute-start | bytes 196616 | tf_op jit(solution)/shard_map/ppermute | solution.py:22
  6.0 9.9 %collective-permute-start.1 = (f32[16,2,512]{2,1,0:T(2,128)S(1)}, f32[16,2,512]{2,1,0:T(2,128)S(1)}, u32[]{:S(2)}, u32[]{:S(2)}) collective-permute-start(f32[16,2,512]{2,1,0:T(2,128)S(1)} %get-tuple-element.76), channel_id=1, source_target_pairs={{4,0},{8,4},{12,8},{16,12},{20,16},{24,20},{28,24},{5,1},{9,5},{13... | collective-permute-start | bytes 196616 | tf_op jit(solution)/shard_map/ppermute | solution.py:23
  8.9 9.8 %collective-permute-start.7 = (f32[2,16,1,512]{3,2,1,0:T(1,128)S(1)}, f32[2,16,1,512]{3,2,1,0:T(1,128)S(1)}, u32[]{:S(2)}, u32[]{:S(2)}) collective-permute-start(f32[2,16,1,512]{3,2,1,0:T(1,128)S(1)} %get-tuple-element.60), channel_id=1, source_target_pairs={{0,4},{4,8},{8,12},{12,16},{16,20},{20,24},{24,28},{1,5},{5,9},{9,... | collective-permute-start | bytes 196616 | tf_op jit(solution)/shard_map/ppermute | solution.py:22
  13.6 6.6 %collective-permute-start.6 = (f32[2,16,1,512]{3,2,1,0:T(1,128)S(1)}, f32[2,16,1,512]{3,2,1,0:T(1,128)S(1)}, u32[]{:S(2)}, u32[]{:S(2)}) collective-permute-start(f32[2,16,1,512]{3,2,1,0:T(1,128)S(1)} %get-tuple-element.61), channel_id=1, source_target_pairs={{4,0},{8,4},{12,8},{16,12},{20,16},{24,20},{28,24},{5,1},{9,5},{13... | collective-permute-start | bytes 196616 | tf_op jit(solution)/shard_map/ppermute | solution.py:23
  16.1 9.6 %collective-permute-start.2 = (f32[16,20,2]{2,1,0:T(8,128)S(1)}, f32[16,20,2]{2,1,0:T(8,128)S(1)}, u32[]{:S(2)}, u32[]{:S(2)}) collective-permute-start(f32[16,20,2]{2,1,0:T(8,128)S(1)} %get-tuple-element.66), channel_id=1, source_target_pairs={{0,1},{1,2},{2,3},{4,5},{5,6},{6,7},{8,9},{9,10},{10,11},{12,13},{... | collective-permute-start | bytes 7688 | tf_op jit(solution)/shard_map/ppermute | solution.py:22
  17.4 8.3 %collective-permute-start.3 = (f32[16,20,2]{2,1,0:T(8,128)S(1)}, f32[16,20,2]{2,1,0:T(8,128)S(1)}, u32[]{:S(2)}, u32[]{:S(2)}) collective-permute-start(f32[16,20,2]{2,1,0:T(8,128)S(1)} %get-tuple-element.67), channel_id=1, source_target_pairs={{1,0},{2,1},{3,2},{5,4},{6,5},{7,6},{9,8},{10,9},{11,10},{13,12},{... | collective-permute-start | bytes 7688 | tf_op jit(solution)/shard_map/ppermute | solution.py:23
  20.4 26.4 %collective-permute-start.10 = (f32[2,16,18,1]{3,2,1,0:T(8,128)S(1)}, f32[2,16,18,1]{3,2,1,0:T(8,128)S(1)}, u32[]{:S(2)}, u32[]{:S(2)}) collective-permute-start(f32[2,16,18,1]{3,2,1,0:T(8,128)S(1)} %get-tuple-element.50), channel_id=1, source_target_pairs={{1,0},{2,1},{3,2},{5,4},{6,5},{7,6},{9,8},{10,9},{11,10},{13,12},{... | collective-permute-start | bytes 6920 | tf_op jit(solution)/shard_map/ppermute | solution.py:23
  21.7 25.1 %collective-permute-start.11 = (f32[2,16,18,1]{3,2,1,0:T(8,128)S(1)}, f32[2,16,18,1]{3,2,1,0:T(8,128)S(1)}, u32[]{:S(2)}, u32[]{:S(2)}) collective-permute-start(f32[2,16,18,1]{3,2,1,0:T(8,128)S(1)} %get-tuple-element.51), channel_id=1, source_target_pairs={{0,1},{1,2},{2,3},{4,5},{5,6},{6,7},{8,9},{9,10},{10,11},{12,13},{... | collective-permute-start | bytes 6920 | tf_op jit(solution)/shard_map/ppermute | solution.py:22
  28.5 6.5 %collective-permute-start.5 = (f32[16,1,512]{2,1,0:T(1,128)S(1)}, f32[16,1,512]{2,1,0:T(1,128)S(1)}, u32[]{:S(2)}, u32[]{:S(2)}) collective-permute-start(f32[16,1,512]{2,1,0:T(1,128)S(1)} %get-tuple-element.73), channel_id=1, source_target_pairs={{0,4},{4,8},{8,12},{12,16},{16,20},{20,24},{24,28},{1,5},{5,9},{9,... | collective-permute-start | bytes 98312 | tf_op jit(solution)/shard_map/ppermute | solution.py:22
  33.5 6.7 %collective-permute-start.4 = (f32[16,1,512]{2,1,0:T(1,128)S(1)}, f32[16,1,512]{2,1,0:T(1,128)S(1)}, u32[]{:S(2)}, u32[]{:S(2)}) collective-permute-start(f32[16,1,512]{2,1,0:T(1,128)S(1)} %get-tuple-element.74), channel_id=1, source_target_pairs={{4,0},{8,4},{12,8},{16,12},{20,16},{24,20},{28,24},{5,1},{9,5},{13... | collective-permute-start | bytes 98312 | tf_op jit(solution)/shard_map/ppermute | solution.py:23
  40.3 4.7 %collective-permute-start.8 = (f32[16,18,1]{2,1,0:T(8,128)S(1)}, f32[16,18,1]{2,1,0:T(8,128)S(1)}, u32[]{:S(2)}, u32[]{:S(2)}) collective-permute-start(f32[16,18,1]{2,1,0:T(8,128)S(1)} %get-tuple-element.68), channel_id=1, source_target_pairs={{1,0},{2,1},{3,2},{5,4},{6,5},{7,6},{9,8},{10,9},{11,10},{13,12},{... | collective-permute-start | bytes 3464 | tf_op jit(solution)/shard_map/ppermute | solution.py:23
  49.3 6.8 %collective-permute-start.13 = (f32[2,16,1,512]{3,2,1,0:T(1,128)S(1)}, f32[2,16,1,512]{3,2,1,0:T(1,128)S(1)}, u32[]{:S(2)}, u32[]{:S(2)}) collective-permute-start(f32[2,16,1,512]{3,2,1,0:T(1,128)S(1)} %get-tuple-element.58), channel_id=1, source_target_pairs={{0,4},{4,8},{8,12},{12,16},{16,20},{20,24},{24,28},{1,5},{5,9},{9,... | collective-permute-start | bytes 196616 | tf_op jit(solution)/shard_map/ppermute | solution.py:22
  54.1 6.2 %collective-permute-start.12 = (f32[2,16,1,512]{3,2,1,0:T(1,128)S(1)}, f32[2,16,1,512]{3,2,1,0:T(1,128)S(1)}, u32[]{:S(2)}, u32[]{:S(2)}) collective-permute-start(f32[2,16,1,512]{3,2,1,0:T(1,128)S(1)} %get-tuple-element.59), channel_id=1, source_target_pairs={{4,0},{8,4},{12,8},{16,12},{20,16},{24,20},{28,24},{5,1},{9,5},{13... | collective-permute-start | bytes 196616 | tf_op jit(solution)/shard_map/ppermute | solution.py:23
  60.5 5.7 %collective-permute-start.14 = (f32[2,16,18,1]{3,2,1,0:T(8,128)S(1)}, f32[2,16,18,1]{3,2,1,0:T(8,128)S(1)}, u32[]{:S(2)}, u32[]{:S(2)}) collective-permute-start(f32[2,16,18,1]{3,2,1,0:T(8,128)S(1)} %get-tuple-element.48), channel_id=1, source_target_pairs={{1,0},{2,1},{3,2},{5,4},{6,5},{7,6},{9,8},{10,9},{11,10},{13,12},{... | collective-permute-start | bytes 6920 | tf_op jit(solution)/shard_map/ppermute | solution.py:23
  61.9 5.7 %collective-permute-start.15 = (f32[2,16,18,1]{3,2,1,0:T(8,128)S(1)}, f32[2,16,18,1]{3,2,1,0:T(8,128)S(1)}, u32[]{:S(2)}, u32[]{:S(2)}) collective-permute-start(f32[2,16,18,1]{3,2,1,0:T(8,128)S(1)} %get-tuple-element.49), channel_id=1, source_target_pairs={{0,1},{1,2},{2,3},{4,5},{5,6},{6,7},{8,9},{9,10},{10,11},{12,13},{... | collective-permute-start | bytes 6920 | tf_op jit(solution)/shard_map/ppermute | solution.py:22
  121.0 6.3 %collective-permute-start.17 = (f32[2,16,1,512]{3,2,1,0:T(1,128)S(1)}, f32[2,16,1,512]{3,2,1,0:T(1,128)S(1)}, u32[]{:S(2)}, u32[]{:S(2)}) collective-permute-start(f32[2,16,1,512]{3,2,1,0:T(1,128)S(1)} %get-tuple-element.56), channel_id=1, source_target_pairs={{0,4},{4,8},{8,12},{12,16},{16,20},{20,24},{24,28},{1,5},{5,9},{9,... | collective-permute-start | bytes 196616 | tf_op jit(solution)/shard_map/ppermute | solution.py:22
  125.4 6.2 %collective-permute-start.16 = (f32[2,16,1,512]{3,2,1,0:T(1,128)S(1)}, f32[2,16,1,512]{3,2,1,0:T(1,128)S(1)}, u32[]{:S(2)}, u32[]{:S(2)}) collective-permute-start(f32[2,16,1,512]{3,2,1,0:T(1,128)S(1)} %get-tuple-element.57), channel_id=1, source_target_pairs={{4,0},{8,4},{12,8},{16,12},{20,16},{24,20},{28,24},{5,1},{9,5},{13... | collective-permute-start | bytes 196616 | tf_op jit(solution)/shard_map/ppermute | solution.py:23
  133.1 4.4 %collective-permute-start.19 = (f32[2,16,18,1]{3,2,1,0:T(8,128)S(1)}, f32[2,16,18,1]{3,2,1,0:T(8,128)S(1)}, u32[]{:S(2)}, u32[]{:S(2)}) collective-permute-start(f32[2,16,18,1]{3,2,1,0:T(8,128)S(1)} %get-tuple-element.47), channel_id=1, source_target_pairs={{0,1},{1,2},{2,3},{4,5},{5,6},{6,7},{8,9},{9,10},{10,11},{12,13},{... | collective-permute-start | bytes 6920 | tf_op jit(solution)/shard_map/ppermute | solution.py:22
  188.9 6.9 %collective-permute-start.21 = (f32[2,16,1,512]{3,2,1,0:T(1,128)S(1)}, f32[2,16,1,512]{3,2,1,0:T(1,128)S(1)}, u32[]{:S(2)}, u32[]{:S(2)}) collective-permute-start(f32[2,16,1,512]{3,2,1,0:T(1,128)S(1)} %get-tuple-element.54), channel_id=1, source_target_pairs={{0,4},{4,8},{8,12},{12,16},{16,20},{20,24},{24,28},{1,5},{5,9},{9,... | collective-permute-start | bytes 196616 | tf_op jit(solution)/shard_map/ppermute | solution.py:22
  193.4 6.2 %collective-permute-start.20 = (f32[2,16,1,512]{3,2,1,0:T(1,128)S(1)}, f32[2,16,1,512]{3,2,1,0:T(1,128)S(1)}, u32[]{:S(2)}, u32[]{:S(2)}) collective-permute-start(f32[2,16,1,512]{3,2,1,0:T(1,128)S(1)} %get-tuple-element.55), channel_id=1, source_target_pairs={{4,0},{8,4},{12,8},{16,12},{20,16},{24,20},{28,24},{5,1},{9,5},{13... | collective-permute-start | bytes 196616 | tf_op jit(solution)/shard_map/ppermute | solution.py:23
  201.1 4.4 %collective-permute-start.23 = (f32[2,16,18,1]{3,2,1,0:T(8,128)S(1)}, f32[2,16,18,1]{3,2,1,0:T(8,128)S(1)}, u32[]{:S(2)}, u32[]{:S(2)}) collective-permute-start(f32[2,16,18,1]{3,2,1,0:T(8,128)S(1)} %get-tuple-element.45), channel_id=1, source_target_pairs={{0,1},{1,2},{2,3},{4,5},{5,6},{6,7},{8,9},{9,10},{10,11},{12,13},{... | collective-permute-start | bytes 6920 | tf_op jit(solution)/shard_map/ppermute | solution.py:22
  257.2 6.7 %collective-permute-start.25 = (f32[2,16,1,512]{3,2,1,0:T(1,128)S(1)}, f32[2,16,1,512]{3,2,1,0:T(1,128)S(1)}, u32[]{:S(2)}, u32[]{:S(2)}) collective-permute-start(f32[2,16,1,512]{3,2,1,0:T(1,128)S(1)} %get-tuple-element.52), channel_id=1, source_target_pairs={{0,4},{4,8},{8,12},{12,16},{16,20},{20,24},{24,28},{1,5},{5,9},{9,... | collective-permute-start | bytes 196616 | tf_op jit(solution)/shard_map/ppermute | solution.py:22
  261.3 6.2 %collective-permute-start.24 = (f32[2,16,1,512]{3,2,1,0:T(1,128)S(1)}, f32[2,16,1,512]{3,2,1,0:T(1,128)S(1)}, u32[]{:S(2)}, u32[]{:S(2)}) collective-permute-start(f32[2,16,1,512]{3,2,1,0:T(1,128)S(1)} %get-tuple-element.53), channel_id=1, source_target_pairs={{4,0},{8,4},{12,8},{16,12},{20,16},{24,20},{28,24},{5,1},{9,5},{13... | collective-permute-start | bytes 196616 | tf_op jit(solution)/shard_map/ppermute | solution.py:23
  267.8 4.8 %collective-permute-start.26 = (f32[2,16,18,1]{3,2,1,0:T(8,128)S(1)}, f32[2,16,18,1]{3,2,1,0:T(8,128)S(1)}, u32[]{:S(2)}, u32[]{:S(2)}) collective-permute-start(f32[2,16,18,1]{3,2,1,0:T(8,128)S(1)} %get-tuple-element.42), channel_id=1, source_target_pairs={{1,0},{2,1},{3,2},{5,4},{6,5},{7,6},{9,8},{10,9},{11,10},{13,12},{... | collective-permute-start | bytes 6920 | tf_op jit(solution)/shard_map/ppermute | solution.py:23
  (34 other events, 378.4 us)
where the time goes:
time: 327 us; the launch traced here: 325 us
  blocking collectives  184 us (56%)
  starting transfers between devices  72.8 us (22%)
  other arithmetic  32.9 us (10%)
  waiting for transfers between devices  31.8 us (10%)
    psum x4, blocking collectives, paired_global(): lax.psum((inner_local(resid, precond), inner_local(image_pre, precond)),...  184 us
    ppermute x14, starting transfers between devices, padded(): before = lax.ppermute(last, axis, up)  54.4 us
    ppermute x14, waiting for transfers between devices, padded(): after = lax.ppermute(initial, axis, down)  22.4 us
    ppermute x14, starting transfers between devices, padded(): after = lax.ppermute(initial, axis, down)  18.4 us
    reduce_sum x5, other arithmetic, inner_local(): return jnp.sum(left * right, axis=(1, 2, 3))  11.8 us
    mul x4, other arithmetic, operate(): free * fields  9.48 us
    ppermute x14, waiting for transfers between devices, padded(): before = lax.ppermute(last, axis, up)  9.34 us
  transfers between devices with their start and end apart: 28, of which 16 were waited for; matrix products, arithmetic and copies ran while one was open for 2% of the time, Pallas kernels for 0%

commit v1 on v0

v1 whole, which is shorter than its diff:
```python
import math

import jax
import jax.numpy as jnp
from jax import lax
from jax.experimental import pallas as pl
from jax.experimental.pallas import tpu as pltpu
from jax.sharding import PartitionSpec as P

ITERS = 4
FIELDS = 2
EDGE_BETA = 60.0
EDGE_FLOOR = 0.05
LANES = 128

IMG_BEFORE, IMG_AFTER = ITERS + 2, ITERS + 3
SEED_BEFORE, SEED_AFTER = ITERS, ITERS + 1
UP = IMG_BEFORE + SEED_BEFORE
DOWN = IMG_AFTER + SEED_AFTER
MOMENTS = 2 * ITERS


def gauss_taps():
    raw = [math.exp(-0.5 * k * k) for k in range(-2, 3)]
    total = sum(raw)
    return [value / total for value in raw]


def slab_of(ref, row, parity, rows, half):
    index = pl.ds(row + rows * parity, half, 2 * rows)
    return jnp.concatenate([ref[t, index, :] for t in range(ref.shape[0])], axis=1)


def tile_copies(source, staged, sems, inward=True):
    copies = []
    for t in range(staged.shape[0]):
        ends = (source.at[:, pl.ds(t * LANES, LANES)], staged.at[t])
        copies.append(pltpu.make_async_copy(*(ends if inward else ends[::-1]), sems.at[t]))
    return copies


def stage(pairs):
    copies = [copy for source, staged, sems in pairs for copy in tile_copies(source, staged, sems)]
    for copy in copies:
        copy.start()
    for copy in copies:
        copy.wait()


def pack_kernel(
    rows, half, image_hbm, seeds_hbm, up, down, right, left, image, seeds, image_sem, seeds_sem
):
    stage([(image_hbm, image, image_sem), (seeds_hbm, seeds, seeds_sem)])
    tiles = image.shape[0]
    for parity in range(2):
        for i in range(IMG_BEFORE):
            up[i, parity] = slab_of(image, rows - IMG_BEFORE + i, parity, rows, half)
        for i in range(SEED_BEFORE):
            up[IMG_BEFORE + i, parity] = slab_of(
                seeds, rows - SEED_BEFORE + i, parity, rows, half
            ).astype(jnp.float32)
        for i in range(IMG_AFTER):
            down[i, parity] = slab_of(image, i, parity, rows, half)
        for i in range(SEED_AFTER):
            down[IMG_AFTER + i, parity] = slab_of(seeds, i, parity, rows, half).astype(
                jnp.float32
            )
        lane = lax.broadcasted_iota(jnp.int32, (half, LANES), 1)
        for kind, source in enumerate((image, seeds)):
            head = jnp.zeros((half, LANES), jnp.float32)
            tail = jnp.zeros((half, LANES), jnp.float32)
            for row in range(rows):
                index = pl.ds(row + rows * parity, half, 2 * rows)
                first = source[0, index, :].astype(jnp.float32)
                last = source[tiles - 1, index, :].astype(jnp.float32)
                here = (lane >= 8 * row) & (lane < 8 * row + 8)
                shift = (8 * row) % LANES
                head = jnp.where(here, pltpu.roll(first, shift, 1) if shift else first, head)
                shift = (8 * row + 8) % LANES
                tail = jnp.where(here, pltpu.roll(last, shift, 1) if shift else last, tail)
            left[kind, parity] = head
            right[kind, parity] = tail


def main_kernel(
    rows,
    half,
    image_hbm,
    seeds_hbm,
    above,
    below,
    from_left,
    from_right,
    corner_above,
    corner_below,
    y_out,
    s_out,
    stats,
    x_ext,
    mark,
    smooth,
    scale,
    w_col,
    w_dep,
    w_row,
    w_raw,
    image,
    seeds,
    image_sem,
    seeds_sem,
):
    stage([(image_hbm, image, image_sem), (seeds_hbm, seeds, seeds_sem)])
    cols = image_hbm.shape[1]
    wide = cols + LANES
    gy, gz = lax.axis_index("gy"), lax.axis_index("gz")
    last_gy, last_gz = lax.axis_size("gy") - 1, lax.axis_size("gz") - 1
    t0, t1, t2 = gauss_taps()[:3]
    tile_lane = lax.broadcasted_iota(jnp.int32, (half, LANES), 1)

    def halo_tile(before, before_at, after, after_at):
        after_tile = pltpu.roll(after, (LANES - after_at) % LANES, 1) if after_at else after
        shift = (LANES - 8 - before_at) % LANES
        before_tile = pltpu.roll(before, shift, 1) if shift else before
        return jnp.where(
            tile_lane < 8, after_tile, jnp.where(tile_lane >= LANES - 8, before_tile, 0.0)
        )

    def put_image(index, parity, core, halo):
        x_ext[index, parity, :, 0:cols] = core
        x_ext[index, parity, :, cols:wide] = halo

    def put_seeds(index, parity, core, halo):
        for part, at in ((core, slice(0, cols)), (halo, slice(cols, wide))):
            mark[0, index, parity, :, at] = (part == 1.0).astype(jnp.float32)
            mark[1, index, parity, :, at] = (part == 2.0).astype(jnp.float32)

    def corner(ref, kind, parity, row):
        tile = ref[kind, parity]
        at = (8 * row) % 64
        return halo_tile(tile, 64 + at, tile, at)

    for parity in range(2):
        for i in range(IMG_BEFORE):
            put_image(
                i, parity, above[i, parity], corner(corner_above, 0, parity, rows - IMG_BEFORE + i)
            )
        for i in range(IMG_AFTER):
            put_image(
                IMG_BEFORE + rows + i, parity, below[i, parity], corner(corner_below, 0, parity, i)
            )
        for i in range(SEED_BEFORE):
            put_seeds(
                i,
                parity,
                above[IMG_BEFORE + i, parity],
                corner(corner_above, 1, parity, rows - SEED_BEFORE + i),
            )
        for i in range(SEED_AFTER):
            put_seeds(
                SEED_BEFORE + rows + i,
                parity,
                below[IMG_AFTER + i, parity],
                corner(corner_below, 1, parity, i),
            )
        for row in range(rows):
            put_image(
                IMG_BEFORE + row,
                parity,
                slab_of(image, row, parity, rows, half),
                halo_tile(from_left[0, parity], 8 * row, from_right[0, parity], 8 * row),
            )
            put_seeds(
                SEED_BEFORE + row,
                parity,
                slab_of(seeds, row, parity, rows, half).astype(jnp.float32),
                halo_tile(from_left[1, parity], 8 * row, from_right[1, parity], 8 * row),
            )

    sub = lax.broadcasted_iota(jnp.int32, (half, wide), 0)
    lane = lax.broadcasted_iota(jnp.int32, (half, wide), 1)
    not_first = (sub > 0).astype(jnp.float32)
    not_last = (sub < half - 1).astype(jnp.float32)

    def next_col(v):
        return pltpu.roll(v, wide - 1, 1)

    def prev_col(v):
        return pltpu.roll(v, 1, 1)

    def next_sub(v):
        return pltpu.roll(v, half - 1, 0)

    def prev_sub(v):
        return pltpu.roll(v, 1, 0)

    def smooth_row(r, carry):
        def along_rows(parity):
            return (
                t0 * (x_ext[r, parity] + x_ext[r + 4, parity])
                + t1 * (x_ext[r + 1, parity] + x_ext[r + 3, parity])
                + t2 * x_ext[r + 2, parity]
            )

        even, odd = along_rows(0), along_rows(1)
        even_up, even_dn = not_last * next_sub(even), not_first * prev_sub(even)
        odd_up, odd_dn = not_last * next_sub(odd), not_first * prev_sub(odd)
        deep = (
            t0 * (even_up + even_dn) + t1 * (odd + odd_dn) + t2 * even,
            t0 * (odd_up + odd_dn) + t1 * (even + even_up) + t2 * odd,
        )
        for parity in range(2):
            v = deep[parity]
            one = next_col(v) + prev_col(v)
            two = pltpu.roll(v, wide - 2, 1) + pltpu.roll(v, 2, 1)
            smooth[r, parity] = t0 * two + t1 * one + t2 * v
        return carry

    lax.fori_loop(0, rows + 2 * ITERS + 1, smooth_row, 0)

    cut_col = jnp.where(
        ((lane == wide - 1) & (gz == 0)) | ((lane == cols - 1) & (gz == last_gz)), 0.0, 1.0
    )

    def weight(step):
        return EDGE_FLOOR + jnp.exp((-EDGE_BETA * step) * step)

    def row_edge(i):
        cut = ((i == ITERS - 1) & (gy == 0)) | ((i == ITERS + rows - 1) & (gy == last_gy))
        keep = jnp.where(cut, 0.0, 1.0)
        for parity in range(2):
            w_raw[i, parity] = keep * weight(smooth[i + 1, parity] - smooth[i, parity])

    row_edge(0)
    zero_slab = jnp.zeros((half, wide), jnp.float32)
    scale[0, 0] = zero_slab
    scale[0, 1] = zero_slab

    def weigh_row(i, carry):
        row_edge(i)
        even, odd = smooth[i, 0], smooth[i, 1]
        dep = (weight(odd - even), not_last * weight(next_sub(even) - odd))
        col = [cut_col * weight(next_col(v) - v) for v in (even, odd)]
        dep_back = (prev_sub(dep[1]), dep[0])
        s = []
        for parity in range(2):
            deg = (
                dep[parity]
                + dep_back[parity]
                + w_raw[i, parity]
                + w_raw[i - 1, parity]
                + col[parity]
                + prev_col(col[parity])
            )
            free = 1.0 - mark[0, i, parity] - mark[1, i, parity]
            s.append(free * lax.rsqrt(deg))
        for f in range(FIELDS):
            m = (mark[f, i, 0], mark[f, i, 1])
            lower = (dep[0] * m[1] + prev_sub(dep[1] * m[1]), dep[1] * next_sub(m[0]) + dep[0] * m[0])
            for parity in range(2):
                total = (
                    lower[parity]
                    + col[parity] * next_col(m[parity])
                    + prev_col(col[parity] * m[parity])
                    + w_raw[i, parity] * mark[f, i + 1, parity]
                    + w_raw[i - 1, parity] * mark[f, i - 1, parity]
                )
                y_out[0, f, i, parity] = s[parity] * total
        w_dep[i, 0] = dep[0] * s[0] * s[1]
        w_dep[i, 1] = dep[1] * s[1] * next_sub(s[0])
        for parity in range(2):
            w_col[i, parity] = col[parity] * s[parity] * next_col(s[parity])
            w_row[i - 1, parity] = w_raw[i - 1, parity] * s[parity] * scale[i - 1, parity]
            scale[i, parity] = s[parity]
        return carry

    lax.fori_loop(1, rows + 2 * ITERS, weigh_row, 0)

    def fold(a, b):
        total = None
        for parity in range(2):
            for at in range(0, cols, LANES):
                part = a[parity][:, at : at + LANES] * b[parity][:, at : at + LANES]
                total = part if total is None else total + part
        return total

    def apply_row(level, f, i):
        even, odd = y_out[level - 1, f, i, 0], y_out[level - 1, f, i, 1]
        dep = (w_dep[i, 0], w_dep[i, 1])
        lower = (
            dep[0] * odd + prev_sub(dep[1] * odd),
            dep[1] * next_sub(even) + dep[0] * even,
        )
        fresh = []
        for parity, v in enumerate((even, odd)):
            col = w_col[i, parity]
            total = (
                lower[parity]
                + col * next_col(v)
                + prev_col(col * v)
                + w_row[i, parity] * y_out[level - 1, f, i + 1, parity]
                + w_row[i - 1, parity] * y_out[level - 1, f, i - 1, parity]
            )
            y_out[level, f, i, parity] = total
            fresh.append(total)
        return (even, odd), fresh

    zero = jnp.zeros((half, LANES), jnp.float32)
    sums = []
    for level in range(1, ITERS):

        def outer_row(i, carry, level=level):
            for f in range(FIELDS):
                apply_row(level, f, i)
            return carry

        def core_row(i, carry, level=level):
            carry = list(carry)
            out = []
            for f in range(FIELDS):
                old, new = apply_row(level, f, i)
                pairs = [(old, new), (new, new)]
                if level == 1:
                    pairs = [(old, old)] + pairs
                for a, b in pairs:
                    out.append(carry[len(out)] + fold(a, b))
            return tuple(out)

        count = 3 if level == 1 else 2
        lax.fori_loop(level + 1, ITERS, outer_row, 0)
        acc = lax.fori_loop(ITERS, ITERS + rows, core_row, (zero,) * (count * FIELDS))
        lax.fori_loop(ITERS + rows, rows + 2 * ITERS - level, outer_row, 0)
        sums.append([acc[:count], acc[count:]])

    def edge_row(i, carry):
        out = []
        for f in range(FIELDS):
            even, odd = y_out[ITERS - 1, f, i, 0], y_out[ITERS - 1, f, i, 1]
            forward = (
                w_dep[i, 0] * odd + w_col[i, 0] * next_col(even)
                + w_row[i, 0] * y_out[ITERS - 1, f, i + 1, 0],
                w_dep[i, 1] * next_sub(even) + w_col[i, 1] * next_col(odd)
                + w_row[i, 1] * y_out[ITERS - 1, f, i + 1, 1],
            )
            out.append(carry[f] + fold(forward, (even, odd)))
        return tuple(out)

    edge = lax.fori_loop(ITERS, ITERS + rows, edge_row, (zero,) * FIELDS)

    one_lane = lax.broadcasted_iota(jnp.int32, (1, LANES), 1)
    packed = jnp.zeros((1, LANES), jnp.float32)
    for f in range(FIELDS):
        parts = [p for level in sums for p in level[f]] + [2.0 * edge[f]]
        for k, part in enumerate(parts):
            value = jnp.sum(jnp.sum(part, axis=0, keepdims=True), axis=1, keepdims=True)
            packed = jnp.where(one_lane == f * MOMENTS + k, value, packed)
    stats[...] = packed
    s_out[...] = scale[ITERS : ITERS + rows, :, :, 0:cols]


def combine(a, b):
    out = [None] * (len(a) + len(b) - 1)
    for i, x in enumerate(a):
        for j, z in enumerate(b):
            out[i + j] = x * z if out[i + j] is None else out[i + j] + x * z
    return out


def weighted(coefs, values):
    total = coefs[0] * values[0]
    for c, v in zip(coefs[1:], values[1:]):
        total = total + c * v
    return total


def krylov_coefs(m):
    gaps = [m[k] - m[k + 1] for k in range(MOMENTS - 1)]
    one = jnp.ones_like(m[0])
    zero = jnp.zeros_like(m[0])
    resid, direct, result = [one], [one], [zero] * ITERS
    rz = m[0]
    for k in range(ITERS):
        curve = weighted(combine(direct, direct), gaps)
        alpha = rz / curve
        result = [
            result[i] + alpha * direct[i] if i < len(direct) else result[i] for i in range(ITERS)
        ]
        if k + 1 == ITERS:
            break
        image = [
            (direct[i] if i < len(direct) else zero) - (direct[i - 1] if i > 0 else zero)
            for i in range(len(direct) + 1)
        ]
        resid = [(resid[i] if i < len(resid) else zero) - alpha * image[i] for i in range(len(image))]
        rz_next = weighted(combine(resid, resid), m)
        ratio = rz_next / rz
        direct = [
            resid[i] + ratio * direct[i] if i < len(direct) else resid[i] for i in range(len(resid))
        ]
        rz = rz_next
    return result


def finish_kernel(rows, half, seeds_hbm, gathered, y, s, out_hbm, seeds, out, seeds_sem, out_sem):
    stage([(seeds_hbm, seeds, seeds_sem)])
    cols = seeds_hbm.shape[1]
    depth_rows = 2 * half * rows
    total = jnp.sum(gathered[...], axis=0, keepdims=True)
    one_lane = lax.broadcasted_iota(jnp.int32, (1, LANES), 1)
    coefs = []
    for f in range(FIELDS):
        moments = []
        for k in range(MOMENTS):
            pick = jnp.where(one_lane == f * MOMENTS + k, total, 0.0)
            value = jnp.sum(pick, axis=1, keepdims=True)
            moments.append(jnp.broadcast_to(value, (half, LANES)))
        coefs.append(krylov_coefs(moments))
    for f in range(FIELDS):
        for row in range(rows):
            for parity in range(2):
                label = slab_of(seeds, row, parity, rows, half)
                index = pl.ds(f * depth_rows + row + rows * parity, half, 2 * rows)
                for at in range(0, cols, LANES):
                    x = weighted(
                        coefs[f],
                        [y[k, f, ITERS + row, parity, :, at : at + LANES] for k in range(ITERS)],
                    )
                    x = x * s[row, parity, :, at : at + LANES]
                    hit = label[:, at : at + LANES] == f + 1
                    out[at // LANES, index, :] = x + hit.astype(jnp.float32)
    copies = tile_copies(out_hbm, out, out_sem, inward=False)
    for copy in copies:
        copy.start()
    for copy in copies:
        copy.wait()


def vmem(count):
    return [pl.BlockSpec(memory_space=pltpu.VMEM)] * count


def on_device(image, seeds):
    depth, rows, cols = image.shape
    half = depth // 2
    wide = cols + LANES
    f32 = jnp.float32
    flat_image = image.reshape(depth * rows, cols)
    flat_seeds = seeds.reshape(depth * rows, cols)
    params = pltpu.CompilerParams(vmem_limit_bytes=48 * 1024 * 1024)

    tiles = cols // LANES

    def call(kernel, shapes, raw, operands, scratch=(), raw_out=False):
        return pl.pallas_call(
            lambda *refs: kernel(rows, half, *refs),
            out_shape=[jax.ShapeDtypeStruct(shape, f32) for shape in shapes],
            in_specs=[pl.BlockSpec(memory_space=pl.ANY)] * len(raw) + vmem(len(operands)),
            out_specs=[pl.BlockSpec(memory_space=pl.ANY)] if raw_out else vmem(len(shapes)),
            scratch_shapes=list(scratch),
            compiler_params=params,
        )(*raw, *operands)

    def staged(dtype, height=depth * rows):
        return pltpu.VMEM((tiles, height, LANES), dtype)

    both = [staged(f32), staged(jnp.int32)] + [pltpu.SemaphoreType.DMA((tiles,))] * 2

    def forward(x, axis):
        return lax.ppermute(x, axis, [(i, i + 1) for i in range(lax.axis_size(axis) - 1)])

    def backward(x, axis):
        return lax.ppermute(x, axis, [(i + 1, i) for i in range(lax.axis_size(axis) - 1)])

    side = (2, 2, half, LANES)
    up, down, right, left = call(
        pack_kernel,
        [(UP, 2, half, cols), (DOWN, 2, half, cols), side, side],
        (flat_image, flat_seeds),
        (),
        both,
    )
    above = forward(up, "gy")
    below = backward(down, "gy")
    from_left = forward(right, "gz")
    from_right = backward(left, "gz")
    mid = LANES // 2
    corner_up = jnp.concatenate([from_right[..., mid:], from_left[..., mid:]], axis=-1)
    corner_down = jnp.concatenate([from_right[..., :mid], from_left[..., :mid]], axis=-1)
    corner_above = forward(corner_up, "gy")
    corner_below = backward(corner_down, "gy")

    span = rows + 2 * ITERS + 1
    slab = (span, 2, half, wide)
    y, s, stats = call(
        main_kernel,
        [(ITERS, FIELDS) + slab, (rows, 2, half, cols), (1, LANES)],
        (flat_image, flat_seeds),
        (above, below, from_left, from_right, corner_above, corner_below),
        [
            pltpu.VMEM(shape, f32)
            for shape in [(rows + IMG_BEFORE + IMG_AFTER, 2, half, wide), (FIELDS,) + slab] + [slab] * 6
        ]
        + both,
    )
    devices = lax.axis_size("gy") * lax.axis_size("gz")
    spread = jnp.broadcast_to(stats[None], (devices, 1, LANES))
    gathered = lax.all_to_all(spread, ("gy", "gz"), 0, 0).reshape(devices, LANES)
    (out,) = call(
        finish_kernel,
        [(FIELDS * depth * rows, cols)],
        (flat_seeds,),
        (gathered, y, s),
        [staged(jnp.int32), staged(f32, FIELDS * depth * rows)]
        + [pltpu.SemaphoreType.DMA((tiles,))] * 2,
        raw_out=True,
    )
    return out.reshape(FIELDS, depth, rows, cols)


def solution(mesh):
    return jax.shard_map(
        on_device,
        mesh=mesh,
        in_specs=(P(None, "gy", "gz"), P(None, "gy", "gz")),
        out_specs=P(None, None, "gy", "gz"),
        check_vma=False,
    )
```

time: 327 us -> 71.6 us (0.22)
  blocking collectives: 184 us -> 12.9 us
  starting transfers between devices: 72.8 us -> 16.3 us
  other arithmetic: 32.9 us -> 0.15 us
  Pallas kernels: 0 us -> 28.8 us
  waiting for transfers between devices: 31.8 us -> 9.61 us
    psum x4 -> x0, blocking collectives: 184 us -> none  [paired_global(): lax.psum((inner_local(resid, precond), inner_local(image_pre, precond)),...]
    ppermute x28 -> x6, starting transfers between devices: 72.8 us -> 16.3 us  [the longest x3 12.5 us: forward(): lax.ppermute(x, axis, [(i, i + 1) for i in range(lax.axis_size(axis) - 1)])]
    pallas_call x0 -> x3, Pallas kernels: none -> 28.8 us  [call(): pl.pallas_call(lambda *refs: kernel(rows, half, *refs), out_shape=[jax.Sh...]
    ppermute x28 -> x6, waiting for transfers between devices: 31.8 us -> 9.61 us  [the longest x3 9.6 us: forward(): lax.ppermute(x, axis, [(i, i + 1) for i in range(lax.axis_size(axis) - 1)])]
    all_to_all x0 -> x1, blocking collectives: none -> 12.9 us  [on_device(): lax.all_to_all(spread, ('gy', 'gz'), 0, 0).reshape(devices, LANES)]
    reduce_sum x5 -> x0, other arithmetic: 11.8 us -> none  [inner_local(): return jnp.sum(left * right, axis=(1, 2, 3))]
    mul x4 -> x0, other arithmetic: 9.48 us -> none  [operate(): free * fields]
    add x6 -> x0, other arithmetic: 5.79 us -> none  [the longest x1 3.94 us: on_device(): return solution + marks]
  transfers between devices with their start and end apart: 28 -> 6, of which waited for: 16 -> 1; matrix products, arithmetic and copies ran while one was open for 2% -> 0% of each run, Pallas kernels for 0% -> 0%
where the time goes in v1:
time: 71.6 us; the launch traced here: 71.1 us
  Pallas kernels  28.8 us (40%)
  starting transfers between devices  16.3 us (23%)
  blocking collectives  12.9 us (18%)
  waiting for transfers between devices  9.61 us (13%)
  local copies, waits for them, and re-layouts  3.28 us (5%)
    pallas_call x3, Pallas kernels, call(): pl.pallas_call(lambda *refs: kernel(rows, half, *refs), out_shape=[jax.Sh...  28.8 us
    all_to_all x1, blocking collectives, on_device(): lax.all_to_all(spread, ('gy', 'gz'), 0, 0).reshape(devices, LANES)  12.9 us
    ppermute x3, starting transfers between devices, forward(): lax.ppermute(x, axis, [(i, i + 1) for i in range(lax.axis_size(axis) - 1)])  12.5 us
    ppermute x3, waiting for transfers between devices, forward(): lax.ppermute(x, axis, [(i, i + 1) for i in range(lax.axis_size(axis) - 1)])  9.6 us
    ppermute x3, starting transfers between devices, backward(): lax.ppermute(x, axis, [(i + 1, i) for i in range(lax.axis_size(axis) - 1)])  3.87 us
    unnamed x6, local copies, waits for them, and re-layouts  3.12 us
  transfers between devices with their start and end apart: 6, of which 1 were waited for; matrix products, arithmetic and copies ran while one was open for 0% of the time, Pallas kernels for 0%

profile of v1, /device:TPU:0, one launch (start us, length us, event | category | flops | bytes accessed | tf_op | source)
XLA Modules:
  0.0 71.1 jit_solution(1451018437449969568)
XLA Ops:
  0.0 0.0 copy-start
  0.0 1.0 %copy-done = s32[16,16,512]{2,1,0:T(8,128)S(1)} copy-done((s32[16,16,512]{2,1,0:T(8,128)S(1)}, s32[16,16,512]{2,1,0:T(8,128)}, u32[]{:S(2)}) %copy-start) | copy-done | bytes 524312
  1.0 1.0 %copy-done.2 = f32[16,16,512]{2,1,0:T(8,128)S(1)} copy-done((f32[16,16,512]{2,1,0:T(8,128)S(1)}, f32[16,16,512]{2,1,0:T(8,128)}, u32[]{:S(2)}) %copy-start.2) | copy-done | bytes 524312
  2.1 1.0 %shard_map.28 = (f32[10,2,8,512]{3,2,1,0:T(8,128)S(1)}, f32[12,2,8,512]{3,2,1,0:T(8,128)S(1)}, f32[2,2,8,128]{3,2,1,0:T(8,128)S(1)}, f32[2,2,8,128]{3,2,1,0:T(8,128)S(1)}) custom-call(f32[256,512]{1,0:T(8,128)S(1)} %bitcast.8, s32[256,512]{1,0:T(8,128)S(1)} %bitcast.5), custom_call_target="tpu_custom_call" | custom-call | tf_op jit(solution)/shard_map/pallas_call | solution.py:453
  3.1 1.3 %collective-permute-start.3 = (f32[2,2,8,128]{3,2,1,0:T(8,128)S(1)}, f32[2,2,8,128]{3,2,1,0:T(8,128)S(1)}, u32[]{:S(2)}, u32[]{:S(2)}) collective-permute-start(f32[2,2,8,128]{3,2,1,0:T(8,128)S(1)} %get-tuple-element.15), channel_id=1, source_target_pairs={{1,0},{2,1},{3,2},{5,4},{6,5},{7,6},{9,8},{10,9},{11,10},{13,12},{... | collective-permute-start | bytes 49160 | tf_op jit(solution)/shard_map/ppermute | solution.py:471
  4.4 3.0 %collective-permute-start.2 = (f32[2,2,8,128]{3,2,1,0:T(8,128)S(1)}, f32[2,2,8,128]{3,2,1,0:T(8,128)S(1)}, u32[]{:S(2)}, u32[]{:S(2)}) collective-permute-start(f32[2,2,8,128]{3,2,1,0:T(8,128)S(1)} %get-tuple-element.14), channel_id=1, source_target_pairs={{0,1},{1,2},{2,3},{4,5},{5,6},{6,7},{8,9},{9,10},{10,11},{12,13},{... | collective-permute-start | bytes 49160 | tf_op jit(solution)/shard_map/ppermute | solution.py:468
  7.4 4.9 %collective-permute-start = (f32[10,2,8,512]{3,2,1,0:T(8,128)S(1)}, f32[10,2,8,512]{3,2,1,0:T(8,128)S(1)}, u32[]{:S(2)}, u32[]{:S(2)}) collective-permute-start(f32[10,2,8,512]{3,2,1,0:T(8,128)S(1)} %get-tuple-element.12), channel_id=1, source_target_pairs={{0,4},{4,8},{8,12},{12,16},{16,20},{20,24},{24,28},{1,5},{5,9},{9,... | collective-permute-start | bytes 983048 | tf_op jit(solution)/shard_map/ppermute | solution.py:468
  12.3 1.3 %collective-permute-start.1 = (f32[12,2,8,512]{3,2,1,0:T(8,128)S(1)}, f32[12,2,8,512]{3,2,1,0:T(8,128)S(1)}, u32[]{:S(2)}, u32[]{:S(2)}) collective-permute-start(f32[12,2,8,512]{3,2,1,0:T(8,128)S(1)} %get-tuple-element.13), channel_id=1, source_target_pairs={{4,0},{8,4},{12,8},{16,12},{20,16},{24,20},{28,24},{5,1},{9,5},{13... | collective-permute-start | bytes 1179656 | tf_op jit(solution)/shard_map/ppermute | solution.py:471
  13.6 0.0 collective-permute-done.3.refs_5_
  13.6 0.1 fusion
  13.7 0.0 collective-permute-done.2.refs_4_
  13.7 0.1 fusion.1
  13.8 0.1 pad_maximum_fusion
  13.8 4.5 %collective-permute-start.4 = (f32[2,2,8,128]{3,2,1,0:T(8,128)S(1)}, f32[2,2,8,128]{3,2,1,0:T(8,128)S(1)}, u32[]{:S(2)}, u32[]{:S(2)}) collective-permute-start(f32[2,2,8,128]{3,2,1,0:T(8,128)S(1)} %pad_maximum_fusion), channel_id=1, source_target_pairs={{0,4},{4,8},{8,12},{12,16},{16,20},{20,24},{24,28},{1,5},{5,9},{9,... | collective-permute-start | bytes 49160 | tf_op jit(solution)/shard_map/ppermute | solution.py:468
  18.4 0.1 pad_maximum_fusion.1
  18.5 1.3 %collective-permute-start.5 = (f32[2,2,8,128]{3,2,1,0:T(8,128)S(1)}, f32[2,2,8,128]{3,2,1,0:T(8,128)S(1)}, u32[]{:S(2)}, u32[]{:S(2)}) collective-permute-start(f32[2,2,8,128]{3,2,1,0:T(8,128)S(1)} %pad_maximum_fusion.1), channel_id=1, source_target_pairs={{4,0},{8,4},{12,8},{16,12},{20,16},{24,20},{28,24},{5,1},{9,5},{13... | collective-permute-start | bytes 49160 | tf_op jit(solution)/shard_map/ppermute | solution.py:471
  19.8 9.6 %collective-permute-done.4.refs_6_ = f32[2,2,8,128]{3,2,1,0:T(8,128)S(1)} collective-permute-done((f32[2,2,8,128]{3,2,1,0:T(8,128)S(1)}, f32[2,2,8,128]{3,2,1,0:T(8,128)S(1)}, u32[]{:S(2)}, u32[]{:S(2)}) %collective-permute-start.4) | collective-permute-done | bytes 16416 | tf_op jit(solution)/shard_map/ppermute | solution.py:468
  29.4 0.0 collective-permute-done.5.refs_7_
  29.4 0.0 collective-permute-done.refs_2_
  29.4 0.0 collective-permute-done.1.refs_3_
  29.4 21.8 %shard_map.29 = (f32[4,2,25,2,8,640]{5,4,3,2,1,0:T(8,128)}, f32[16,2,8,512]{3,2,1,0:T(8,128)S(1)}, f32[1,128]{1,0:T(1,128)S(1)}) custom-call(f32[256,512]{1,0:T(8,128)S(1)} %bitcast.9, s32[256,512]{1,0:T(8,128)S(1)} %bitcast.6, f32[10,2,8,512]{3,2,1,0:T(8,128)S(1)} %collective-permute-done.refs_2_, f32[12,2,8,512]{3,2,1,0:T(8,128)S(1)} %collective-permute-done.1.refs_3_, ...), custom_call_target="tpu_custom_call" | custom-call | tf_op jit(solution)/shard_map/pallas_call | solution.py:453
  51.2 12.9 %all_to_all.5 = f32[32,1,128]{2,1,0:T(1,128)S(1)} all-to-all(f32[32,1,128]{2,1,0:T(1,128)S(1)} %broadcast_in_dim.9), channel_id=1, replica_groups=mesh['gy'=8,'gz'=4] {'gy','gz'}, dimensions={0} | all-to-all | bytes 32768 | tf_op jit(solution)/shard_map/all_to_all | solution.py:506
  64.1 1.0 %copy-done.1 = s32[16,16,512]{2,1,0:T(8,128)S(1)} copy-done((s32[16,16,512]{2,1,0:T(8,128)S(1)}, s32[16,16,512]{2,1,0:T(8,128)}, u32[]{:S(2)}) %copy-start.1) | copy-done | bytes 524312
  65.1 6.0 %shard_map.30 = f32[512,512]{1,0:T(8,128)} custom-call(s32[256,512]{1,0:T(8,128)S(1)} %bitcast.7, f32[32,128]{1,0:T(8,128)S(1)} %bitcast.10, f32[4,2,25,2,8,640]{5,4,3,2,1,0:T(8,128)} %get-tuple-element.17.refs_2_, f32[16,2,8,512]{3,2,1,0:T(8,128)S(1)} %get-tuple-element.18.refs_3_), custom_call_target="tpu_custom_call" | custom-call | tf_op jit(solution)/shard_map/pallas_call | solution.py:453
  (3 shorter events, 0.0 us)
Async XLA Ops:
  0.0 1.0 %copy-start = (s32[16,16,512]{2,1,0:T(8,128)S(1)}, s32[16,16,512]{2,1,0:T(8,128)}, u32[]{:S(2)}) copy-start(s32[16,16,512]{2,1,0:T(8,128)} %param.3) | copy-start | bytes 1572868
  1.0 1.0 %copy-start.2 = (f32[16,16,512]{2,1,0:T(8,128)S(1)}, f32[16,16,512]{2,1,0:T(8,128)}, u32[]{:S(2)}) copy-start(f32[16,16,512]{2,1,0:T(8,128)} %param.2) | copy-start | bytes 1572868
  3.1 10.5 %collective-permute-start.3 = (f32[2,2,8,128]{3,2,1,0:T(8,128)S(1)}, f32[2,2,8,128]{3,2,1,0:T(8,128)S(1)}, u32[]{:S(2)}, u32[]{:S(2)}) collective-permute-start(f32[2,2,8,128]{3,2,1,0:T(8,128)S(1)} %get-tuple-element.15), channel_id=1, source_target_pairs={{1,0},{2,1},{3,2},{5,4},{6,5},{7,6},{9,8},{10,9},{11,10},{13,12},{... | collective-permute-start | bytes 49160 | tf_op jit(solution)/shard_map/ppermute | solution.py:471
  4.4 9.3 %collective-permute-start.2 = (f32[2,2,8,128]{3,2,1,0:T(8,128)S(1)}, f32[2,2,8,128]{3,2,1,0:T(8,128)S(1)}, u32[]{:S(2)}, u32[]{:S(2)}) collective-permute-start(f32[2,2,8,128]{3,2,1,0:T(8,128)S(1)} %get-tuple-element.14), channel_id=1, source_target_pairs={{0,1},{1,2},{2,3},{4,5},{5,6},{6,7},{8,9},{9,10},{10,11},{12,13},{... | collective-permute-start | bytes 49160 | tf_op jit(solution)/shard_map/ppermute | solution.py:468
  7.4 22.0 %collective-permute-start = (f32[10,2,8,512]{3,2,1,0:T(8,128)S(1)}, f32[10,2,8,512]{3,2,1,0:T(8,128)S(1)}, u32[]{:S(2)}, u32[]{:S(2)}) collective-permute-start(f32[10,2,8,512]{3,2,1,0:T(8,128)S(1)} %get-tuple-element.12), channel_id=1, source_target_pairs={{0,4},{4,8},{8,12},{12,16},{16,20},{20,24},{24,28},{1,5},{5,9},{9,... | collective-permute-start | bytes 983048 | tf_op jit(solution)/shard_map/ppermute | solution.py:468
  12.3 17.1 %collective-permute-start.1 = (f32[12,2,8,512]{3,2,1,0:T(8,128)S(1)}, f32[12,2,8,512]{3,2,1,0:T(8,128)S(1)}, u32[]{:S(2)}, u32[]{:S(2)}) collective-permute-start(f32[12,2,8,512]{3,2,1,0:T(8,128)S(1)} %get-tuple-element.13), channel_id=1, source_target_pairs={{4,0},{8,4},{12,8},{16,12},{20,16},{24,20},{28,24},{5,1},{9,5},{13... | collective-permute-start | bytes 1179656 | tf_op jit(solution)/shard_map/ppermute | solution.py:471
  13.8 15.5 %collective-permute-start.4 = (f32[2,2,8,128]{3,2,1,0:T(8,128)S(1)}, f32[2,2,8,128]{3,2,1,0:T(8,128)S(1)}, u32[]{:S(2)}, u32[]{:S(2)}) collective-permute-start(f32[2,2,8,128]{3,2,1,0:T(8,128)S(1)} %pad_maximum_fusion), channel_id=1, source_target_pairs={{0,4},{4,8},{8,12},{12,16},{16,20},{20,24},{24,28},{1,5},{5,9},{9,... | collective-permute-start | bytes 49160 | tf_op jit(solution)/shard_map/ppermute | solution.py:468
  18.5 10.9 %collective-permute-start.5 = (f32[2,2,8,128]{3,2,1,0:T(8,128)S(1)}, f32[2,2,8,128]{3,2,1,0:T(8,128)S(1)}, u32[]{:S(2)}, u32[]{:S(2)}) collective-permute-start(f32[2,2,8,128]{3,2,1,0:T(8,128)S(1)} %pad_maximum_fusion.1), channel_id=1, source_target_pairs={{4,0},{8,4},{12,8},{16,12},{20,16},{24,20},{28,24},{5,1},{9,5},{13... | collective-permute-start | bytes 49160 | tf_op jit(solution)/shard_map/ppermute | solution.py:471
  64.1 1.0 %copy-start.1 = (s32[16,16,512]{2,1,0:T(8,128)S(1)}, s32[16,16,512]{2,1,0:T(8,128)}, u32[]{:S(2)}) copy-start(s32[16,16,512]{2,1,0:T(8,128)} %param.3) | copy-start | bytes 1572868

commit v2 on v1

v2 whole, which is shorter than its diff:
```python
import math

import jax
import jax.numpy as jnp
from jax import lax
from jax.experimental import pallas as pl
from jax.experimental.pallas import tpu as pltpu
from jax.sharding import PartitionSpec as P

ITERS = 4
FIELDS = 2
EDGE_BETA = 60.0
EDGE_FLOOR = 0.05
LANES = 128

IMG_BEFORE, IMG_AFTER = ITERS + 2, ITERS + 3
SEED_BEFORE, SEED_AFTER = ITERS, ITERS + 1
UP = IMG_BEFORE + SEED_BEFORE
DOWN = IMG_AFTER + SEED_AFTER
MOMENTS = 2 * ITERS

SMOOTH_UNROLL = 5
WEIGH_UNROLL = 1
LEVEL_UNROLL = 4


def gauss_taps():
    raw = [math.exp(-0.5 * k * k) for k in range(-2, 3)]
    total = sum(raw)
    return [value / total for value in raw]


def slab_of(ref, row, parity, rows, half):
    index = pl.ds(row + rows * parity, half, 2 * rows)
    return jnp.concatenate([ref[t, index, :] for t in range(ref.shape[0])], axis=1)


def stage(pairs):
    copies = [
        pltpu.make_async_copy(source.at[:, pl.ds(t * LANES, LANES)], staged.at[t], sems.at[t])
        for source, staged, sems in pairs
        for t in range(staged.shape[0])
    ]
    for copy in copies:
        copy.start()
    for copy in copies:
        copy.wait()


def rows_kernel(rows, half, image_hbm, seeds_hbm, up, down, own, label, image, seeds, image_sem, seeds_sem):
    stage([(image_hbm, image, image_sem), (seeds_hbm, seeds, seeds_sem)])
    for row in range(rows):
        for parity in range(2):
            grey = slab_of(image, row, parity, rows, half)
            seed = slab_of(seeds, row, parity, rows, half).astype(jnp.float32)
            own[row, parity] = grey
            label[row, parity] = seed
            if row >= rows - IMG_BEFORE:
                up[row - (rows - IMG_BEFORE), parity] = grey
            if row >= rows - SEED_BEFORE:
                up[IMG_BEFORE + row - (rows - SEED_BEFORE), parity] = seed
            if row < IMG_AFTER:
                down[row, parity] = grey
            if row < SEED_AFTER:
                down[IMG_AFTER + row, parity] = seed


def cols_kernel(rows, half, own, label, right, left):
    cols = own.shape[3]
    lane = lax.broadcasted_iota(jnp.int32, (half, LANES), 1)
    for kind, source in enumerate((own, label)):
        for parity in range(2):
            head = jnp.zeros((half, LANES), jnp.float32)
            tail = jnp.zeros((half, LANES), jnp.float32)
            for row in range(rows):
                first = source[row, parity, :, 0:LANES]
                last = source[row, parity, :, cols - LANES : cols]
                here = (lane >= 8 * row) & (lane < 8 * row + 8)
                shift = (8 * row) % LANES
                head = jnp.where(here, pltpu.roll(first, shift, 1) if shift else first, head)
                shift = (8 * row + 8) % LANES
                tail = jnp.where(here, pltpu.roll(last, shift, 1) if shift else last, tail)
            left[kind, parity] = head
            right[kind, parity] = tail


def once(get):
    known = {}

    def value(parity, t):
        if (parity, t) not in known:
            known[parity, t] = get(parity, t)
        return known[parity, t]

    return value


def main_kernel(
    rows,
    half,
    own,
    label,
    above,
    below,
    from_left,
    from_right,
    corner_above,
    corner_below,
    basis,
    stats,
    x_ext,
    mark,
    smooth,
    scale,
    w_col,
    w_dep,
    w_row,
    w_raw,
    y,
):
    cols = own.shape[3]
    wide = cols + LANES
    tiles = wide // LANES
    core_tiles = cols // LANES
    gy, gz = lax.axis_index("gy"), lax.axis_index("gz")
    last_gy, last_gz = lax.axis_size("gy") - 1, lax.axis_size("gz") - 1
    t0, t1, t2 = gauss_taps()[:3]
    lane = lax.broadcasted_iota(jnp.int32, (half, LANES), 1)
    sub = lax.broadcasted_iota(jnp.int32, (half, LANES), 0)
    not_first = (sub > 0).astype(jnp.float32)
    not_last = (sub < half - 1).astype(jnp.float32)

    def at(t):
        return slice(t * LANES, (t + 1) * LANES)

    def halo_tile(before, before_at, after, after_at):
        after_tile = pltpu.roll(after, (LANES - after_at) % LANES, 1) if after_at else after
        shift = (LANES - 8 - before_at) % LANES
        before_tile = pltpu.roll(before, shift, 1) if shift else before
        return jnp.where(lane < 8, after_tile, jnp.where(lane >= LANES - 8, before_tile, 0.0))

    def put_image(index, parity, core, halo):
        for t in range(core_tiles):
            x_ext[index, parity, :, at(t)] = core[:, at(t)]
        x_ext[index, parity, :, at(core_tiles)] = halo

    def put_seeds(index, parity, core, halo):
        for t in range(tiles):
            part = core[:, at(t)] if t < core_tiles else halo
            for f in range(FIELDS):
                mark[f, index, parity, :, at(t)] = (part == f + 1.0).astype(jnp.float32)

    def corner(ref, kind, parity, row):
        tile = ref[kind, parity]
        place = (8 * row) % 64
        return halo_tile(tile, 64 + place, tile, place)

    for parity in range(2):
        for i in range(IMG_BEFORE):
            put_image(
                i, parity, above[i, parity], corner(corner_above, 0, parity, rows - IMG_BEFORE + i)
            )
        for i in range(IMG_AFTER):
            put_image(
                IMG_BEFORE + rows + i, parity, below[i, parity], corner(corner_below, 0, parity, i)
            )
        for i in range(SEED_BEFORE):
            put_seeds(
                i,
                parity,
                above[IMG_BEFORE + i, parity],
                corner(corner_above, 1, parity, rows - SEED_BEFORE + i),
            )
        for i in range(SEED_AFTER):
            put_seeds(
                SEED_BEFORE + rows + i,
                parity,
                below[IMG_AFTER + i, parity],
                corner(corner_below, 1, parity, i),
            )
        for row in range(rows):
            put_image(
                IMG_BEFORE + row,
                parity,
                own[row, parity],
                halo_tile(from_left[0, parity], 8 * row, from_right[0, parity], 8 * row),
            )
            put_seeds(
                SEED_BEFORE + row,
                parity,
                label[row, parity],
                halo_tile(from_left[1, parity], 8 * row, from_right[1, parity], 8 * row),
            )

    def shifted(get, by):
        turned = once(lambda parity, t: pltpu.roll(get(parity, t), -by % LANES, 1))
        if by > 0:
            return once(
                lambda parity, t: jnp.where(
                    lane < LANES - by, turned(parity, t), turned(parity, (t + 1) % tiles)
                )
            )
        return once(
            lambda parity, t: jnp.where(lane >= -by, turned(parity, t), turned(parity, (t - 1) % tiles))
        )

    def next_sub(v):
        return pltpu.roll(v, half - 1, 0)

    def prev_sub(v):
        return pltpu.roll(v, 1, 0)

    def load(ref, *index):
        return once(lambda parity, t: ref[(*index, parity, slice(None), at(t))])

    def every():
        return [(t, parity) for t in range(tiles) for parity in range(2)]

    def smooth_row(r, carry):
        x = [load(x_ext, r + k) for k in range(5)]
        flat = once(
            lambda p, t: t0 * (x[0](p, t) + x[4](p, t)) + t1 * (x[1](p, t) + x[3](p, t)) + t2 * x[2](p, t)
        )
        above_ = once(lambda p, t: not_last * next_sub(flat(p, t)))
        below_ = once(lambda p, t: not_first * prev_sub(flat(p, t)))

        def depth(p, t):
            if p == 0:
                near = flat(1, t) + below_(1, t)
            else:
                near = flat(0, t) + above_(0, t)
            return t0 * (above_(p, t) + below_(p, t)) + t1 * near + t2 * flat(p, t)

        deep = once(depth)
        near_next, near_prev = shifted(deep, 1), shifted(deep, -1)
        far_next, far_prev = shifted(deep, 2), shifted(deep, -2)
        for t, p in every():
            smooth[r, p, :, at(t)] = (
                t0 * (far_next(p, t) + far_prev(p, t))
                + t1 * (near_next(p, t) + near_prev(p, t))
                + t2 * deep(p, t)
            )
        return carry

    lax.fori_loop(0, rows + 2 * ITERS + 1, smooth_row, 0, unroll=SMOOTH_UNROLL)

    cut_tile = {
        core_tiles - 1: jnp.where((lane == LANES - 1) & (gz == last_gz), 0.0, 1.0),
        tiles - 1: jnp.where((lane == LANES - 1) & (gz == 0), 0.0, 1.0),
    }

    def weight(step):
        return EDGE_FLOOR + jnp.exp((-EDGE_BETA * step) * step)

    def row_edge(i, here):
        cut = ((i == ITERS - 1) & (gy == 0)) | ((i == ITERS + rows - 1) & (gy == last_gy))
        keep = jnp.where(cut, 0.0, 1.0)
        after = load(smooth, i + 1)
        return once(lambda p, t: keep * weight(after(p, t) - here(p, t)))

    first_edge = row_edge(0, load(smooth, 0))
    for t, p in every():
        w_raw[0, p, :, at(t)] = first_edge(p, t)
        scale[0, p, :, at(t)] = jnp.zeros((half, LANES), jnp.float32)

    def weigh_row(i, carry):
        here = load(smooth, i)
        down_edge, up_edge = row_edge(i, here), load(w_raw, i - 1)

        def dep_of(p, t):
            if p == 0:
                return weight(here(1, t) - here(0, t))
            return not_last * weight(next_sub(here(0, t)) - here(1, t))

        dep = once(dep_of)
        beyond = shifted(here, 1)

        def col_of(p, t):
            value = weight(beyond(p, t) - here(p, t))
            return cut_tile[t] * value if t in cut_tile else value

        col = once(col_of)
        col_back = shifted(col, -1)
        marks = [load(mark, f, i) for f in range(FIELDS)]

        def scale_of(p, t):
            back = prev_sub(dep(1, t)) if p == 0 else dep(0, t)
            deg = dep(p, t) + back + down_edge(p, t) + up_edge(p, t) + col(p, t) + col_back(p, t)
            return jnp.where(marks[0](p, t) + marks[1](p, t) == 0.0, lax.rsqrt(deg), 0.0)

        s = once(scale_of)
        s_beyond = shifted(s, 1)
        before = load(scale, i - 1)
        total = []
        for f in range(FIELDS):
            total.append(neighbour_sum(marks[f], dep, col, down_edge, up_edge, mark, f, i))
        for t, p in every():
            place = (p, slice(None), at(t))
            w_raw[(i, *place)] = down_edge(p, t)
            scale[(i, *place)] = s(p, t)
            w_row[(i - 1, *place)] = up_edge(p, t) * s(p, t) * before(p, t)
            other = s(1, t) if p == 0 else next_sub(s(0, t))
            w_dep[(i, *place)] = dep(p, t) * s(p, t) * other
            w_col[(i, *place)] = col(p, t) * s(p, t) * s_beyond(p, t)
            for f in range(FIELDS):
                y[(0, f, i, *place)] = s(p, t) * total[f](p, t)
        return carry

    def neighbour_sum(v, dep, col, down_edge, up_edge, ref, f, i):
        above_, below_ = load(ref, f, i - 1), load(ref, f, i + 1)
        beyond = shifted(v, 1)
        pushed = shifted(lambda p, t: col(p, t) * v(p, t), -1)

        def total(p, t):
            if p == 0:
                depth = dep(0, t) * v(1, t) + prev_sub(dep(1, t) * v(1, t))
            else:
                depth = dep(1, t) * next_sub(v(0, t)) + dep(0, t) * v(0, t)
            return (
                (depth + (col(p, t) * beyond(p, t) + pushed(p, t)))
                + (down_edge(p, t) * below_(p, t) + up_edge(p, t) * above_(p, t))
            )

        return once(total)

    lax.fori_loop(1, rows + 2 * ITERS, weigh_row, 0, unroll=WEIGH_UNROLL)

    zero = jnp.zeros((half, LANES), jnp.float32)
    inner = [(p, t) for t in range(core_tiles) for p in range(2)]

    def fold(a, b):
        total = None
        for p, t in inner:
            part = a(p, t) * b(p, t)
            total = part if total is None else total + part
        return total

    def weights_at(i):
        return load(w_dep, i), load(w_col, i), load(w_row, i), load(w_row, i - 1)

    def apply_row(level, i):
        weights = weights_at(i)
        olds = [load(y.at[level - 1], f, i) for f in range(FIELDS)]
        news = [
            neighbour_sum(olds[f], *weights, y.at[level - 1], f, i) for f in range(FIELDS)
        ]
        for t, p in every():
            for f in range(FIELDS):
                y[level, f, i, p, :, at(t)] = news[f](p, t)
        return olds, news

    def keep_basis(level, i, values):
        s = load(scale, i)
        for p, t in inner:
            for f in range(FIELDS):
                basis[level, f, i - ITERS, p, :, at(t)] = s(p, t) * values[f](p, t)

    sums = []
    for level in range(1, ITERS):

        def outer_row(i, carry, level=level):
            apply_row(level, i)
            return carry

        def core_row(i, carry, level=level):
            olds, news = apply_row(level, i)
            if level == 1:
                keep_basis(0, i, olds)
            keep_basis(level, i, news)
            out = []
            for f in range(FIELDS):
                pairs = [(olds[f], news[f]), (news[f], news[f])]
                if level == 1:
                    pairs = [(olds[f], olds[f])] + pairs
                for a, b in pairs:
                    out.append(carry[len(out)] + fold(a, b))
            return tuple(out)

        count = 3 if level == 1 else 2
        for i in (*range(level + 1, ITERS), *range(ITERS + rows, rows + 2 * ITERS - level)):
            outer_row(i, 0)
        acc = lax.fori_loop(
            ITERS, ITERS + rows, core_row, (zero,) * (count * FIELDS), unroll=LEVEL_UNROLL
        )
        sums.append([acc[:count], acc[count:]])

    def edge_row(i, carry):
        dep, col, row, _ = weights_at(i)
        out = []
        for f in range(FIELDS):
            v, below_ = load(y, ITERS - 1, f, i), load(y, ITERS - 1, f, i + 1)
            beyond = shifted(v, 1)

            def forward(p, t, v=v, below_=below_, beyond=beyond):
                lower = v(1, t) if p == 0 else next_sub(v(0, t))
                return dep(p, t) * lower + col(p, t) * beyond(p, t) + row(p, t) * below_(p, t)

            out.append(carry[f] + fold(once(forward), v))
        return tuple(out)

    edge = lax.fori_loop(ITERS, ITERS + rows, edge_row, (zero,) * FIELDS, unroll=LEVEL_UNROLL)

    one_lane = lax.broadcasted_iota(jnp.int32, (1, LANES), 1)
    packed = jnp.zeros((1, LANES), jnp.float32)
    for f in range(FIELDS):
        parts = [p for level in sums for p in level[f]] + [2.0 * edge[f]]
        for k, part in enumerate(parts):
            value = jnp.sum(jnp.sum(part, axis=0, keepdims=True), axis=1, keepdims=True)
            packed = jnp.where(one_lane == f * MOMENTS + k, value, packed)
    stats[...] = packed


def combine(a, b):
    out = [None] * (len(a) + len(b) - 1)
    for i, x in enumerate(a):
        for j, z in enumerate(b):
            out[i + j] = x * z if out[i + j] is None else out[i + j] + x * z
    return out


def weighted(coefs, values):
    total = coefs[0] * values[0]
    for c, v in zip(coefs[1:], values[1:]):
        total = total + c * v
    return total


def krylov_coefs(m):
    gaps = [m[k] - m[k + 1] for k in range(MOMENTS - 1)]
    one = jnp.ones_like(m[0])
    zero = jnp.zeros_like(m[0])
    resid, direct, result = [one], [one], [zero] * ITERS
    rz = m[0]
    for k in range(ITERS):
        curve = weighted(combine(direct, direct), gaps)
        alpha = jnp.where(curve > 0.0, rz / curve, 0.0)
        result = [
            result[i] + alpha * direct[i] if i < len(direct) else result[i] for i in range(ITERS)
        ]
        if k + 1 == ITERS:
            break
        image = [
            (direct[i] if i < len(direct) else zero) - (direct[i - 1] if i > 0 else zero)
            for i in range(len(direct) + 1)
        ]
        resid = [(resid[i] if i < len(resid) else zero) - alpha * image[i] for i in range(len(image))]
        rz_next = weighted(combine(resid, resid), m)
        ratio = jnp.where(rz > 0.0, rz_next / rz, 0.0)
        direct = [
            resid[i] + ratio * direct[i] if i < len(direct) else resid[i] for i in range(len(resid))
        ]
        rz = rz_next
    return result


def finish_kernel(rows, half, gathered, basis, label, out_hbm, out, out_sem):
    core_tiles = out.shape[1]
    total = jnp.sum(gathered[...], axis=0, keepdims=True)
    one_lane = lax.broadcasted_iota(jnp.int32, (1, LANES), 1)
    coefs = []
    for f in range(FIELDS):
        moments = []
        for k in range(MOMENTS):
            pick = jnp.where(one_lane == f * MOMENTS + k, total, 0.0)
            value = jnp.sum(pick, axis=1, keepdims=True)
            moments.append(jnp.broadcast_to(value, (half, LANES)))
        coefs.append(krylov_coefs(moments))
    depth_rows = 2 * half * rows
    copies = []
    for f in range(FIELDS):
        for t in range(core_tiles):
            at = slice(t * LANES, (t + 1) * LANES)
            for row in range(rows):
                for parity in range(2):
                    x = weighted(coefs[f], [basis[k, f, row, parity, :, at] for k in range(ITERS)])
                    hit = label[row, parity, :, at] == f + 1.0
                    index = pl.ds(row + rows * parity, half, 2 * rows)
                    out[f, t, index, :] = x + hit.astype(jnp.float32)
            copy = pltpu.make_async_copy(
                out.at[f, t],
                out_hbm.at[pl.ds(f * depth_rows, depth_rows), pl.ds(t * LANES, LANES)],
                out_sem.at[f, t],
            )
            copy.start()
            copies.append(copy)
    for copy in copies:
        copy.wait()


def vmem(count):
    return [pl.BlockSpec(memory_space=pltpu.VMEM)] * count


def hbm(count):
    return [pl.BlockSpec(memory_space=pltpu.HBM)] * count


def on_device(image, seeds):
    depth, rows, cols = image.shape
    half = depth // 2
    wide = cols + LANES
    core_tiles = cols // LANES
    f32 = jnp.float32

    def call(kernel, name, shapes, raw, operands, scratch=(), raw_out=False, mib=16):
        return pl.pallas_call(
            lambda *refs: kernel(rows, half, *refs),
            out_shape=[jax.ShapeDtypeStruct(shape, f32) for shape in shapes],
            in_specs=hbm(len(raw)) + vmem(len(operands)),
            out_specs=hbm(len(shapes)) if raw_out else vmem(len(shapes)),
            scratch_shapes=list(scratch),
            compiler_params=pltpu.CompilerParams(vmem_limit_bytes=mib * 1024 * 1024),
            name=name,
        )(*raw, *operands)

    def forward(x, axis):
        return lax.ppermute(x, axis, [(i, i + 1) for i in range(lax.axis_size(axis) - 1)])

    def backward(x, axis):
        return lax.ppermute(x, axis, [(i + 1, i) for i in range(lax.axis_size(axis) - 1)])

    def staged(dtype):
        return pltpu.VMEM((core_tiles, depth * rows, LANES), dtype)

    slabs = (rows, 2, half, cols)
    up, down, own, label = call(
        rows_kernel,
        "own_rows",
        [(UP,) + slabs[1:], (DOWN,) + slabs[1:], slabs, slabs],
        (image.reshape(depth * rows, cols), seeds.reshape(depth * rows, cols)),
        (),
        [staged(f32), staged(jnp.int32)] + [pltpu.SemaphoreType.DMA((core_tiles,))] * 2,
    )
    above = forward(up, "gy")
    below = backward(down, "gy")
    side = (2, 2, half, LANES)
    right, left = call(cols_kernel, "own_columns", [side, side], (), (own, label))
    from_left = forward(right, "gz")
    from_right = backward(left, "gz")
    mid = LANES // 2
    corner_up = jnp.concatenate([from_right[..., mid:], from_left[..., mid:]], axis=-1)
    corner_down = jnp.concatenate([from_right[..., :mid], from_left[..., :mid]], axis=-1)
    corner_above = forward(corner_up, "gy")
    corner_below = backward(corner_down, "gy")

    slab = (rows + 2 * ITERS + 1, 2, half, wide)
    shapes = [(rows + IMG_BEFORE + IMG_AFTER, 2, half, wide), (FIELDS,) + slab]
    shapes += [slab] * 6 + [(ITERS, FIELDS) + slab]
    basis, stats = call(
        main_kernel,
        "krylov",
        [(ITERS, FIELDS) + slabs, (1, LANES)],
        (),
        (own, label, above, below, from_left, from_right, corner_above, corner_below),
        [pltpu.VMEM(shape, f32) for shape in shapes],
        mib=32,
    )
    devices = lax.axis_size("gy") * lax.axis_size("gz")
    spread = jnp.broadcast_to(stats[None], (devices, 1, LANES))
    gathered = lax.all_to_all(spread, ("gy", "gz"), 0, 0).reshape(devices, LANES)
    (out,) = call(
        finish_kernel,
        "finish",
        [(FIELDS * depth * rows, cols)],
        (),
        (gathered, basis, label),
        [
            pltpu.VMEM((FIELDS, core_tiles, depth * rows, LANES), f32),
            pltpu.SemaphoreType.DMA((FIELDS, core_tiles)),
        ],
        raw_out=True,
    )
    return out.reshape(FIELDS, depth, rows, cols)


def solution(mesh):
    return jax.shard_map(
        on_device,
        mesh=mesh,
        in_specs=(P(None, "gy", "gz"), P(None, "gy", "gz")),
        out_specs=P(None, None, "gy", "gz"),
        check_vma=False,
    )
```

time: 71.6 us -> 61 us (0.85)
  Pallas kernels: 28.8 us -> 19.3 us
  local copies, waits for them, and re-layouts: 3.28 us -> 2.24 us
    pallas_call x3 -> x4, Pallas kernels: 28.8 us -> 19.3 us  [call(): pl.pallas_call(lambda *refs: kernel(rows, half, *refs), out_shape=[jax.Sh...]
    unnamed x6 -> x4, local copies, waits for them, and re-layouts: 3.12 us -> 2.08 us
where the time goes in v2:
time: 61 us; the launch traced here: 60.6 us
  Pallas kernels  19.3 us (32%)
  starting transfers between devices  16.3 us (27%)
  blocking collectives  12.9 us (21%)
  waiting for transfers between devices  9.61 us (16%)
  local copies, waits for them, and re-layouts  2.24 us (4%)
    pallas_call x4, Pallas kernels, call(): pl.pallas_call(lambda *refs: kernel(rows, half, *refs), out_shape=[jax.Sh...  19.3 us
    all_to_all x1, blocking collectives, on_device(): lax.all_to_all(spread, ('gy', 'gz'), 0, 0).reshape(devices, LANES)  12.9 us
    ppermute x3, starting transfers between devices, forward(): lax.ppermute(x, axis, [(i, i + 1) for i in range(lax.axis_size(axis) - 1)])  12.5 us
    ppermute x3, waiting for transfers between devices, forward(): lax.ppermute(x, axis, [(i, i + 1) for i in range(lax.axis_size(axis) - 1)])  9.6 us
    ppermute x3, starting transfers between devices, backward(): lax.ppermute(x, axis, [(i + 1, i) for i in range(lax.axis_size(axis) - 1)])  3.87 us
    unnamed x4, local copies, waits for them, and re-layouts  2.08 us
  transfers between devices with their start and end apart: 6, of which 1 were waited for; matrix products, arithmetic and copies ran while one was open for 0% of the time, Pallas kernels for 0%

profile of v2, /device:TPU:0, one launch (start us, length us, event | category | flops | bytes accessed | tf_op | source)
XLA Modules:
  0.0 60.6 jit_solution(416402105296426592)
XLA Ops:
  0.0 0.0 copy-start
  0.0 1.0 %copy-done = f32[16,16,512]{2,1,0:T(8,128)S(1)} copy-done((f32[16,16,512]{2,1,0:T(8,128)S(1)}, f32[16,16,512]{2,1,0:T(8,128)}, u32[]{:S(2)}) %copy-start) | copy-done | bytes 524312
  1.0 1.0 %copy-done.1 = s32[16,16,512]{2,1,0:T(8,128)S(1)} copy-done((s32[16,16,512]{2,1,0:T(8,128)S(1)}, s32[16,16,512]{2,1,0:T(8,128)}, u32[]{:S(2)}) %copy-start.1) | copy-done | bytes 524312
  2.1 0.8 %own_rows.1 = (f32[10,2,8,512]{3,2,1,0:T(8,128)S(1)}, f32[12,2,8,512]{3,2,1,0:T(8,128)S(1)}, f32[16,2,8,512]{3,2,1,0:T(8,128)S(1)}, f32[16,2,8,512]{3,2,1,0:T(8,128)S(1)}) custom-call(f32[256,512]{1,0:T(8,128)S(1)} %bitcast.5, s32[256,512]{1,0:T(8,128)S(1)} %bitcast.6), custom_call_target="tpu_custom_call" | custom-call | tf_op jit(solution)/shard_map/own_rows/pallas_call | solution.py:506
  2.9 0.2 own_columns.1
  3.1 1.3 %collective-permute-start.3 = (f32[2,2,8,128]{3,2,1,0:T(8,128)S(1)}, f32[2,2,8,128]{3,2,1,0:T(8,128)S(1)}, u32[]{:S(2)}, u32[]{:S(2)}) collective-permute-start(f32[2,2,8,128]{3,2,1,0:T(8,128)S(1)} %get-tuple-element.18), channel_id=1, source_target_pairs={{1,0},{2,1},{3,2},{5,4},{6,5},{7,6},{9,8},{10,9},{11,10},{13,12},{... | collective-permute-start | bytes 49160 | tf_op jit(solution)/shard_map/ppermute | solution.py:520
  4.4 3.0 %collective-permute-start.2 = (f32[2,2,8,128]{3,2,1,0:T(8,128)S(1)}, f32[2,2,8,128]{3,2,1,0:T(8,128)S(1)}, u32[]{:S(2)}, u32[]{:S(2)}) collective-permute-start(f32[2,2,8,128]{3,2,1,0:T(8,128)S(1)} %get-tuple-element.17), channel_id=1, source_target_pairs={{0,1},{1,2},{2,3},{4,5},{5,6},{6,7},{8,9},{9,10},{10,11},{12,13},{... | collective-permute-start | bytes 49160 | tf_op jit(solution)/shard_map/ppermute | solution.py:517
  7.5 4.9 %collective-permute-start = (f32[10,2,8,512]{3,2,1,0:T(8,128)S(1)}, f32[10,2,8,512]{3,2,1,0:T(8,128)S(1)}, u32[]{:S(2)}, u32[]{:S(2)}) collective-permute-start(f32[10,2,8,512]{3,2,1,0:T(8,128)S(1)} %get-tuple-element.15), channel_id=1, source_target_pairs={{0,4},{4,8},{8,12},{12,16},{16,20},{20,24},{24,28},{1,5},{5,9},{9,... | collective-permute-start | bytes 983048 | tf_op jit(solution)/shard_map/ppermute | solution.py:517
  12.4 1.3 %collective-permute-start.1 = (f32[12,2,8,512]{3,2,1,0:T(8,128)S(1)}, f32[12,2,8,512]{3,2,1,0:T(8,128)S(1)}, u32[]{:S(2)}, u32[]{:S(2)}) collective-permute-start(f32[12,2,8,512]{3,2,1,0:T(8,128)S(1)} %get-tuple-element.16), channel_id=1, source_target_pairs={{4,0},{8,4},{12,8},{16,12},{20,16},{24,20},{28,24},{5,1},{9,5},{13... | collective-permute-start | bytes 1179656 | tf_op jit(solution)/shard_map/ppermute | solution.py:520
  13.7 0.0 collective-permute-done.3.refs_5_
  13.7 0.1 fusion
  13.8 0.0 collective-permute-done.2.refs_4_
  13.8 0.1 fusion.1
  13.8 0.1 pad_maximum_fusion
  13.9 4.5 %collective-permute-start.4 = (f32[2,2,8,128]{3,2,1,0:T(8,128)S(1)}, f32[2,2,8,128]{3,2,1,0:T(8,128)S(1)}, u32[]{:S(2)}, u32[]{:S(2)}) collective-permute-start(f32[2,2,8,128]{3,2,1,0:T(8,128)S(1)} %pad_maximum_fusion), channel_id=1, source_target_pairs={{0,4},{4,8},{8,12},{12,16},{16,20},{20,24},{24,28},{1,5},{5,9},{9,... | collective-permute-start | bytes 49160 | tf_op jit(solution)/shard_map/ppermute | solution.py:517
  18.5 0.1 pad_maximum_fusion.1
  18.5 1.3 %collective-permute-start.5 = (f32[2,2,8,128]{3,2,1,0:T(8,128)S(1)}, f32[2,2,8,128]{3,2,1,0:T(8,128)S(1)}, u32[]{:S(2)}, u32[]{:S(2)}) collective-permute-start(f32[2,2,8,128]{3,2,1,0:T(8,128)S(1)} %pad_maximum_fusion.1), channel_id=1, source_target_pairs={{4,0},{8,4},{12,8},{16,12},{20,16},{24,20},{28,24},{5,1},{9,5},{13... | collective-permute-start | bytes 49160 | tf_op jit(solution)/shard_map/ppermute | solution.py:520
  19.8 9.6 %collective-permute-done.4.refs_6_ = f32[2,2,8,128]{3,2,1,0:T(8,128)S(1)} collective-permute-done((f32[2,2,8,128]{3,2,1,0:T(8,128)S(1)}, f32[2,2,8,128]{3,2,1,0:T(8,128)S(1)}, u32[]{:S(2)}, u32[]{:S(2)}) %collective-permute-start.4) | collective-permute-done | bytes 16416 | tf_op jit(solution)/shard_map/ppermute | solution.py:517
  29.4 0.0 collective-permute-done.5.refs_7_
  29.4 0.0 collective-permute-done.refs_2_
  29.4 0.0 collective-permute-done.1.refs_3_
  29.4 16.5 %krylov.1 = (f32[4,2,16,2,8,512]{5,4,3,2,1,0:T(8,128)S(1)}, f32[1,128]{1,0:T(1,128)S(1)}) custom-call(f32[16,2,8,512]{3,2,1,0:T(8,128)S(1)} %get-tuple-element.13.refs_0_, f32[16,2,8,512]{3,2,1,0:T(8,128)S(1)} %get-tuple-element.14.refs_1_.refs_2_, f32[10,2,8,512]{3,2,1,0:T(8,128)S(1)} %collective-permute-done.refs_2_, ...), custom_call_target="tpu_custom_call" | custom-call | tf_op jit(solution)/shard_map/krylov/pallas_call | solution.py:506
  45.9 12.9 %all_to_all.5 = f32[32,1,128]{2,1,0:T(1,128)S(1)} all-to-all(f32[32,1,128]{2,1,0:T(1,128)S(1)} %broadcast_in_dim.9), channel_id=1, replica_groups=mesh['gy'=8,'gz'=4] {'gy','gz'}, dimensions={0} | all-to-all | bytes 32768 | tf_op jit(solution)/shard_map/all_to_all | solution.py:560
  58.8 1.8 %finish.1 = f32[512,512]{1,0:T(8,128)} custom-call(f32[32,128]{1,0:T(8,128)S(1)} %bitcast.7, f32[4,2,16,2,8,512]{5,4,3,2,1,0:T(8,128)S(1)} %get-tuple-element.20.refs_1_, f32[16,2,8,512]{3,2,1,0:T(8,128)S(1)} %get-tuple-element.14.refs_1_.refs_2_), custom_call_target="tpu_custom_call" | custom-call | tf_op jit(solution)/shard_map/finish/pallas_call | solution.py:506
  (2 shorter events, 0.0 us)
Async XLA Ops:
  0.0 1.0 %copy-start = (f32[16,16,512]{2,1,0:T(8,128)S(1)}, f32[16,16,512]{2,1,0:T(8,128)}, u32[]{:S(2)}) copy-start(f32[16,16,512]{2,1,0:T(8,128)} %param.2) | copy-start | bytes 1572868
  1.0 1.0 %copy-start.1 = (s32[16,16,512]{2,1,0:T(8,128)S(1)}, s32[16,16,512]{2,1,0:T(8,128)}, u32[]{:S(2)}) copy-start(s32[16,16,512]{2,1,0:T(8,128)} %param.3) | copy-start | bytes 1572868
  3.1 10.5 %collective-permute-start.3 = (f32[2,2,8,128]{3,2,1,0:T(8,128)S(1)}, f32[2,2,8,128]{3,2,1,0:T(8,128)S(1)}, u32[]{:S(2)}, u32[]{:S(2)}) collective-permute-start(f32[2,2,8,128]{3,2,1,0:T(8,128)S(1)} %get-tuple-element.18), channel_id=1, source_target_pairs={{1,0},{2,1},{3,2},{5,4},{6,5},{7,6},{9,8},{10,9},{11,10},{13,12},{... | collective-permute-start | bytes 49160 | tf_op jit(solution)/shard_map/ppermute | solution.py:520
  4.4 9.3 %collective-permute-start.2 = (f32[2,2,8,128]{3,2,1,0:T(8,128)S(1)}, f32[2,2,8,128]{3,2,1,0:T(8,128)S(1)}, u32[]{:S(2)}, u32[]{:S(2)}) collective-permute-start(f32[2,2,8,128]{3,2,1,0:T(8,128)S(1)} %get-tuple-element.17), channel_id=1, source_target_pairs={{0,1},{1,2},{2,3},{4,5},{5,6},{6,7},{8,9},{9,10},{10,11},{12,13},{... | collective-permute-start | bytes 49160 | tf_op jit(solution)/shard_map/ppermute | solution.py:517
  7.5 22.0 %collective-permute-start = (f32[10,2,8,512]{3,2,1,0:T(8,128)S(1)}, f32[10,2,8,512]{3,2,1,0:T(8,128)S(1)}, u32[]{:S(2)}, u32[]{:S(2)}) collective-permute-start(f32[10,2,8,512]{3,2,1,0:T(8,128)S(1)} %get-tuple-element.15), channel_id=1, source_target_pairs={{0,4},{4,8},{8,12},{12,16},{16,20},{20,24},{24,28},{1,5},{5,9},{9,... | collective-permute-start | bytes 983048 | tf_op jit(solution)/shard_map/ppermute | solution.py:517
  12.4 17.1 %collective-permute-start.1 = (f32[12,2,8,512]{3,2,1,0:T(8,128)S(1)}, f32[12,2,8,512]{3,2,1,0:T(8,128)S(1)}, u32[]{:S(2)}, u32[]{:S(2)}) collective-permute-start(f32[12,2,8,512]{3,2,1,0:T(8,128)S(1)} %get-tuple-element.16), channel_id=1, source_target_pairs={{4,0},{8,4},{12,8},{16,12},{20,16},{24,20},{28,24},{5,1},{9,5},{13... | collective-permute-start | bytes 1179656 | tf_op jit(solution)/shard_map/ppermute | solution.py:520
  13.9 15.5 %collective-permute-start.4 = (f32[2,2,8,128]{3,2,1,0:T(8,128)S(1)}, f32[2,2,8,128]{3,2,1,0:T(8,128)S(1)}, u32[]{:S(2)}, u32[]{:S(2)}) collective-permute-start(f32[2,2,8,128]{3,2,1,0:T(8,128)S(1)} %pad_maximum_fusion), channel_id=1, source_target_pairs={{0,4},{4,8},{8,12},{12,16},{16,20},{20,24},{24,28},{1,5},{5,9},{9,... | collective-permute-start | bytes 49160 | tf_op jit(solution)/shard_map/ppermute | solution.py:517
  18.5 10.9 %collective-permute-start.5 = (f32[2,2,8,128]{3,2,1,0:T(8,128)S(1)}, f32[2,2,8,128]{3,2,1,0:T(8,128)S(1)}, u32[]{:S(2)}, u32[]{:S(2)}) collective-permute-start(f32[2,2,8,128]{3,2,1,0:T(8,128)S(1)} %pad_maximum_fusion.1), channel_id=1, source_target_pairs={{4,0},{8,4},{12,8},{16,12},{20,16},{24,20},{28,24},{5,1},{9,5},{13... | collective-permute-start | bytes 49160 | tf_op jit(solution)/shard_map/ppermute | solution.py:520

commit v3 on v2

--- a/solution.py
+++ b/solution.py
@@ -19,9 +19,13 @@
 DOWN = IMG_AFTER + SEED_AFTER
 MOMENTS = 2 * ITERS
 
-SMOOTH_UNROLL = 5
-WEIGH_UNROLL = 1
-LEVEL_UNROLL = 4
+DEEP_UNROLL = 0
+WIDE_UNROLL = 0
+EDGE_UNROLL = 0
+SCALE_UNROLL = 0
+FIRST_UNROLL = 0
+RESCALE_UNROLL = 0
+LEVEL_UNROLL = 16
 
 
 def gauss_taps():
@@ -216,33 +220,30 @@
     def every():
         return [(t, parity) for t in range(tiles) for parity in range(2)]
 
-    def smooth_row(r, carry):
+    def deep_row(r):
         x = [load(x_ext, r + k) for k in range(5)]
         flat = once(
             lambda p, t: t0 * (x[0](p, t) + x[4](p, t)) + t1 * (x[1](p, t) + x[3](p, t)) + t2 * x[2](p, t)
         )
         above_ = once(lambda p, t: not_last * next_sub(flat(p, t)))
         below_ = once(lambda p, t: not_first * prev_sub(flat(p, t)))
-
-        def depth(p, t):
-            if p == 0:
-                near = flat(1, t) + below_(1, t)
-            else:
-                near = flat(0, t) + above_(0, t)
-            return t0 * (above_(p, t) + below_(p, t)) + t1 * near + t2 * flat(p, t)
-
-        deep = once(depth)
+        for t, p in every():
+            near = flat(1, t) + below_(1, t) if p == 0 else flat(0, t) + above_(0, t)
+            far = above_(p, t) + below_(p, t)
+            smooth[r, p, :, at(t)] = t0 * far + t1 * near + t2 * flat(p, t)
+
+    def wide_row(r):
+        deep = load(smooth, r)
         near_next, near_prev = shifted(deep, 1), shifted(deep, -1)
         far_next, far_prev = shifted(deep, 2), shifted(deep, -2)
-        for t, p in every():
-            smooth[r, p, :, at(t)] = (
-                t0 * (far_next(p, t) + far_prev(p, t))
-                + t1 * (near_next(p, t) + near_prev(p, t))
-                + t2 * deep(p, t)
-            )
-        return carry
-
-    lax.fori_loop(0, rows + 2 * ITERS + 1, smooth_row, 0, unroll=SMOOTH_UNROLL)
+        fresh = {
+            (p, t): t0 * (far_next(p, t) + far_prev(p, t))
+            + t1 * (near_next(p, t) + near_prev(p, t))
+            + t2 * deep(p, t)
+            for t, p in every()
+        }
+        for (p, t), value in fresh.items():
+            smooth[r, p, :, at(t)] = value
 
     cut_tile = {
         core_tiles - 1: jnp.where((lane == LANES - 1) & (gz == last_gz), 0.0, 1.0),
@@ -252,59 +253,69 @@
     def weight(step):
         return EDGE_FLOOR + jnp.exp((-EDGE_BETA * step) * step)
 
-    def row_edge(i, here):
+    def edges_row(i, cols_too=True):
+        here, after = load(smooth, i), load(smooth, i + 1)
         cut = ((i == ITERS - 1) & (gy == 0)) | ((i == ITERS + rows - 1) & (gy == last_gy))
         keep = jnp.where(cut, 0.0, 1.0)
-        after = load(smooth, i + 1)
-        return once(lambda p, t: keep * weight(after(p, t) - here(p, t)))
-
-    first_edge = row_edge(0, load(smooth, 0))
-    for t, p in every():
-        w_raw[0, p, :, at(t)] = first_edge(p, t)
-        scale[0, p, :, at(t)] = jnp.zeros((half, LANES), jnp.float32)
-
-    def weigh_row(i, carry):
-        here = load(smooth, i)
-        down_edge, up_edge = row_edge(i, here), load(w_raw, i - 1)
-
-        def dep_of(p, t):
-            if p == 0:
-                return weight(here(1, t) - here(0, t))
-            return not_last * weight(next_sub(here(0, t)) - here(1, t))
-
-        dep = once(dep_of)
         beyond = shifted(here, 1)
-
-        def col_of(p, t):
-            value = weight(beyond(p, t) - here(p, t))
-            return cut_tile[t] * value if t in cut_tile else value
-
-        col = once(col_of)
+        for t, p in every():
+            place = (i, p, slice(None), at(t))
+            w_raw[place] = keep * weight(after(p, t) - here(p, t))
+            if cols_too:
+                if p == 0:
+                    w_dep[place] = weight(here(1, t) - here(0, t))
+                else:
+                    w_dep[place] = not_last * weight(next_sub(here(0, t)) - here(1, t))
+                value = weight(beyond(p, t) - here(p, t))
+                w_col[place] = cut_tile[t] * value if t in cut_tile else value
+
+    def scale_row(i):
+        dep, col, down_edge, up_edge = weights_at(i, w_raw)
         col_back = shifted(col, -1)
         marks = [load(mark, f, i) for f in range(FIELDS)]
-
-        def scale_of(p, t):
+        for t, p in every():
             back = prev_sub(dep(1, t)) if p == 0 else dep(0, t)
             deg = dep(p, t) + back + down_edge(p, t) + up_edge(p, t) + col(p, t) + col_back(p, t)
-            return jnp.where(marks[0](p, t) + marks[1](p, t) == 0.0, lax.rsqrt(deg), 0.0)
-
-        s = once(scale_of)
-        s_beyond = shifted(s, 1)
-        before = load(scale, i - 1)
-        total = []
-        for f in range(FIELDS):
-            total.append(neighbour_sum(marks[f], dep, col, down_edge, up_edge, mark, f, i))
+            free = marks[0](p, t) + marks[1](p, t) == 0.0
+            scale[i, p, :, at(t)] = jnp.where(free, lax.rsqrt(deg), 0.0)
+
+    def first_row(i):
+        weights = weights_at(i, w_raw)
+        s = load(scale, i)
+        sums = [neighbour_sum(load(mark, f, i), *weights, mark, f, i) for f in range(FIELDS)]
         for t, p in every():
-            place = (p, slice(None), at(t))
-            w_raw[(i, *place)] = down_edge(p, t)
-            scale[(i, *place)] = s(p, t)
-            w_row[(i - 1, *place)] = up_edge(p, t) * s(p, t) * before(p, t)
-            other = s(1, t) if p == 0 else next_sub(s(0, t))
-            w_dep[(i, *place)] = dep(p, t) * s(p, t) * other
-            w_col[(i, *place)] = col(p, t) * s(p, t) * s_beyond(p, t)
             for f in range(FIELDS):
-                y[(0, f, i, *place)] = s(p, t) * total[f](p, t)
-        return carry
+                y[0, f, i, p, :, at(t)] = s(p, t) * sums[f](p, t)
+
+    def rescale_row(i, cols_too=True):
+        s, after = load(scale, i), load(scale, i + 1)
+        dep, col, down_edge, _ = weights_at(i, w_raw)
+        beyond = shifted(s, 1)
+        for t, p in every():
+            place = (i, p, slice(None), at(t))
+            w_row[place] = down_edge(p, t) * s(p, t) * after(p, t)
+            if cols_too:
+                w_dep[place] = dep(p, t) * s(p, t) * (s(1, t) if p == 0 else next_sub(s(0, t)))
+                w_col[place] = col(p, t) * s(p, t) * beyond(p, t)
+
+    def weights_at(i, row_ref):
+        return load(w_dep, i), load(w_col, i), load(row_ref, i), load(row_ref, i - 1)
+
+    def run(body, first, stop, unroll):
+        if unroll <= 0:
+            for i in range(first, stop):
+                body(i)
+            return
+        steps = (stop - first) // unroll
+
+        def chunk(n, carry):
+            for k in range(unroll):
+                body(first + n * unroll + k)
+            return carry
+
+        lax.fori_loop(0, steps, chunk, 0)
+        for i in range(first + steps * unroll, stop):
+            body(i)
 
     def neighbour_sum(v, dep, col, down_edge, up_edge, ref, f, i):
         above_, below_ = load(ref, f, i - 1), load(ref, f, i + 1)
@@ -323,7 +334,15 @@
 
         return once(total)
 
-    lax.fori_loop(1, rows + 2 * ITERS, weigh_row, 0, unroll=WEIGH_UNROLL)
+    last = rows + 2 * ITERS
+    run(deep_row, 0, last + 1, DEEP_UNROLL)
+    run(wide_row, 0, last + 1, WIDE_UNROLL)
+    edges_row(0, False)
+    run(edges_row, 1, last, EDGE_UNROLL)
+    run(scale_row, 1, last, SCALE_UNROLL)
+    run(first_row, 1, last, FIRST_UNROLL)
+    rescale_row(1, False)
+    run(rescale_row, 2, last - 1, RESCALE_UNROLL)
 
     zero = jnp.zeros((half, LANES), jnp.float32)
     inner = [(p, t) for t in range(core_tiles) for p in range(2)]
@@ -335,11 +354,8 @@
             total = part if total is None else total + part
         return total
 
-    def weights_at(i):
-        return load(w_dep, i), load(w_col, i), load(w_row, i), load(w_row, i - 1)
-
     def apply_row(level, i):
-        weights = weights_at(i)
+        weights = weights_at(i, w_row)
         olds = [load(y.at[level - 1], f, i) for f in range(FIELDS)]
         news = [
             neighbour_sum(olds[f], *weights, y.at[level - 1], f, i) for f in range(FIELDS)
@@ -385,7 +401,7 @@
         sums.append([acc[:count], acc[count:]])
 
     def edge_row(i, carry):
-        dep, col, row, _ = weights_at(i)
+        dep, col, row, _ = weights_at(i, w_row)
         out = []
         for f in range(FIELDS):
             v, below_ = load(y, ITERS - 1, f, i), load(y, ITERS - 1, f, i + 1)
@@ -527,7 +543,10 @@
         rows_kernel,
         "own_rows",
         [(UP,) + slabs[1:], (DOWN,) + slabs[1:], slabs, slabs],
-        (image.reshape(depth * rows, cols), seeds.reshape(depth * rows, cols)),
+        tuple(
+            pltpu.with_memory_space_constraint(v.reshape(depth * rows, cols), pltpu.HBM)
+            for v in (image, seeds)
+        ),
         (),
         [staged(f32), staged(jnp.int32)] + [pltpu.SemaphoreType.DMA((core_tiles,))] * 2,
     )

time: 61 us -> 51 us (0.84)
  Pallas kernels: 19.3 us -> 11.5 us
  local copies, waits for them, and re-layouts: 2.24 us -> 0.16 us
    pallas_call x4, Pallas kernels: 19.3 us -> 11.5 us  [call(): pl.pallas_call(lambda *refs: kernel(rows, half, *refs), out_shape=[jax.Sh...]
    unnamed x4 -> x0, local copies, waits for them, and re-layouts: 2.08 us -> none
  transfers between devices with their start and end apart: 6 -> 6, of which waited for: 1 -> 1; matrix products, arithmetic and copies ran while one was open for 0% -> 1% of each run, Pallas kernels for 0% -> 0%
where the time goes in v3:
time: 51 us; the launch traced here: 50.8 us
  starting transfers between devices  16.3 us (32%)
  blocking collectives  12.9 us (25%)
  Pallas kernels  11.5 us (23%)
  waiting for transfers between devices  9.61 us (19%)
    all_to_all x1, blocking collectives, on_device(): lax.all_to_all(spread, ('gy', 'gz'), 0, 0).reshape(devices, LANES)  12.9 us
    ppermute x3, starting transfers between devices, forward(): lax.ppermute(x, axis, [(i, i + 1) for i in range(lax.axis_size(axis) - 1)])  12.5 us
    pallas_call x4, Pallas kernels, call(): pl.pallas_call(lambda *refs: kernel(rows, half, *refs), out_shape=[jax.Sh...  11.5 us
    ppermute x3, waiting for transfers between devices, forward(): lax.ppermute(x, axis, [(i, i + 1) for i in range(lax.axis_size(axis) - 1)])  9.6 us
    ppermute x3, starting transfers between devices, backward(): lax.ppermute(x, axis, [(i + 1, i) for i in range(lax.axis_size(axis) - 1)])  3.87 us
  transfers between devices with their start and end apart: 6, of which 1 were waited for; matrix products, arithmetic and copies ran while one was open for 1% of the time, Pallas kernels for 0%

profile of v3, /device:TPU:0, one launch (start us, length us, event | category | flops | bytes accessed | tf_op | source)
XLA Modules:
  0.0 50.8 jit_solution(15009669374722287374)
XLA Ops:
  0.0 2.0 %own_rows.1 = (f32[10,2,8,512]{3,2,1,0:T(8,128)S(1)}, f32[12,2,8,512]{3,2,1,0:T(8,128)S(1)}, f32[16,2,8,512]{3,2,1,0:T(8,128)S(1)}, f32[16,2,8,512]{3,2,1,0:T(8,128)S(1)}) custom-call(f32[256,512]{1,0:T(8,128)} %bitcast.7, s32[256,512]{1,0:T(8,128)} %bitcast.8), custom_call_target="tpu_custom_call" | custom-call | tf_op jit(solution)/shard_map/own_rows/pallas_call | solution.py:522
  2.0 0.2 own_columns.1
  2.2 1.3 %collective-permute-start.3 = (f32[2,2,8,128]{3,2,1,0:T(8,128)S(1)}, f32[2,2,8,128]{3,2,1,0:T(8,128)S(1)}, u32[]{:S(2)}, u32[]{:S(2)}) collective-permute-start(f32[2,2,8,128]{3,2,1,0:T(8,128)S(1)} %get-tuple-element.18), channel_id=1, source_target_pairs={{1,0},{2,1},{3,2},{5,4},{6,5},{7,6},{9,8},{10,9},{11,10},{13,12},{... | collective-permute-start | bytes 49160 | tf_op jit(solution)/shard_map/ppermute | solution.py:536
  3.5 3.0 %collective-permute-start.2 = (f32[2,2,8,128]{3,2,1,0:T(8,128)S(1)}, f32[2,2,8,128]{3,2,1,0:T(8,128)S(1)}, u32[]{:S(2)}, u32[]{:S(2)}) collective-permute-start(f32[2,2,8,128]{3,2,1,0:T(8,128)S(1)} %get-tuple-element.17), channel_id=1, source_target_pairs={{0,1},{1,2},{2,3},{4,5},{5,6},{6,7},{8,9},{9,10},{10,11},{12,13},{... | collective-permute-start | bytes 49160 | tf_op jit(solution)/shard_map/ppermute | solution.py:533
  6.5 4.9 %collective-permute-start = (f32[10,2,8,512]{3,2,1,0:T(8,128)S(1)}, f32[10,2,8,512]{3,2,1,0:T(8,128)S(1)}, u32[]{:S(2)}, u32[]{:S(2)}) collective-permute-start(f32[10,2,8,512]{3,2,1,0:T(8,128)S(1)} %get-tuple-element.15), channel_id=1, source_target_pairs={{0,4},{4,8},{8,12},{12,16},{16,20},{20,24},{24,28},{1,5},{5,9},{9,... | collective-permute-start | bytes 983048 | tf_op jit(solution)/shard_map/ppermute | solution.py:533
  11.4 1.3 %collective-permute-start.1 = (f32[12,2,8,512]{3,2,1,0:T(8,128)S(1)}, f32[12,2,8,512]{3,2,1,0:T(8,128)S(1)}, u32[]{:S(2)}, u32[]{:S(2)}) collective-permute-start(f32[12,2,8,512]{3,2,1,0:T(8,128)S(1)} %get-tuple-element.16), channel_id=1, source_target_pairs={{4,0},{8,4},{12,8},{16,12},{20,16},{24,20},{28,24},{5,1},{9,5},{13... | collective-permute-start | bytes 1179656 | tf_op jit(solution)/shard_map/ppermute | solution.py:536
  12.7 0.0 collective-permute-done.3.refs_5_
  12.7 0.1 fusion
  12.8 0.0 collective-permute-done.2.refs_4_
  12.8 0.1 fusion.1
  12.9 0.1 pad_maximum_fusion
  13.0 4.5 %collective-permute-start.4 = (f32[2,2,8,128]{3,2,1,0:T(8,128)S(1)}, f32[2,2,8,128]{3,2,1,0:T(8,128)S(1)}, u32[]{:S(2)}, u32[]{:S(2)}) collective-permute-start(f32[2,2,8,128]{3,2,1,0:T(8,128)S(1)} %pad_maximum_fusion), channel_id=1, source_target_pairs={{0,4},{4,8},{8,12},{12,16},{16,20},{20,24},{24,28},{1,5},{5,9},{9,... | collective-permute-start | bytes 49160 | tf_op jit(solution)/shard_map/ppermute | solution.py:533
  17.5 0.1 pad_maximum_fusion.1
  17.6 1.3 %collective-permute-start.5 = (f32[2,2,8,128]{3,2,1,0:T(8,128)S(1)}, f32[2,2,8,128]{3,2,1,0:T(8,128)S(1)}, u32[]{:S(2)}, u32[]{:S(2)}) collective-permute-start(f32[2,2,8,128]{3,2,1,0:T(8,128)S(1)} %pad_maximum_fusion.1), channel_id=1, source_target_pairs={{4,0},{8,4},{12,8},{16,12},{20,16},{24,20},{28,24},{5,1},{9,5},{13... | collective-permute-start | bytes 49160 | tf_op jit(solution)/shard_map/ppermute | solution.py:536
  18.9 9.6 %collective-permute-done.4.refs_6_ = f32[2,2,8,128]{3,2,1,0:T(8,128)S(1)} collective-permute-done((f32[2,2,8,128]{3,2,1,0:T(8,128)S(1)}, f32[2,2,8,128]{3,2,1,0:T(8,128)S(1)}, u32[]{:S(2)}, u32[]{:S(2)}) %collective-permute-start.4) | collective-permute-done | bytes 16416 | tf_op jit(solution)/shard_map/ppermute | solution.py:533
  28.5 0.0 collective-permute-done.5.refs_7_
  28.5 0.0 collective-permute-done.refs_2_
  28.5 0.0 collective-permute-done.1.refs_3_
  28.5 7.5 %krylov.1 = (f32[4,2,16,2,8,512]{5,4,3,2,1,0:T(8,128)S(1)}, f32[1,128]{1,0:T(1,128)S(1)}) custom-call(f32[16,2,8,512]{3,2,1,0:T(8,128)S(1)} %get-tuple-element.13.refs_0_, f32[16,2,8,512]{3,2,1,0:T(8,128)S(1)} %get-tuple-element.14.refs_1_.refs_2_, f32[10,2,8,512]{3,2,1,0:T(8,128)S(1)} %collective-permute-done.refs_2_, ...), custom_call_target="tpu_custom_call" | custom-call | tf_op jit(solution)/shard_map/krylov/pallas_call | solution.py:522
  36.1 12.9 %all_to_all.5 = f32[32,1,128]{2,1,0:T(1,128)S(1)} all-to-all(f32[32,1,128]{2,1,0:T(1,128)S(1)} %broadcast_in_dim.9), channel_id=1, replica_groups=mesh['gy'=8,'gz'=4] {'gy','gz'}, dimensions={0} | all-to-all | bytes 32768 | tf_op jit(solution)/shard_map/all_to_all | solution.py:579
  49.0 1.8 %finish.1 = f32[512,512]{1,0:T(8,128)} custom-call(f32[32,128]{1,0:T(8,128)S(1)} %bitcast.5, f32[4,2,16,2,8,512]{5,4,3,2,1,0:T(8,128)S(1)} %get-tuple-element.20.refs_1_, f32[16,2,8,512]{3,2,1,0:T(8,128)S(1)} %get-tuple-element.14.refs_1_.refs_2_), custom_call_target="tpu_custom_call" | custom-call | tf_op jit(solution)/shard_map/finish/pallas_call | solution.py:522
  (1 shorter events, 0.0 us)
Async XLA Ops:
  2.2 10.5 %collective-permute-start.3 = (f32[2,2,8,128]{3,2,1,0:T(8,128)S(1)}, f32[2,2,8,128]{3,2,1,0:T(8,128)S(1)}, u32[]{:S(2)}, u32[]{:S(2)}) collective-permute-start(f32[2,2,8,128]{3,2,1,0:T(8,128)S(1)} %get-tuple-element.18), channel_id=1, source_target_pairs={{1,0},{2,1},{3,2},{5,4},{6,5},{7,6},{9,8},{10,9},{11,10},{13,12},{... | collective-permute-start | bytes 49160 | tf_op jit(solution)/shard_map/ppermute | solution.py:536
  3.5 9.3 %collective-permute-start.2 = (f32[2,2,8,128]{3,2,1,0:T(8,128)S(1)}, f32[2,2,8,128]{3,2,1,0:T(8,128)S(1)}, u32[]{:S(2)}, u32[]{:S(2)}) collective-permute-start(f32[2,2,8,128]{3,2,1,0:T(8,128)S(1)} %get-tuple-element.17), channel_id=1, source_target_pairs={{0,1},{1,2},{2,3},{4,5},{5,6},{6,7},{8,9},{9,10},{10,11},{12,13},{... | collective-permute-start | bytes 49160 | tf_op jit(solution)/shard_map/ppermute | solution.py:533
  6.5 22.0 %collective-permute-start = (f32[10,2,8,512]{3,2,1,0:T(8,128)S(1)}, f32[10,2,8,512]{3,2,1,0:T(8,128)S(1)}, u32[]{:S(2)}, u32[]{:S(2)}) collective-permute-start(f32[10,2,8,512]{3,2,1,0:T(8,128)S(1)} %get-tuple-element.15), channel_id=1, source_target_pairs={{0,4},{4,8},{8,12},{12,16},{16,20},{20,24},{24,28},{1,5},{5,9},{9,... | collective-permute-start | bytes 983048 | tf_op jit(solution)/shard_map/ppermute | solution.py:533
  11.4 17.1 %collective-permute-start.1 = (f32[12,2,8,512]{3,2,1,0:T(8,128)S(1)}, f32[12,2,8,512]{3,2,1,0:T(8,128)S(1)}, u32[]{:S(2)}, u32[]{:S(2)}) collective-permute-start(f32[12,2,8,512]{3,2,1,0:T(8,128)S(1)} %get-tuple-element.16), channel_id=1, source_target_pairs={{4,0},{8,4},{12,8},{16,12},{20,16},{24,20},{28,24},{5,1},{9,5},{13... | collective-permute-start | bytes 1179656 | tf_op jit(solution)/shard_map/ppermute | solution.py:536
  13.0 15.5 %collective-permute-start.4 = (f32[2,2,8,128]{3,2,1,0:T(8,128)S(1)}, f32[2,2,8,128]{3,2,1,0:T(8,128)S(1)}, u32[]{:S(2)}, u32[]{:S(2)}) collective-permute-start(f32[2,2,8,128]{3,2,1,0:T(8,128)S(1)} %pad_maximum_fusion), channel_id=1, source_target_pairs={{0,4},{4,8},{8,12},{12,16},{16,20},{20,24},{24,28},{1,5},{5,9},{9,... | collective-permute-start | bytes 49160 | tf_op jit(solution)/shard_map/ppermute | solution.py:533
  17.6 10.9 %collective-permute-start.5 = (f32[2,2,8,128]{3,2,1,0:T(8,128)S(1)}, f32[2,2,8,128]{3,2,1,0:T(8,128)S(1)}, u32[]{:S(2)}, u32[]{:S(2)}) collective-permute-start(f32[2,2,8,128]{3,2,1,0:T(8,128)S(1)} %pad_maximum_fusion.1), channel_id=1, source_target_pairs={{4,0},{8,4},{12,8},{16,12},{20,16},{24,20},{28,24},{5,1},{9,5},{13... | collective-permute-start | bytes 49160 | tf_op jit(solution)/shard_map/ppermute | solution.py:536

commit v4 on v2

v4 whole, which is shorter than its diff:
```python
import math

import jax
import jax.numpy as jnp
from jax import lax
from jax.experimental import pallas as pl
from jax.experimental.pallas import tpu as pltpu
from jax.sharding import PartitionSpec as P

ITERS = 4
FIELDS = 2
EDGE_BETA = 60.0
EDGE_FLOOR = 0.05
LANES = 128

IMG_BEFORE, IMG_AFTER = ITERS + 2, ITERS + 3
SEED_BEFORE, SEED_AFTER = ITERS, ITERS + 1
UP = IMG_BEFORE + SEED_BEFORE
DOWN = IMG_AFTER + SEED_AFTER
MOMENTS = 2 * ITERS


def gauss_taps():
    raw = [math.exp(-0.5 * k * k) for k in range(-2, 3)]
    total = sum(raw)
    return [value / total for value in raw]


def slab_of(ref, row, parity, rows, half):
    index = pl.ds(row + rows * parity, half, 2 * rows)
    return jnp.concatenate([ref[t, index, :] for t in range(ref.shape[0])], axis=1)


def stage(pairs):
    copies = [
        pltpu.make_async_copy(source.at[:, pl.ds(t * LANES, LANES)], staged.at[t], sems.at[t])
        for source, staged, sems in pairs
        for t in range(staged.shape[0])
    ]
    for copy in copies:
        copy.start()
    for copy in copies:
        copy.wait()


def rows_kernel(rows, half, image_hbm, seeds_hbm, up, down, own, label, image, seeds, image_sem, seeds_sem):
    stage([(image_hbm, image, image_sem), (seeds_hbm, seeds, seeds_sem)])
    for row in range(rows):
        for parity in range(2):
            grey = slab_of(image, row, parity, rows, half)
            seed = slab_of(seeds, row, parity, rows, half).astype(jnp.float32)
            own[row, parity] = grey
            label[row, parity] = seed
            if row >= rows - IMG_BEFORE:
                up[row - (rows - IMG_BEFORE), parity] = grey
            if row >= rows - SEED_BEFORE:
                up[IMG_BEFORE + row - (rows - SEED_BEFORE), parity] = seed
            if row < IMG_AFTER:
                down[row, parity] = grey
            if row < SEED_AFTER:
                down[IMG_AFTER + row, parity] = seed


def cols_kernel(rows, half, own, label, pair, cross):
    even = lax.rem(lax.axis_index("gz"), 2) == 0
    cols = own.shape[3]
    lane = lax.broadcasted_iota(jnp.int32, (half, LANES), 1)
    for kind, source in enumerate((own, label)):
        for parity in range(2):
            head = jnp.zeros((half, LANES), jnp.float32)
            tail = jnp.zeros((half, LANES), jnp.float32)
            for row in range(rows):
                first = source[row, parity, :, 0:LANES]
                last = source[row, parity, :, cols - LANES : cols]
                here = (lane >= 8 * row) & (lane < 8 * row + 8)
                shift = (8 * row) % LANES
                head = jnp.where(here, pltpu.roll(first, shift, 1) if shift else first, head)
                shift = (8 * row + 8) % LANES
                tail = jnp.where(here, pltpu.roll(last, shift, 1) if shift else last, tail)
            pair[kind, parity] = jnp.where(even, tail, head)
            cross[kind, parity] = jnp.where(even, head, tail)


def once(get):
    known = {}

    def value(parity, t):
        if (parity, t) not in known:
            known[parity, t] = get(parity, t)
        return known[parity, t]

    return value


class Rows:
    def __init__(self, ref, first, lead=(), earlier=None):
        self.ref, self.first, self.lead, self.earlier = ref, first, lead, earlier

    def place(self, i, parity, t):
        lanes = slice(t * LANES, (t + 1) * LANES)
        return (*self.lead, i - self.first, parity, slice(None), lanes)

    def row(self, i):
        if self.earlier is not None and i < self.first:
            return self.earlier.row(i)
        return once(lambda parity, t: self.ref[self.place(i, parity, t)])

    def put(self, i, parity, t, value):
        self.ref[self.place(i, parity, t)] = value


WEIGHTS = ("smooth", "w_raw", "d_raw", "c_raw", "scale", "w_row", "w_dep", "w_col")


def extents(rows):
    table = {
        "image": (0, rows + IMG_BEFORE, rows + IMG_BEFORE + IMG_AFTER),
        "mark": (0, rows + SEED_BEFORE, rows + SEED_BEFORE + SEED_AFTER),
        "smooth": (0, rows + 2, rows + 2 * ITERS + 1),
        "w_raw": (0, rows + 1, rows + 2 * ITERS),
        "d_raw": (1, rows + 2, rows + 2 * ITERS),
        "c_raw": (1, rows + 2, rows + 2 * ITERS),
        "scale": (1, rows + 1, rows + 2 * ITERS),
        "w_row": (1, rows, rows + 2 * ITERS - 1),
        "w_dep": (2, rows + 1, rows + 2 * ITERS - 1),
        "w_col": (2, rows + 1, rows + 2 * ITERS - 1),
        "edge": (ITERS, rows + 1 - ITERS, rows + ITERS),
    }
    for level in range(ITERS):
        table["y", level] = (1 + level, rows + 1 - level, rows + 2 * ITERS - level)
    return table


def sweep(rows, half, second, fetch_image, fetch_seeds, stores, basis, basis_first, sums):
    span = {
        name: range(mid, stop) if second else range(first, mid)
        for name, (first, mid, stop) in extents(rows).items()
    }
    wide = stores["smooth"].ref.shape[-1]
    tiles = wide // LANES
    core_tiles = tiles - 1
    gy, gz = lax.axis_index("gy"), lax.axis_index("gz")
    last_gy, last_gz = lax.axis_size("gy") - 1, lax.axis_size("gz") - 1
    t0, t1, t2 = gauss_taps()[:3]
    lane = lax.broadcasted_iota(jnp.int32, (half, LANES), 1)
    sub = lax.broadcasted_iota(jnp.int32, (half, LANES), 0)
    not_first = (sub > 0).astype(jnp.float32)
    not_last = (sub < half - 1).astype(jnp.float32)
    every = [(t, p) for t in range(tiles) for p in range(2)]
    inner = [(t, p) for t in range(core_tiles) for p in range(2)]

    def shifted(get, by):
        turned = once(lambda parity, t: pltpu.roll(get(parity, t), -by % LANES, 1))
        if by > 0:
            return once(
                lambda parity, t: jnp.where(
                    lane < LANES - by, turned(parity, t), turned(parity, (t + 1) % tiles)
                )
            )
        return once(
            lambda parity, t: jnp.where(lane >= -by, turned(parity, t), turned(parity, (t - 1) % tiles))
        )

    def next_sub(v):
        return pltpu.roll(v, half - 1, 0)

    def prev_sub(v):
        return pltpu.roll(v, 1, 0)

    image, smooth, scale = stores["image"], stores["smooth"], stores["scale"]
    w_raw, d_raw, c_raw = stores["w_raw"], stores["d_raw"], stores["c_raw"]
    w_row, w_dep, w_col = stores["w_row"], stores["w_dep"], stores["w_col"]
    marks = [stores["mark", f] for f in range(FIELDS)]
    y = [[stores["y", level, f] for f in range(FIELDS)] for level in range(ITERS)]

    for i in span["image"]:
        for p in range(2):
            for t, part in enumerate(fetch_image(i, p, lane)):
                image.put(i, p, t, part)
    for i in span["mark"]:
        for p in range(2):
            for t, part in enumerate(fetch_seeds(i, p, lane)):
                for f in range(FIELDS):
                    marks[f].put(i, p, t, (part == f + 1.0).astype(jnp.float32))

    for i in span["smooth"]:
        x = [image.row(i + k) for k in range(5)]
        flat = once(
            lambda p, t, x=x: t0 * (x[0](p, t) + x[4](p, t))
            + t1 * (x[1](p, t) + x[3](p, t))
            + t2 * x[2](p, t)
        )
        later = once(lambda p, t, flat=flat: not_last * next_sub(flat(p, t)))
        sooner = once(lambda p, t, flat=flat: not_first * prev_sub(flat(p, t)))
        for t, p in every:
            near = flat(1, t) + sooner(1, t) if p == 0 else flat(0, t) + later(0, t)
            smooth.put(i, p, t, t0 * (later(p, t) + sooner(p, t)) + t1 * near + t2 * flat(p, t))
    for i in span["smooth"]:
        deep = smooth.row(i)
        near_next, near_prev = shifted(deep, 1), shifted(deep, -1)
        far_next, far_prev = shifted(deep, 2), shifted(deep, -2)
        fresh = [
            (
                p,
                t,
                t0 * (far_next(p, t) + far_prev(p, t))
                + t1 * (near_next(p, t) + near_prev(p, t))
                + t2 * deep(p, t),
            )
            for t, p in every
        ]
        for p, t, value in fresh:
            smooth.put(i, p, t, value)

    cut_tile = {
        core_tiles - 1: jnp.where((lane == LANES - 1) & (gz == last_gz), 0.0, 1.0),
        tiles - 1: jnp.where((lane == LANES - 1) & (gz == 0), 0.0, 1.0),
    }

    def weight(step):
        return EDGE_FLOOR + jnp.exp((-EDGE_BETA * step) * step)

    cut_row = {
        ITERS - 1: jnp.where(gy == 0, 0.0, 1.0),
        ITERS + rows - 1: jnp.where(gy == last_gy, 0.0, 1.0),
    }
    for i in sorted(set(span["w_raw"]) | set(span["d_raw"])):
        here = smooth.row(i)
        if i in span["w_raw"]:
            after = smooth.row(i + 1)
            for t, p in every:
                value = weight(after(p, t) - here(p, t))
                w_raw.put(i, p, t, cut_row[i] * value if i in cut_row else value)
        if i in span["d_raw"]:
            beyond = shifted(here, 1)
            for t, p in every:
                if p == 0:
                    d_raw.put(i, p, t, weight(here(1, t) - here(0, t)))
                else:
                    d_raw.put(i, p, t, not_last * weight(next_sub(here(0, t)) - here(1, t)))
                value = weight(beyond(p, t) - here(p, t))
                c_raw.put(i, p, t, cut_tile[t] * value if t in cut_tile else value)

    for i in span["scale"]:
        dep, col, down, up = d_raw.row(i), c_raw.row(i), w_raw.row(i), w_raw.row(i - 1)
        col_back = shifted(col, -1)
        seeded = [mark.row(i) for mark in marks]
        for t, p in every:
            back = prev_sub(dep(1, t)) if p == 0 else dep(0, t)
            deg = dep(p, t) + back + down(p, t) + up(p, t) + col(p, t) + col_back(p, t)
            free = seeded[0](p, t) + seeded[1](p, t) == 0.0
            scale.put(i, p, t, jnp.where(free, lax.rsqrt(deg), 0.0))

    def neighbour_sum(v, field, i, dep, col, down, up):
        above, below = field.row(i - 1), field.row(i + 1)
        beyond = shifted(v, 1)
        pushed = shifted(lambda p, t: col(p, t) * v(p, t), -1)

        def total(p, t):
            if p == 0:
                depth = dep(0, t) * v(1, t) + prev_sub(dep(1, t) * v(1, t))
            else:
                depth = dep(1, t) * next_sub(v(0, t)) + dep(0, t) * v(0, t)
            return (depth + (col(p, t) * beyond(p, t) + pushed(p, t))) + (
                down(p, t) * below(p, t) + up(p, t) * above(p, t)
            )

        return once(total)

    for i in span["y", 0]:
        edges = d_raw.row(i), c_raw.row(i), w_raw.row(i), w_raw.row(i - 1)
        s = scale.row(i)
        totals = [neighbour_sum(mark.row(i), mark, i, *edges) for mark in marks]
        for t, p in every:
            for f in range(FIELDS):
                y[0][f].put(i, p, t, s(p, t) * totals[f](p, t))

    for i in sorted(set(span["w_row"]) | set(span["w_dep"])):
        s = scale.row(i)
        if i in span["w_row"]:
            after, down = scale.row(i + 1), w_raw.row(i)
            for t, p in every:
                w_row.put(i, p, t, down(p, t) * s(p, t) * after(p, t))
        if i in span["w_dep"]:
            dep, col = d_raw.row(i), c_raw.row(i)
            beyond = shifted(s, 1)
            for t, p in every:
                other = s(1, t) if p == 0 else next_sub(s(0, t))
                w_dep.put(i, p, t, dep(p, t) * s(p, t) * other)
                w_col.put(i, p, t, col(p, t) * s(p, t) * beyond(p, t))

    sums = [list(column) for column in sums]

    def add_products(f, k, a, b):
        total = None
        for t, p in inner:
            part = a(p, t) * b(p, t)
            total = part if total is None else total + part
        sums[f][k] = total if sums[f][k] is None else sums[f][k] + total

    def keep_basis(level, i, values):
        s = scale.row(i)
        for t, p in inner:
            for f in range(FIELDS):
                lanes = slice(t * LANES, (t + 1) * LANES)
                basis[level, f, i - ITERS - basis_first, p, :, lanes] = s(p, t) * values[f](p, t)

    own = range(ITERS, ITERS + rows)
    for i in span["y", 0]:
        if i in own:
            values = [y[0][f].row(i) for f in range(FIELDS)]
            keep_basis(0, i, values)
            for f in range(FIELDS):
                add_products(f, 0, values[f], values[f])
    for level in range(1, ITERS):
        for i in span["y", level]:
            edges = w_dep.row(i), w_col.row(i), w_row.row(i), w_row.row(i - 1)
            olds = [y[level - 1][f].row(i) for f in range(FIELDS)]
            news = [neighbour_sum(olds[f], y[level - 1][f], i, *edges) for f in range(FIELDS)]
            for t, p in every:
                for f in range(FIELDS):
                    y[level][f].put(i, p, t, news[f](p, t))
            if i in own:
                keep_basis(level, i, news)
                for f in range(FIELDS):
                    add_products(f, 2 * level - 1, olds[f], news[f])
                    add_products(f, 2 * level, news[f], news[f])
    for i in span["edge"]:
        dep, col, row = w_dep.row(i), w_col.row(i), w_row.row(i)
        for f in range(FIELDS):
            v, below = y[ITERS - 1][f].row(i), y[ITERS - 1][f].row(i + 1)
            beyond = shifted(v, 1)

            def forward(p, t, v=v, below=below, beyond=beyond):
                lower = v(1, t) if p == 0 else next_sub(v(0, t))
                return dep(p, t) * lower + col(p, t) * beyond(p, t) + row(p, t) * below(p, t)

            add_products(f, MOMENTS - 1, once(forward), v)
    return sums


def halo_tile(lane, before, before_at, after, after_at):
    after_tile = pltpu.roll(after, (LANES - after_at) % LANES, 1) if after_at else after
    shift = (LANES - 8 - before_at) % LANES
    before_tile = pltpu.roll(before, shift, 1) if shift else before
    return jnp.where(lane < 8, after_tile, jnp.where(lane >= LANES - 8, before_tile, 0.0))


def tiles_of(slab, halo):
    cols = slab.shape[-1]
    return [slab[:, at : at + LANES] for at in range(0, cols, LANES)] + [halo]


def corner_tile(lane, ref, kind, parity, row):
    tile = ref[kind, parity]
    place = (8 * row) % (LANES // 2)
    return halo_tile(lane, tile, LANES // 2 + place, tile, place)


def make_stores(rows, refs, earlier=None):
    table = extents(rows)
    stores = {}

    def add(key, name, ref, lead=()):
        first, mid, _ = table[name]
        if earlier is None:
            stores[key] = Rows(ref, first, lead)
        else:
            stores[key] = Rows(ref, mid, lead, earlier.get(key))

    for name in ("image", *WEIGHTS):
        add(name, name, refs[name])
    for f in range(FIELDS):
        add(("mark", f), "mark", refs["mark"], (f,))
        for level in range(ITERS):
            add(("y", level, f), ("y", level), refs["y", level], (f,))
    return stores


STATE = ("image", "mark", *WEIGHTS, *(("y", level) for level in range(ITERS)))


def first_kernel(rows, half, own, label, above, from_left, from_right, corner_above, *refs):
    state = dict(zip(STATE, refs))
    basis, partial = refs[len(STATE) :]

    def fetch(source, kind, before, above_first):
        def parts(i, p, lane):
            row = i - before
            if row < 0:
                halo = corner_tile(lane, corner_above, kind, p, rows + row)
                return tiles_of(above.at[above_first + i, p], halo)
            halo = halo_tile(lane, from_left[kind, p], 8 * row, from_right[kind, p], 8 * row)
            return tiles_of(source.at[row, p], halo)

        return parts

    sums = sweep(
        rows,
        half,
        False,
        fetch(own, 0, IMG_BEFORE, 0),
        fetch(label, 1, SEED_BEFORE, IMG_BEFORE),
        make_stores(rows, state),
        basis,
        0,
        [[None] * MOMENTS] * FIELDS,
    )
    for f in range(FIELDS):
        for k in range(MOMENTS):
            partial[f, k] = sums[f][k]


def second_kernel(rows, half, below, corner_below, *refs):
    earlier = make_stores(rows, dict(zip(STATE, refs)))
    partial = refs[len(STATE)]
    basis, stats = refs[len(STATE) + 1 : len(STATE) + 3]
    state = dict(zip(STATE, refs[len(STATE) + 3 :]))

    def fetch(kind, before, below_first):
        def parts(i, p, lane):
            row = i - before - rows
            return tiles_of(
                below.at[below_first + row, p], corner_tile(lane, corner_below, kind, p, row)
            )

        return parts

    sums = sweep(
        rows,
        half,
        True,
        fetch(0, IMG_BEFORE, 0),
        fetch(1, SEED_BEFORE, IMG_AFTER),
        make_stores(rows, state, earlier),
        basis,
        rows + 2 - 2 * ITERS,
        [[partial[f, k] for k in range(MOMENTS)] for f in range(FIELDS)],
    )
    one_lane = lax.broadcasted_iota(jnp.int32, (1, LANES), 1)
    packed = jnp.zeros((1, LANES), jnp.float32)
    for f in range(FIELDS):
        for k, part in enumerate(sums[f]):
            part = 2.0 * part if k == MOMENTS - 1 else part
            value = jnp.sum(jnp.sum(part, axis=0, keepdims=True), axis=1, keepdims=True)
            packed = jnp.where(one_lane == f * MOMENTS + k, value, packed)
    stats[...] = packed


def combine(a, b):
    out = [None] * (len(a) + len(b) - 1)
    for i, x in enumerate(a):
        for j, z in enumerate(b):
            out[i + j] = x * z if out[i + j] is None else out[i + j] + x * z
    return out


def weighted(coefs, values):
    total = coefs[0] * values[0]
    for c, v in zip(coefs[1:], values[1:]):
        total = total + c * v
    return total


def krylov_coefs(m):
    gaps = [m[k] - m[k + 1] for k in range(MOMENTS - 1)]
    one = jnp.ones_like(m[0])
    zero = jnp.zeros_like(m[0])
    resid, direct, result = [one], [one], [zero] * ITERS
    rz = m[0]
    for k in range(ITERS):
        curve = weighted(combine(direct, direct), gaps)
        alpha = jnp.where(curve > 0.0, rz / curve, 0.0)
        result = [
            result[i] + alpha * direct[i] if i < len(direct) else result[i] for i in range(ITERS)
        ]
        if k + 1 == ITERS:
            break
        image = [
            (direct[i] if i < len(direct) else zero) - (direct[i - 1] if i > 0 else zero)
            for i in range(len(direct) + 1)
        ]
        resid = [(resid[i] if i < len(resid) else zero) - alpha * image[i] for i in range(len(image))]
        rz_next = weighted(combine(resid, resid), m)
        ratio = jnp.where(rz > 0.0, rz_next / rz, 0.0)
        direct = [
            resid[i] + ratio * direct[i] if i < len(direct) else resid[i] for i in range(len(resid))
        ]
        rz = rz_next
    return result


def finish_kernel(rows, half, gathered, basis_one, basis_two, label, out_hbm, out, out_sem):
    core_tiles = out.shape[1]
    total = jnp.sum(gathered[...], axis=0, keepdims=True)
    one_lane = lax.broadcasted_iota(jnp.int32, (1, LANES), 1)
    coefs = []
    for f in range(FIELDS):
        moments = []
        for k in range(MOMENTS):
            pick = jnp.where(one_lane == f * MOMENTS + k, total, 0.0)
            value = jnp.sum(pick, axis=1, keepdims=True)
            moments.append(jnp.broadcast_to(value, (half, LANES)))
        coefs.append(krylov_coefs(moments))
    depth_rows = 2 * half * rows
    second_first = rows + 2 - 2 * ITERS
    copies = []
    for f in range(FIELDS):
        for t in range(core_tiles):
            at = slice(t * LANES, (t + 1) * LANES)
            for row in range(rows):
                for parity in range(2):
                    parts = []
                    for k in range(ITERS):
                        first, mid, _ = extents(rows)["y", k]
                        if row + ITERS < mid:
                            parts.append(basis_one[k, f, row, parity, :, at])
                        else:
                            parts.append(basis_two[k, f, row - second_first, parity, :, at])
                    x = weighted(coefs[f], parts)
                    hit = label[row, parity, :, at] == f + 1.0
                    index = pl.ds(row + rows * parity, half, 2 * rows)
                    out[f, t, index, :] = x + hit.astype(jnp.float32)
            copy = pltpu.make_async_copy(
                out.at[f, t],
                out_hbm.at[pl.ds(f * depth_rows, depth_rows), pl.ds(t * LANES, LANES)],
                out_sem.at[f, t],
            )
            copy.start()
            copies.append(copy)
    for copy in copies:
        copy.wait()


def vmem(count):
    return [pl.BlockSpec(memory_space=pltpu.VMEM)] * count


def hbm(count):
    return [pl.BlockSpec(memory_space=pltpu.HBM)] * count


def on_device(image, seeds):
    depth, rows, cols = image.shape
    half = depth // 2
    wide = cols + LANES
    core_tiles = cols // LANES
    f32 = jnp.float32

    def call(kernel, name, shapes, raw, operands, scratch=(), raw_out=False, mib=16, cost=None):
        return pl.pallas_call(
            lambda *refs: kernel(rows, half, *refs),
            out_shape=[jax.ShapeDtypeStruct(shape, f32) for shape in shapes],
            in_specs=hbm(len(raw)) + vmem(len(operands)),
            out_specs=hbm(len(shapes)) if raw_out else vmem(len(shapes)),
            scratch_shapes=list(scratch),
            compiler_params=pltpu.CompilerParams(vmem_limit_bytes=mib * 1024 * 1024),
            cost_estimate=cost,
            name=name,
        )(*raw, *operands)

    def forward(x, axis):
        return lax.ppermute(x, axis, [(i, i + 1) for i in range(lax.axis_size(axis) - 1)])

    def backward(x, axis):
        return lax.ppermute(x, axis, [(i + 1, i) for i in range(lax.axis_size(axis) - 1)])

    def staged(dtype):
        return pltpu.VMEM((core_tiles, depth * rows, LANES), dtype)

    slabs = (rows, 2, half, cols)
    up, down, own, label = call(
        rows_kernel,
        "own_rows",
        [(UP,) + slabs[1:], (DOWN,) + slabs[1:], slabs, slabs],
        tuple(
            pltpu.with_memory_space_constraint(v.reshape(depth * rows, cols), pltpu.HBM)
            for v in (image, seeds)
        ),
        (),
        [staged(f32), staged(jnp.int32)] + [pltpu.SemaphoreType.DMA((core_tiles,))] * 2,
    )
    above = forward(up, "gy")
    below = backward(down, "gy")
    side = (2, 2, half, LANES)
    even = lax.rem(lax.axis_index("gz"), 2) == 0

    def swap_columns(own, label):
        pair, cross = call(cols_kernel, "own_columns", [side, side], (), (own, label))
        count = lax.axis_size("gz")
        within = [(i, i ^ 1) for i in range(count) if i ^ 1 < count]
        between = [(i, i + 1) for i in range(1, count - 1, 2)]
        pair = lax.ppermute(pair, "gz", within)
        cross = lax.ppermute(cross, "gz", between + [(j, i) for i, j in between])
        left, right = jnp.where(even, cross, pair), jnp.where(even, pair, cross)
        mid = LANES // 2
        corner_up = jnp.concatenate([right[..., mid:], left[..., mid:]], axis=-1)
        corner_down = jnp.concatenate([right[..., :mid], left[..., :mid]], axis=-1)
        return pair, cross, corner_up, corner_down

    def exchange_columns(own, label):
        return swap_columns(own, label)

    pair, cross, corner_up, corner_down = exchange_columns(own, label)
    from_left, from_right = jnp.where(even, cross, pair), jnp.where(even, pair, cross)
    corner_above = forward(corner_up, "gy")
    corner_below = backward(corner_down, "gy")

    table = extents(rows)

    def state_shapes(second):
        shapes = []
        for name in STATE:
            first, mid, stop = table[name]
            count = stop - mid if second else mid - first
            lead = () if name == "image" or name in WEIGHTS else (FIELDS,)
            shapes.append(lead + (count, 2, half, wide))
        return shapes

    second_first = rows + 2 - 2 * ITERS
    basis_rows = (rows + 1 - ITERS, rows - second_first)
    *state, basis_one, partial = call(
        first_kernel,
        "krylov_one",
        state_shapes(False)
        + [(ITERS, FIELDS, basis_rows[0]) + slabs[1:], (FIELDS, MOMENTS, half, LANES)],
        (),
        (own, label, above, from_left, from_right, corner_above),
        cost=pl.CostEstimate(flops=0, bytes_accessed=16 << 20, transcendentals=0),
    )
    basis_two, stats = call(
        second_kernel,
        "krylov_two",
        [(ITERS, FIELDS, basis_rows[1]) + slabs[1:], (1, LANES)],
        (),
        (below, corner_below, *state, partial),
        [pltpu.VMEM(shape, f32) for shape in state_shapes(True)],
    )
    devices = lax.axis_size("gy") * lax.axis_size("gz")
    spread = jnp.broadcast_to(stats[None], (devices, 1, LANES))
    gathered = lax.all_to_all(spread, ("gy", "gz"), 0, 0).reshape(devices, LANES)
    (out,) = call(
        finish_kernel,
        "finish",
        [(FIELDS * depth * rows, cols)],
        (),
        (gathered, basis_one, basis_two, label),
        [
            pltpu.VMEM((FIELDS, core_tiles, depth * rows, LANES), f32),
            pltpu.SemaphoreType.DMA((FIELDS, core_tiles)),
        ],
        raw_out=True,
    )
    return out.reshape(FIELDS, depth, rows, cols)


def solution(mesh):
    return jax.shard_map(
        on_device,
        mesh=mesh,
        in_specs=(P(None, "gy", "gz"), P(None, "gy", "gz")),
        out_specs=P(None, None, "gy", "gz"),
        check_vma=False,
    )
```

time: 61 us -> 47 us (0.77)
  Pallas kernels: 19.3 us -> 11.6 us
  starting transfers between devices: 16.3 us -> 12.7 us
  local copies, waits for them, and re-layouts: 2.24 us -> 0.09 us
  waiting for transfers between devices: 9.61 us -> 7.84 us
  blocking collectives: 12.9 us -> 14.2 us
    pallas_call x4 -> x5, Pallas kernels: 19.3 us -> 11.6 us  [call(): pl.pallas_call(lambda *refs: kernel(rows, half, *refs), out_shape=[jax.Sh...]
    ppermute x3 -> x2, starting transfers between devices: 12.5 us -> 9 us  [forward(): lax.ppermute(x, axis, [(i, i + 1) for i in range(lax.axis_size(axis) - 1)])]
    unnamed x4 -> x0, local copies, waits for them, and re-layouts: 2.08 us -> none
    ppermute x3 -> x2, waiting for transfers between devices: 9.6 us -> 7.83 us  [forward(): lax.ppermute(x, axis, [(i, i + 1) for i in range(lax.axis_size(axis) - 1)])]
    all_to_all x1, blocking collectives: 12.9 us -> 14.2 us  [on_device(): lax.all_to_all(spread, ('gy', 'gz'), 0, 0).reshape(devices, LANES)]
    ppermute x3 -> x2, starting transfers between devices: 3.87 us -> 2.57 us  [backward(): lax.ppermute(x, axis, [(i + 1, i) for i in range(lax.axis_size(axis) - 1)])]
    ppermute x0 -> x2, starting transfers between devices: none -> 1.17 us  [the longest x1 0.65 us: swap_columns(): cross = lax.ppermute(cross, 'gz', between + [(j, i) for i, j in between])]
  transfers between devices with their start and end apart: 6 -> 6, of which waited for: 1 -> 1; matrix products, arithmetic and copies ran while one was open for 0% -> 1% of each run, Pallas kernels for 0% -> 11%
where the time goes in v4:
time: 47 us; the launch traced here: 46.8 us
  blocking collectives  14.2 us (30%)
  starting transfers between devices  12.7 us (27%)
  Pallas kernels  11.6 us (25%)
  waiting for transfers between devices  7.84 us (17%)
    all_to_all x1, blocking collectives, on_device(): lax.all_to_all(spread, ('gy', 'gz'), 0, 0).reshape(devices, LANES)  14.2 us
    pallas_call x5, Pallas kernels, call(): pl.pallas_call(lambda *refs: kernel(rows, half, *refs), out_shape=[jax.Sh...  11.6 us
    ppermute x2, starting transfers between devices, forward(): lax.ppermute(x, axis, [(i, i + 1) for i in range(lax.axis_size(axis) - 1)])  9 us
    ppermute x2, waiting for transfers between devices, forward(): lax.ppermute(x, axis, [(i, i + 1) for i in range(lax.axis_size(axis) - 1)])  7.83 us
    ppermute x2, starting transfers between devices, backward(): lax.ppermute(x, axis, [(i + 1, i) for i in range(lax.axis_size(axis) - 1)])  2.57 us
  transfers between devices with their start and end apart: 6, of which 1 were waited for; matrix products, arithmetic and copies ran while one was open for 1% of the time, Pallas kernels for 11%

profile of v4, /device:TPU:0, one launch (start us, length us, event | category | flops | bytes accessed | tf_op | source)
XLA Modules:
  0.0 46.8 jit_solution(2826696979902272118)
XLA Ops:
  0.0 2.0 %own_rows.1 = (f32[10,2,8,512]{3,2,1,0:T(8,128)S(1)}, f32[12,2,8,512]{3,2,1,0:T(8,128)S(1)}, f32[16,2,8,512]{3,2,1,0:T(8,128)S(1)}, f32[16,2,8,512]{3,2,1,0:T(8,128)S(1)}) custom-call(f32[256,512]{1,0:T(8,128)} %bitcast.7, s32[256,512]{1,0:T(8,128)} %bitcast.8), custom_call_target="tpu_custom_call" | custom-call | tf_op jit(solution)/shard_map/own_rows/pallas_call | solution.py:551
  2.0 0.2 own_columns.1
  2.2 0.5 %collective-permute-start.1 = (f32[2,2,8,128]{3,2,1,0:T(8,128)S(1)}, f32[2,2,8,128]{3,2,1,0:T(8,128)S(1)}, u32[]{:S(2)}, u32[]{:S(2)}) collective-permute-start(f32[2,2,8,128]{3,2,1,0:T(8,128)S(1)} %get-tuple-element.32), channel_id=1, source_target_pairs={{0,1},{1,0},{2,3},{3,2},{4,5},{5,4},{6,7},{7,6},{8,9},{9,8},{10,11... | collective-permute-start | bytes 49160 | tf_op jit(solution)/shard_map/ppermute | solution.py:593
  2.7 0.7 %collective-permute-start.2 = (f32[2,2,8,128]{3,2,1,0:T(8,128)S(1)}, f32[2,2,8,128]{3,2,1,0:T(8,128)S(1)}, u32[]{:S(2)}, u32[]{:S(2)}) collective-permute-start(f32[2,2,8,128]{3,2,1,0:T(8,128)S(1)} %get-tuple-element.33), channel_id=1, source_target_pairs={{1,2},{2,1},{5,6},{6,5},{9,10},{10,9},{13,14},{14,13},{17,18},{18,... | collective-permute-start | bytes 49160 | tf_op jit(solution)/shard_map/ppermute | solution.py:594
  3.4 4.5 %collective-permute-start.4 = (f32[10,2,8,512]{3,2,1,0:T(8,128)S(1)}, f32[10,2,8,512]{3,2,1,0:T(8,128)S(1)}, u32[]{:S(2)}, u32[]{:S(2)}) collective-permute-start(f32[10,2,8,512]{3,2,1,0:T(8,128)S(1)} %get-tuple-element.34), channel_id=1, source_target_pairs={{0,4},{4,8},{8,12},{12,16},{16,20},{20,24},{24,28},{1,5},{5,9},{9,... | collective-permute-start | bytes 983048 | tf_op jit(solution)/shard_map/ppermute | solution.py:563
  7.8 1.3 %collective-permute-start = (f32[12,2,8,512]{3,2,1,0:T(8,128)S(1)}, f32[12,2,8,512]{3,2,1,0:T(8,128)S(1)}, u32[]{:S(2)}, u32[]{:S(2)}) collective-permute-start(f32[12,2,8,512]{3,2,1,0:T(8,128)S(1)} %get-tuple-element.29), channel_id=1, source_target_pairs={{4,0},{8,4},{12,8},{16,12},{20,16},{24,20},{28,24},{5,1},{9,5},{13... | collective-permute-start | bytes 1179656 | tf_op jit(solution)/shard_map/ppermute | solution.py:566
  9.1 0.0 collective-permute-done.1
  9.2 0.0 collective-permute-done.2
  9.2 0.1 fusion
  9.3 0.1 pad_maximum_fusion.1
  9.3 4.5 %collective-permute-start.5 = (f32[2,2,8,128]{3,2,1,0:T(8,128)S(1)}, f32[2,2,8,128]{3,2,1,0:T(8,128)S(1)}, u32[]{:S(2)}, u32[]{:S(2)}) collective-permute-start(f32[2,2,8,128]{3,2,1,0:T(8,128)S(1)} %pad_maximum_fusion.1), channel_id=1, source_target_pairs={{0,4},{4,8},{8,12},{12,16},{16,20},{20,24},{24,28},{1,5},{5,9},{9,... | collective-permute-start | bytes 49160 | tf_op jit(solution)/shard_map/ppermute | solution.py:563
  13.9 0.1 pad_maximum_fusion
  14.0 1.3 %collective-permute-start.3 = (f32[2,2,8,128]{3,2,1,0:T(8,128)S(1)}, f32[2,2,8,128]{3,2,1,0:T(8,128)S(1)}, u32[]{:S(2)}, u32[]{:S(2)}) collective-permute-start(f32[2,2,8,128]{3,2,1,0:T(8,128)S(1)} %pad_maximum_fusion), channel_id=1, source_target_pairs={{4,0},{8,4},{12,8},{16,12},{20,16},{24,20},{28,24},{5,1},{9,5},{13... | collective-permute-start | bytes 49160 | tf_op jit(solution)/shard_map/ppermute | solution.py:566
  15.2 7.8 %collective-permute-done.5.refs_5_ = f32[2,2,8,128]{3,2,1,0:T(8,128)S(1)} collective-permute-done((f32[2,2,8,128]{3,2,1,0:T(8,128)S(1)}, f32[2,2,8,128]{3,2,1,0:T(8,128)S(1)}, u32[]{:S(2)}, u32[]{:S(2)}) %collective-permute-start.5) | collective-permute-done | bytes 16416 | tf_op jit(solution)/shard_map/ppermute | solution.py:563
  23.1 0.0 collective-permute-done.4.refs_2_
  23.1 5.1 %krylov_one.1 = (f32[22,2,8,640]{3,2,1,0:T(8,128)S(1)}, f32[2,20,2,8,640]{4,3,2,1,0:T(8,128)S(1)}, f32[18,2,8,640]{3,2,1,0:T(8,128)S(1)}, f32[17,2,8,640]{3,2,1,...) custom-call(f32[16,2,8,512]{3,2,1,0:T(8,128)S(1)} %get-tuple-element, ...), custom_call_target="tpu_custom_call" | custom-call | bytes 16777216 | tf_op jit(solution)/shard_map/krylov_one/pallas_call | solution.py:551
  28.2 0.0 collective-permute-done.3.refs_1_
  28.2 0.0 collective-permute-done.refs_0_
  28.2 2.5 %krylov_two.1 = (f32[4,2,6,2,8,512]{5,4,3,2,1,0:T(8,128)S(1)}, f32[1,128]{1,0:T(1,128)S(1)}) custom-call(f32[12,2,8,512]{3,2,1,0:T(8,128)S(1)} %collective-permute-done.refs_0_, f32[2,2,8,128]{3,2,1,0:T(8,128)S(1)} %collective-permute-done.3.refs_1_, f32[22,2,8,640]{3,2,1,0:T(8,128)S(1)} %get-tuple-element.35.refs_2_, ...), custom_call_target="tpu_custom_call" | custom-call | tf_op jit(solution)/shard_map/krylov_two/pallas_call | solution.py:551
  30.8 14.2 %all_to_all.5 = f32[32,1,128]{2,1,0:T(1,128)S(1)} all-to-all(f32[32,1,128]{2,1,0:T(1,128)S(1)} %broadcast_in_dim.9), channel_id=1, replica_groups=mesh['gy'=8,'gz'=4] {'gy','gz'}, dimensions={0} | all-to-all | bytes 32768 | tf_op jit(solution)/shard_map/all_to_all | solution.py:641
  45.0 1.8 %finish.1 = f32[512,512]{1,0:T(8,128)} custom-call(f32[32,128]{1,0:T(8,128)S(1)} %bitcast.5, f32[4,2,13,2,8,512]{5,4,3,2,1,0:T(8,128)S(1)} %get-tuple-element.51.refs_1_, f32[4,2,6,2,8,512]{5,4,3,2,1,0:T(8,128)S(1)} %get-tuple-element.52.refs_2_, f32[16,2,8,512]{3,2,1,0:T(8,128)S(1)} %get-tuple-element.31.refs_1_.refs_3_), custom_call_target="tpu_custom_call" | custom-call | tf_op jit(solution)/shard_map/finish/pallas_call | solution.py:551
  (2 shorter events, 0.0 us)
Async XLA Ops:
  2.2 7.0 %collective-permute-start.1 = (f32[2,2,8,128]{3,2,1,0:T(8,128)S(1)}, f32[2,2,8,128]{3,2,1,0:T(8,128)S(1)}, u32[]{:S(2)}, u32[]{:S(2)}) collective-permute-start(f32[2,2,8,128]{3,2,1,0:T(8,128)S(1)} %get-tuple-element.32), channel_id=1, source_target_pairs={{0,1},{1,0},{2,3},{3,2},{4,5},{5,4},{6,7},{7,6},{8,9},{9,8},{10,11... | collective-permute-start | bytes 49160 | tf_op jit(solution)/shard_map/ppermute | solution.py:593
  2.7 6.4 %collective-permute-start.2 = (f32[2,2,8,128]{3,2,1,0:T(8,128)S(1)}, f32[2,2,8,128]{3,2,1,0:T(8,128)S(1)}, u32[]{:S(2)}, u32[]{:S(2)}) collective-permute-start(f32[2,2,8,128]{3,2,1,0:T(8,128)S(1)} %get-tuple-element.33), channel_id=1, source_target_pairs={{1,2},{2,1},{5,6},{6,5},{9,10},{10,9},{13,14},{14,13},{17,18},{18,... | collective-permute-start | bytes 49160 | tf_op jit(solution)/shard_map/ppermute | solution.py:594
  3.4 19.7 %collective-permute-start.4 = (f32[10,2,8,512]{3,2,1,0:T(8,128)S(1)}, f32[10,2,8,512]{3,2,1,0:T(8,128)S(1)}, u32[]{:S(2)}, u32[]{:S(2)}) collective-permute-start(f32[10,2,8,512]{3,2,1,0:T(8,128)S(1)} %get-tuple-element.34), channel_id=1, source_target_pairs={{0,4},{4,8},{8,12},{12,16},{16,20},{20,24},{24,28},{1,5},{5,9},{9,... | collective-permute-start | bytes 983048 | tf_op jit(solution)/shard_map/ppermute | solution.py:563
  7.8 20.4 %collective-permute-start = (f32[12,2,8,512]{3,2,1,0:T(8,128)S(1)}, f32[12,2,8,512]{3,2,1,0:T(8,128)S(1)}, u32[]{:S(2)}, u32[]{:S(2)}) collective-permute-start(f32[12,2,8,512]{3,2,1,0:T(8,128)S(1)} %get-tuple-element.29), channel_id=1, source_target_pairs={{4,0},{8,4},{12,8},{16,12},{20,16},{24,20},{28,24},{5,1},{9,5},{13... | collective-permute-start | bytes 1179656 | tf_op jit(solution)/shard_map/ppermute | solution.py:566
  9.3 13.7 %collective-permute-start.5 = (f32[2,2,8,128]{3,2,1,0:T(8,128)S(1)}, f32[2,2,8,128]{3,2,1,0:T(8,128)S(1)}, u32[]{:S(2)}, u32[]{:S(2)}) collective-permute-start(f32[2,2,8,128]{3,2,1,0:T(8,128)S(1)} %pad_maximum_fusion.1), channel_id=1, source_target_pairs={{0,4},{4,8},{8,12},{12,16},{16,20},{20,24},{24,28},{1,5},{5,9},{9,... | collective-permute-start | bytes 49160 | tf_op jit(solution)/shard_map/ppermute | solution.py:563
  14.0 14.2 %collective-permute-start.3 = (f32[2,2,8,128]{3,2,1,0:T(8,128)S(1)}, f32[2,2,8,128]{3,2,1,0:T(8,128)S(1)}, u32[]{:S(2)}, u32[]{:S(2)}) collective-permute-start(f32[2,2,8,128]{3,2,1,0:T(8,128)S(1)} %pad_maximum_fusion), channel_id=1, source_target_pairs={{4,0},{8,4},{12,8},{16,12},{20,16},{24,20},{28,24},{5,1},{9,5},{13... | collective-permute-start | bytes 49160 | tf_op jit(solution)/shard_map/ppermute | solution.py:566

commit v5 on v4

--- a/solution.py
+++ b/solution.py
@@ -18,6 +18,7 @@
 UP = IMG_BEFORE + SEED_BEFORE
 DOWN = IMG_AFTER + SEED_AFTER
 MOMENTS = 2 * ITERS
+MIDDLE_COST = 10
 
 
 def gauss_taps():
@@ -93,51 +94,63 @@
 
 
 class Rows:
-    def __init__(self, ref, first, lead=(), earlier=None):
-        self.ref, self.first, self.lead, self.earlier = ref, first, lead, earlier
-
-    def place(self, i, parity, t):
+    def __init__(self, pieces, lead=()):
+        self.pieces, self.lead = pieces, lead
+
+    def place(self, start, i, parity, t):
         lanes = slice(t * LANES, (t + 1) * LANES)
-        return (*self.lead, i - self.first, parity, slice(None), lanes)
+        return (*self.lead, i - start, parity, slice(None), lanes)
 
     def row(self, i):
-        if self.earlier is not None and i < self.first:
-            return self.earlier.row(i)
-        return once(lambda parity, t: self.ref[self.place(i, parity, t)])
+        for span, ref in self.pieces:
+            if i in span:
+                return once(lambda parity, t: ref[self.place(span.start, i, parity, t)])
+        raise IndexError(i)
 
     def put(self, i, parity, t, value):
-        self.ref[self.place(i, parity, t)] = value
-
-
+        span, ref = self.pieces[0]
+        if i not in span:
+            raise IndexError(i)
+        ref[self.place(span.start, i, parity, t)] = value
+
+
+MIDDLE, HEAD, TAIL = range(3)
 WEIGHTS = ("smooth", "w_raw", "d_raw", "c_raw", "scale", "w_row", "w_dep", "w_col")
 
 
-def extents(rows):
+def extents(rows, part):
+    low = IMG_BEFORE
     table = {
-        "image": (0, rows + IMG_BEFORE, rows + IMG_BEFORE + IMG_AFTER),
-        "mark": (0, rows + SEED_BEFORE, rows + SEED_BEFORE + SEED_AFTER),
-        "smooth": (0, rows + 2, rows + 2 * ITERS + 1),
-        "w_raw": (0, rows + 1, rows + 2 * ITERS),
-        "d_raw": (1, rows + 2, rows + 2 * ITERS),
-        "c_raw": (1, rows + 2, rows + 2 * ITERS),
-        "scale": (1, rows + 1, rows + 2 * ITERS),
-        "w_row": (1, rows, rows + 2 * ITERS - 1),
-        "w_dep": (2, rows + 1, rows + 2 * ITERS - 1),
-        "w_col": (2, rows + 1, rows + 2 * ITERS - 1),
-        "edge": (ITERS, rows + 1 - ITERS, rows + ITERS),
+        "image": (0, low, rows + IMG_BEFORE, rows + IMG_BEFORE + IMG_AFTER),
+        "mark": (0, SEED_BEFORE, rows + SEED_BEFORE, rows + SEED_BEFORE + SEED_AFTER),
+        "smooth": (0, low, rows + 2, rows + 2 * ITERS + 1),
+        "w_raw": (0, low, rows + 1, rows + 2 * ITERS),
+        "d_raw": (1, low, rows + 2, rows + 2 * ITERS),
+        "c_raw": (1, low, rows + 2, rows + 2 * ITERS),
+        "scale": (1, low + 1, rows + 1, rows + 2 * ITERS),
+        "w_row": (1, low + 1, rows, rows + 2 * ITERS - 1),
+        "w_dep": (2, low + 1, rows + 1, rows + 2 * ITERS - 1),
+        "w_col": (2, low + 1, rows + 1, rows + 2 * ITERS - 1),
+        "edge": (ITERS, low + ITERS, rows + 1 - ITERS, rows + ITERS),
     }
     for level in range(ITERS):
-        table["y", level] = (1 + level, rows + 1 - level, rows + 2 * ITERS - level)
-    return table
-
-
-def sweep(rows, half, second, fetch_image, fetch_seeds, stores, basis, basis_first, sums):
-    span = {
-        name: range(mid, stop) if second else range(first, mid)
-        for name, (first, mid, stop) in extents(rows).items()
+        table["y", level] = (1 + level, low + 1 + level, rows + 1 - level, rows + 2 * ITERS - level)
+    return {
+        name: (range(low, high), range(first, low), range(high, stop))[part]
+        for name, (first, low, high, stop) in table.items()
     }
-    wide = stores["smooth"].ref.shape[-1]
-    tiles = wide // LANES
+
+
+def basis_span(rows, part):
+    spans = [extents(rows, part)["y", level] for level in range(ITERS)]
+    first = max(min(span.start for span in spans), ITERS)
+    return range(first - ITERS, min(max(span.stop for span in spans), rows + ITERS) - ITERS)
+
+
+def sweep(rows, half, part, fetch_image, fetch_seeds, stores, basis, partial):
+    span = extents(rows, part)
+    basis_first = basis_span(rows, part).start
+    tiles = stores["smooth"].pieces[0][1].shape[-1] // LANES
     core_tiles = tiles - 1
     gy, gz = lax.axis_index("gy"), lax.axis_index("gz")
     last_gy, last_gz = lax.axis_size("gy") - 1, lax.axis_size("gz") - 1
@@ -289,7 +302,7 @@
                 w_dep.put(i, p, t, dep(p, t) * s(p, t) * other)
                 w_col.put(i, p, t, col(p, t) * s(p, t) * beyond(p, t))
 
-    sums = [list(column) for column in sums]
+    sums = [[None] * MOMENTS for _ in range(FIELDS)]
 
     def add_products(f, k, a, b):
         total = None
@@ -336,7 +349,9 @@
                 return dep(p, t) * lower + col(p, t) * beyond(p, t) + row(p, t) * below(p, t)
 
             add_products(f, MOMENTS - 1, once(forward), v)
-    return sums
+    for f in range(FIELDS):
+        for k in range(MOMENTS):
+            partial[f, k] = sums[f][k]
 
 
 def halo_tile(lane, before, before_at, after, after_at):
@@ -357,92 +372,79 @@
     return halo_tile(lane, tile, LANES // 2 + place, tile, place)
 
 
-def make_stores(rows, refs, earlier=None):
-    table = extents(rows)
+STATE = ("image", "mark", *WEIGHTS, *(("y", level) for level in range(ITERS)))
+
+
+def make_stores(rows, *parts):
     stores = {}
 
-    def add(key, name, ref, lead=()):
-        first, mid, _ = table[name]
-        if earlier is None:
-            stores[key] = Rows(ref, first, lead)
-        else:
-            stores[key] = Rows(ref, mid, lead, earlier.get(key))
+    def pieces(name):
+        return [(extents(rows, part)[name], refs[STATE.index(name)]) for part, refs in parts]
 
     for name in ("image", *WEIGHTS):
-        add(name, name, refs[name])
+        stores[name] = Rows(pieces(name))
     for f in range(FIELDS):
-        add(("mark", f), "mark", refs["mark"], (f,))
+        stores["mark", f] = Rows(pieces("mark"), (f,))
         for level in range(ITERS):
-            add(("y", level, f), ("y", level), refs["y", level], (f,))
+            stores["y", level, f] = Rows(pieces(("y", level)), (f,))
     return stores
 
 
-STATE = ("image", "mark", *WEIGHTS, *(("y", level) for level in range(ITERS)))
-
-
-def first_kernel(rows, half, own, label, above, from_left, from_right, corner_above, *refs):
-    state = dict(zip(STATE, refs))
-    basis, partial = refs[len(STATE) :]
-
-    def fetch(source, kind, before, above_first):
+def middle_kernel(rows, half, own, label, from_left, from_right, *refs):
+    state, (basis, partial) = refs[: len(STATE)], refs[len(STATE) :]
+
+    def fetch(source, kind, before):
         def parts(i, p, lane):
             row = i - before
-            if row < 0:
-                halo = corner_tile(lane, corner_above, kind, p, rows + row)
-                return tiles_of(above.at[above_first + i, p], halo)
             halo = halo_tile(lane, from_left[kind, p], 8 * row, from_right[kind, p], 8 * row)
             return tiles_of(source.at[row, p], halo)
 
         return parts
 
-    sums = sweep(
-        rows,
-        half,
-        False,
-        fetch(own, 0, IMG_BEFORE, 0),
-        fetch(label, 1, SEED_BEFORE, IMG_BEFORE),
-        make_stores(rows, state),
-        basis,
-        0,
-        [[None] * MOMENTS] * FIELDS,
-    )
-    for f in range(FIELDS):
-        for k in range(MOMENTS):
-            partial[f, k] = sums[f][k]
-
-
-def second_kernel(rows, half, below, corner_below, *refs):
-    earlier = make_stores(rows, dict(zip(STATE, refs)))
-    partial = refs[len(STATE)]
-    basis, stats = refs[len(STATE) + 1 : len(STATE) + 3]
-    state = dict(zip(STATE, refs[len(STATE) + 3 :]))
-
-    def fetch(kind, before, below_first):
+    images, labels = fetch(own, 0, IMG_BEFORE), fetch(label, 1, SEED_BEFORE)
+    stores = make_stores(rows, (MIDDLE, state))
+    sweep(rows, half, MIDDLE, images, labels, stores, basis, partial)
+
+
+def head_kernel(rows, half, above, corner_above, *refs):
+    count = len(STATE)
+    middle, (basis, partial), state = refs[:count], refs[count : count + 2], refs[count + 2 :]
+
+    def fetch(kind, before, first):
+        def parts(i, p, lane):
+            halo = corner_tile(lane, corner_above, kind, p, rows + i - before)
+            return tiles_of(above.at[first + i, p], halo)
+
+        return parts
+
+    images, labels = fetch(0, IMG_BEFORE, 0), fetch(1, SEED_BEFORE, IMG_BEFORE)
+    stores = make_stores(rows, (HEAD, state), (MIDDLE, middle))
+    sweep(rows, half, HEAD, images, labels, stores, basis, partial)
+
+
+def tail_kernel(rows, half, below, corner_below, *refs):
+    count = len(STATE)
+    middle, refs = refs[:count], refs[count:]
+    (others, (basis, stats), partial), state = (refs[:2], refs[2:4], refs[4]), refs[5:]
+
+    def fetch(kind, before, first):
         def parts(i, p, lane):
             row = i - before - rows
-            return tiles_of(
-                below.at[below_first + row, p], corner_tile(lane, corner_below, kind, p, row)
-            )
+            halo = corner_tile(lane, corner_below, kind, p, row)
+            return tiles_of(below.at[first + row, p], halo)
 
         return parts
 
-    sums = sweep(
-        rows,
-        half,
-        True,
-        fetch(0, IMG_BEFORE, 0),
-        fetch(1, SEED_BEFORE, IMG_AFTER),
-        make_stores(rows, state, earlier),
-        basis,
-        rows + 2 - 2 * ITERS,
-        [[partial[f, k] for k in range(MOMENTS)] for f in range(FIELDS)],
-    )
+    images, labels = fetch(0, IMG_BEFORE, 0), fetch(1, SEED_BEFORE, IMG_AFTER)
+    stores = make_stores(rows, (TAIL, state), (MIDDLE, middle))
+    sweep(rows, half, TAIL, images, labels, stores, basis, partial)
     one_lane = lax.broadcasted_iota(jnp.int32, (1, LANES), 1)
     packed = jnp.zeros((1, LANES), jnp.float32)
     for f in range(FIELDS):
-        for k, part in enumerate(sums[f]):
-            part = 2.0 * part if k == MOMENTS - 1 else part
-            value = jnp.sum(jnp.sum(part, axis=0, keepdims=True), axis=1, keepdims=True)
+        for k in range(MOMENTS):
+            whole = partial[f, k] + others[0][f, k] + others[1][f, k]
+            whole = 2.0 * whole if k == MOMENTS - 1 else whole
+            value = jnp.sum(jnp.sum(whole, axis=0, keepdims=True), axis=1, keepdims=True)
             packed = jnp.where(one_lane == f * MOMENTS + k, value, packed)
     stats[...] = packed
 
@@ -490,7 +492,7 @@
     return result
 
 
-def finish_kernel(rows, half, gathered, basis_one, basis_two, label, out_hbm, out, out_sem):
+def finish_kernel(rows, half, gathered, middle, head, tail, label, out_hbm, out, out_sem):
     core_tiles = out.shape[1]
     total = jnp.sum(gathered[...], axis=0, keepdims=True)
     one_lane = lax.broadcasted_iota(jnp.int32, (1, LANES), 1)
@@ -503,7 +505,6 @@
             moments.append(jnp.broadcast_to(value, (half, LANES)))
         coefs.append(krylov_coefs(moments))
     depth_rows = 2 * half * rows
-    second_first = rows + 2 - 2 * ITERS
     copies = []
     for f in range(FIELDS):
         for t in range(core_tiles):
@@ -512,11 +513,10 @@
                 for parity in range(2):
                     parts = []
                     for k in range(ITERS):
-                        first, mid, _ = extents(rows)["y", k]
-                        if row + ITERS < mid:
-                            parts.append(basis_one[k, f, row, parity, :, at])
-                        else:
-                            parts.append(basis_two[k, f, row - second_first, parity, :, at])
+                        for part, basis in enumerate((middle, head, tail)):
+                            if row + ITERS in extents(rows, part)["y", k]:
+                                place = row - basis_span(rows, part).start
+                                parts.append(basis[k, f, place, parity, :, at])
                     x = weighted(coefs[f], parts)
                     hit = label[row, parity, :, at] == f + 1.0
                     index = pl.ds(row + rows * parity, half, 2 * rows)
@@ -606,35 +606,44 @@
     corner_above = forward(corner_up, "gy")
     corner_below = backward(corner_down, "gy")
 
-    table = extents(rows)
-
-    def state_shapes(second):
+    def state_shapes(part):
         shapes = []
         for name in STATE:
-            first, mid, stop = table[name]
-            count = stop - mid if second else mid - first
             lead = () if name == "image" or name in WEIGHTS else (FIELDS,)
-            shapes.append(lead + (count, 2, half, wide))
+            shapes.append(lead + (len(extents(rows, part)[name]), 2, half, wide))
         return shapes
 
-    second_first = rows + 2 - 2 * ITERS
-    basis_rows = (rows + 1 - ITERS, rows - second_first)
-    *state, basis_one, partial = call(
-        first_kernel,
-        "krylov_one",
-        state_shapes(False)
-        + [(ITERS, FIELDS, basis_rows[0]) + slabs[1:], (FIELDS, MOMENTS, half, LANES)],
+    def basis_shape(part):
+        return (ITERS, FIELDS, len(basis_span(rows, part))) + slabs[1:]
+
+    def scratch(part):
+        return [pltpu.VMEM(shape, f32) for shape in state_shapes(part)]
+
+    sums = (FIELDS, MOMENTS, half, LANES)
+    *state, basis_middle, sums_middle = call(
+        middle_kernel,
+        "middle",
+        state_shapes(MIDDLE) + [basis_shape(MIDDLE), sums],
         (),
-        (own, label, above, from_left, from_right, corner_above),
-        cost=pl.CostEstimate(flops=0, bytes_accessed=16 << 20, transcendentals=0),
+        (own, label, from_left, from_right),
+        cost=pl.CostEstimate(flops=0, bytes_accessed=MIDDLE_COST << 20, transcendentals=0),
     )
-    basis_two, stats = call(
-        second_kernel,
-        "krylov_two",
-        [(ITERS, FIELDS, basis_rows[1]) + slabs[1:], (1, LANES)],
+    basis_head, sums_head = call(
+        head_kernel,
+        "head",
+        [basis_shape(HEAD), sums],
         (),
-        (below, corner_below, *state, partial),
-        [pltpu.VMEM(shape, f32) for shape in state_shapes(True)],
+        (above, corner_above, *state),
+        scratch(HEAD),
+        cost=pl.CostEstimate(flops=0, bytes_accessed=8 << 20, transcendentals=0),
+    )
+    basis_tail, stats = call(
+        tail_kernel,
+        "tail",
+        [basis_shape(TAIL), (1, LANES)],
+        (),
+        (below, corner_below, *state, sums_middle, sums_head),
+        [pltpu.VMEM(sums, f32)] + scratch(TAIL),
     )
     devices = lax.axis_size("gy") * lax.axis_size("gz")
     spread = jnp.broadcast_to(stats[None], (devices, 1, LANES))
@@ -644,7 +653,7 @@
         "finish",
         [(FIELDS * depth * rows, cols)],
         (),
-        (gathered, basis_one, basis_two, label),
+        (gathered, basis_middle, basis_head, basis_tail, label),
         [
             pltpu.VMEM((FIELDS, core_tiles, depth * rows, LANES), f32),
             pltpu.SemaphoreType.DMA((FIELDS, core_tiles)),

time: 47 us -> 44 us (0.936)
  waiting for transfers between devices: 7.84 us -> 4.82 us
    ppermute x2, waiting for transfers between devices: 7.83 us -> 4.81 us  [forward(): lax.ppermute(x, axis, [(i, i + 1) for i in range(lax.axis_size(axis) - 1)])]
    pallas_call x5 -> x6, Pallas kernels: 11.6 us -> 11.5 us  [call(): pl.pallas_call(lambda *refs: kernel(rows, half, *refs), out_shape=[jax.Sh...]
  transfers between devices with their start and end apart: 6 -> 6, of which waited for: 1 -> 1; matrix products, arithmetic and copies ran while one was open for 1% -> 1% of each run, Pallas kernels for 11% -> 12%
where the time goes in v5:
time: 44 us; the launch traced here: 43.7 us
  blocking collectives  14.2 us (32%)
  starting transfers between devices  12.7 us (29%)
  Pallas kernels  11.5 us (26%)
  waiting for transfers between devices  4.82 us (11%)
    all_to_all x1, blocking collectives, on_device(): lax.all_to_all(spread, ('gy', 'gz'), 0, 0).reshape(devices, LANES)  14.2 us
    pallas_call x6, Pallas kernels, call(): pl.pallas_call(lambda *refs: kernel(rows, half, *refs), out_shape=[jax.Sh...  11.5 us
    ppermute x2, starting transfers between devices, forward(): lax.ppermute(x, axis, [(i, i + 1) for i in range(lax.axis_size(axis) - 1)])  9 us
    ppermute x2, waiting for transfers between devices, forward(): lax.ppermute(x, axis, [(i, i + 1) for i in range(lax.axis_size(axis) - 1)])  4.81 us
    ppermute x2, starting transfers between devices, backward(): lax.ppermute(x, axis, [(i + 1, i) for i in range(lax.axis_size(axis) - 1)])  2.57 us
  transfers between devices with their start and end apart: 6, of which 1 were waited for; matrix products, arithmetic and copies ran while one was open for 1% of the time, Pallas kernels for 12%

profile of v5, /device:TPU:0, one launch (start us, length us, event | category | flops | bytes accessed | tf_op | source)
XLA Modules:
  0.0 43.7 jit_solution(9413342609637298256)
XLA Ops:
  0.0 2.0 %own_rows.1 = (f32[10,2,8,512]{3,2,1,0:T(8,128)S(1)}, f32[12,2,8,512]{3,2,1,0:T(8,128)S(1)}, f32[16,2,8,512]{3,2,1,0:T(8,128)S(1)}, f32[16,2,8,512]{3,2,1,0:T(8,128)S(1)}) custom-call(f32[256,512]{1,0:T(8,128)} %bitcast.7, s32[256,512]{1,0:T(8,128)} %bitcast.8), custom_call_target="tpu_custom_call" | custom-call | tf_op jit(solution)/shard_map/own_rows/pallas_call | solution.py:551
  2.0 0.2 own_columns.1
  2.2 0.5 %collective-permute-start.1 = (f32[2,2,8,128]{3,2,1,0:T(8,128)S(1)}, f32[2,2,8,128]{3,2,1,0:T(8,128)S(1)}, u32[]{:S(2)}, u32[]{:S(2)}) collective-permute-start(f32[2,2,8,128]{3,2,1,0:T(8,128)S(1)} %get-tuple-element.34), channel_id=1, source_target_pairs={{0,1},{1,0},{2,3},{3,2},{4,5},{5,4},{6,7},{7,6},{8,9},{9,8},{10,11... | collective-permute-start | bytes 49160 | tf_op jit(solution)/shard_map/ppermute | solution.py:593
  2.7 0.7 %collective-permute-start.2 = (f32[2,2,8,128]{3,2,1,0:T(8,128)S(1)}, f32[2,2,8,128]{3,2,1,0:T(8,128)S(1)}, u32[]{:S(2)}, u32[]{:S(2)}) collective-permute-start(f32[2,2,8,128]{3,2,1,0:T(8,128)S(1)} %get-tuple-element.35), channel_id=1, source_target_pairs={{1,2},{2,1},{5,6},{6,5},{9,10},{10,9},{13,14},{14,13},{17,18},{18,... | collective-permute-start | bytes 49160 | tf_op jit(solution)/shard_map/ppermute | solution.py:594
  3.4 4.5 %collective-permute-start.4 = (f32[10,2,8,512]{3,2,1,0:T(8,128)S(1)}, f32[10,2,8,512]{3,2,1,0:T(8,128)S(1)}, u32[]{:S(2)}, u32[]{:S(2)}) collective-permute-start(f32[10,2,8,512]{3,2,1,0:T(8,128)S(1)} %get-tuple-element.51), channel_id=1, source_target_pairs={{0,4},{4,8},{8,12},{12,16},{16,20},{20,24},{24,28},{1,5},{5,9},{9,... | collective-permute-start | bytes 983048 | tf_op jit(solution)/shard_map/ppermute | solution.py:563
  7.8 1.3 %collective-permute-start = (f32[12,2,8,512]{3,2,1,0:T(8,128)S(1)}, f32[12,2,8,512]{3,2,1,0:T(8,128)S(1)}, u32[]{:S(2)}, u32[]{:S(2)}) collective-permute-start(f32[12,2,8,512]{3,2,1,0:T(8,128)S(1)} %get-tuple-element.31), channel_id=1, source_target_pairs={{4,0},{8,4},{12,8},{16,12},{20,16},{24,20},{28,24},{5,1},{9,5},{13... | collective-permute-start | bytes 1179656 | tf_op jit(solution)/shard_map/ppermute | solution.py:566
  9.1 0.0 collective-permute-done.1
  9.2 0.0 collective-permute-done.2
  9.2 0.1 fusion
  9.3 0.1 pad_maximum_fusion.1
  9.3 4.5 %collective-permute-start.5 = (f32[2,2,8,128]{3,2,1,0:T(8,128)S(1)}, f32[2,2,8,128]{3,2,1,0:T(8,128)S(1)}, u32[]{:S(2)}, u32[]{:S(2)}) collective-permute-start(f32[2,2,8,128]{3,2,1,0:T(8,128)S(1)} %pad_maximum_fusion.1), channel_id=1, source_target_pairs={{0,4},{4,8},{8,12},{12,16},{16,20},{20,24},{24,28},{1,5},{5,9},{9,... | collective-permute-start | bytes 49160 | tf_op jit(solution)/shard_map/ppermute | solution.py:563
  13.9 0.1 pad_maximum_fusion
  14.0 1.3 %collective-permute-start.3 = (f32[2,2,8,128]{3,2,1,0:T(8,128)S(1)}, f32[2,2,8,128]{3,2,1,0:T(8,128)S(1)}, u32[]{:S(2)}, u32[]{:S(2)}) collective-permute-start(f32[2,2,8,128]{3,2,1,0:T(8,128)S(1)} %pad_maximum_fusion), channel_id=1, source_target_pairs={{4,0},{8,4},{12,8},{16,12},{20,16},{24,20},{28,24},{5,1},{9,5},{13... | collective-permute-start | bytes 49160 | tf_op jit(solution)/shard_map/ppermute | solution.py:566
  15.2 3.0 %middle.1 = (f32[16,2,8,640]{3,2,1,0:T(8,128)S(1)}, f32[2,16,2,8,640]{4,3,2,1,0:T(8,128)S(1)}, f32[12,2,8,640]{3,2,1,0:T(8,128)S(1)}, f32[11,2,8,640]{3,2,1,0:T(...) custom-call(f32[16,2,8,512]{3,2,1,0:T(8,128)S(1)} %get-tuple-element, ...), custom_call_target="tpu_custom_call" | custom-call | bytes 10485760 | tf_op jit(solution)/shard_map/middle/pallas_call | solution.py:551
  18.3 4.8 %collective-permute-done.5.refs_1_ = f32[2,2,8,128]{3,2,1,0:T(8,128)S(1)} collective-permute-done((f32[2,2,8,128]{3,2,1,0:T(8,128)S(1)}, f32[2,2,8,128]{3,2,1,0:T(8,128)S(1)}, u32[]{:S(2)}, u32[]{:S(2)}) %collective-permute-start.5) | collective-permute-done | bytes 16416 | tf_op jit(solution)/shard_map/ppermute | solution.py:563
  23.1 0.0 collective-permute-done.4.refs_0_
  23.1 2.1 %head.1 = (f32[4,2,6,2,8,512]{5,4,3,2,1,0:T(8,128)S(1)}, f32[2,8,8,128]{3,2,1,0:T(8,128)S(1)}) custom-call(f32[10,2,8,512]{3,2,1,0:T(8,128)S(1)} %collective-permute-done.4.refs_0_, f32[2,2,8,128]{3,2,1,0:T(8,128)S(1)} %collective-permute-done.5.refs_1_, f32[16,2,8,640]{3,2,1,0:T(8,128)S(1)} %get-tuple-element.36.refs_2_, ...), custom_call_target="tpu_custom_call" | custom-call | bytes 8388608 | tf_op jit(solution)/shard_map/head/pallas_call | solution.py:551
  25.2 0.0 collective-permute-done.3.refs_1_
  25.2 0.0 collective-permute-done.refs_0_
  25.2 2.5 %tail.1 = (f32[4,2,6,2,8,512]{5,4,3,2,1,0:T(8,128)S(1)}, f32[1,128]{1,0:T(1,128)S(1)}) custom-call(f32[12,2,8,512]{3,2,1,0:T(8,128)S(1)} %collective-permute-done.refs_0_, f32[2,2,8,128]{3,2,1,0:T(8,128)S(1)} %collective-permute-done.3.refs_1_, f32[16,2,8,640]{3,2,1,0:T(8,128)S(1)} %get-tuple-element.36.refs_2_, ...), custom_call_target="tpu_custom_call" | custom-call | tf_op jit(solution)/shard_map/tail/pallas_call | solution.py:551
  27.7 14.2 %all_to_all.5 = f32[32,1,128]{2,1,0:T(1,128)S(1)} all-to-all(f32[32,1,128]{2,1,0:T(1,128)S(1)} %broadcast_in_dim.9), channel_id=1, replica_groups=mesh['gy'=8,'gz'=4] {'gy','gz'}, dimensions={0} | all-to-all | bytes 32768 | tf_op jit(solution)/shard_map/all_to_all | solution.py:650
  41.9 1.8 %finish.1 = f32[512,512]{1,0:T(8,128)} custom-call(f32[32,128]{1,0:T(8,128)S(1)} %bitcast.5, f32[4,2,10,2,8,512]{5,4,3,2,1,0:T(8,128)S(1)} %get-tuple-element.54.refs_1_, f32[4,2,6,2,8,512]{5,4,3,2,1,0:T(8,128)S(1)} %get-tuple-element.55.refs_2_, f32[4,2,6,2,8,512]{5,4,3,2,1,0:T(8,128)S(1)} %get-tuple-element.56.refs_3_, ...), custom_call_target="tpu_custom_call" | custom-call | tf_op jit(solution)/shard_map/finish/pallas_call | solution.py:551
  (2 shorter events, 0.0 us)
Async XLA Ops:
  2.2 7.0 %collective-permute-start.1 = (f32[2,2,8,128]{3,2,1,0:T(8,128)S(1)}, f32[2,2,8,128]{3,2,1,0:T(8,128)S(1)}, u32[]{:S(2)}, u32[]{:S(2)}) collective-permute-start(f32[2,2,8,128]{3,2,1,0:T(8,128)S(1)} %get-tuple-element.34), channel_id=1, source_target_pairs={{0,1},{1,0},{2,3},{3,2},{4,5},{5,4},{6,7},{7,6},{8,9},{9,8},{10,11... | collective-permute-start | bytes 49160 | tf_op jit(solution)/shard_map/ppermute | solution.py:593
  2.7 6.4 %collective-permute-start.2 = (f32[2,2,8,128]{3,2,1,0:T(8,128)S(1)}, f32[2,2,8,128]{3,2,1,0:T(8,128)S(1)}, u32[]{:S(2)}, u32[]{:S(2)}) collective-permute-start(f32[2,2,8,128]{3,2,1,0:T(8,128)S(1)} %get-tuple-element.35), channel_id=1, source_target_pairs={{1,2},{2,1},{5,6},{6,5},{9,10},{10,9},{13,14},{14,13},{17,18},{18,... | collective-permute-start | bytes 49160 | tf_op jit(solution)/shard_map/ppermute | solution.py:594
  3.4 19.7 %collective-permute-start.4 = (f32[10,2,8,512]{3,2,1,0:T(8,128)S(1)}, f32[10,2,8,512]{3,2,1,0:T(8,128)S(1)}, u32[]{:S(2)}, u32[]{:S(2)}) collective-permute-start(f32[10,2,8,512]{3,2,1,0:T(8,128)S(1)} %get-tuple-element.51), channel_id=1, source_target_pairs={{0,4},{4,8},{8,12},{12,16},{16,20},{20,24},{24,28},{1,5},{5,9},{9,... | collective-permute-start | bytes 983048 | tf_op jit(solution)/shard_map/ppermute | solution.py:563
  7.8 17.3 %collective-permute-start = (f32[12,2,8,512]{3,2,1,0:T(8,128)S(1)}, f32[12,2,8,512]{3,2,1,0:T(8,128)S(1)}, u32[]{:S(2)}, u32[]{:S(2)}) collective-permute-start(f32[12,2,8,512]{3,2,1,0:T(8,128)S(1)} %get-tuple-element.31), channel_id=1, source_target_pairs={{4,0},{8,4},{12,8},{16,12},{20,16},{24,20},{28,24},{5,1},{9,5},{13... | collective-permute-start | bytes 1179656 | tf_op jit(solution)/shard_map/ppermute | solution.py:566
  9.3 13.7 %collective-permute-start.5 = (f32[2,2,8,128]{3,2,1,0:T(8,128)S(1)}, f32[2,2,8,128]{3,2,1,0:T(8,128)S(1)}, u32[]{:S(2)}, u32[]{:S(2)}) collective-permute-start(f32[2,2,8,128]{3,2,1,0:T(8,128)S(1)} %pad_maximum_fusion.1), channel_id=1, source_target_pairs={{0,4},{4,8},{8,12},{12,16},{16,20},{20,24},{24,28},{1,5},{5,9},{9,... | collective-permute-start | bytes 49160 | tf_op jit(solution)/shard_map/ppermute | solution.py:563
  14.0 11.2 %collective-permute-start.3 = (f32[2,2,8,128]{3,2,1,0:T(8,128)S(1)}, f32[2,2,8,128]{3,2,1,0:T(8,128)S(1)}, u32[]{:S(2)}, u32[]{:S(2)}) collective-permute-start(f32[2,2,8,128]{3,2,1,0:T(8,128)S(1)} %pad_maximum_fusion), channel_id=1, source_target_pairs={{4,0},{8,4},{12,8},{16,12},{20,16},{24,20},{28,24},{5,1},{9,5},{13... | collective-permute-start | bytes 49160 | tf_op jit(solution)/shard_map/ppermute | solution.py:566

commit v6 on v5

--- a/solution.py
+++ b/solution.py
@@ -27,39 +27,37 @@
     return [value / total for value in raw]
 
 
-def slab_of(ref, row, parity, rows, half):
-    index = pl.ds(row + rows * parity, half, 2 * rows)
-    return jnp.concatenate([ref[t, index, :] for t in range(ref.shape[0])], axis=1)
-
-
-def stage(pairs):
+def rows_kernel(rows, half, image_hbm, seeds_hbm, up, down, own, label, image, seeds, image_sem, seeds_sem):
+    sources = ((image_hbm, image, image_sem), (seeds_hbm, seeds, seeds_sem))
     copies = [
-        pltpu.make_async_copy(source.at[:, pl.ds(t * LANES, LANES)], staged.at[t], sems.at[t])
-        for source, staged, sems in pairs
-        for t in range(staged.shape[0])
+        [
+            pltpu.make_async_copy(source.at[:, pl.ds(t * LANES, LANES)], staged.at[t], sems.at[t])
+            for source, staged, sems in sources
+        ]
+        for t in range(image.shape[0])
     ]
-    for copy in copies:
-        copy.start()
-    for copy in copies:
-        copy.wait()
-
-
-def rows_kernel(rows, half, image_hbm, seeds_hbm, up, down, own, label, image, seeds, image_sem, seeds_sem):
-    stage([(image_hbm, image, image_sem), (seeds_hbm, seeds, seeds_sem)])
-    for row in range(rows):
-        for parity in range(2):
-            grey = slab_of(image, row, parity, rows, half)
-            seed = slab_of(seeds, row, parity, rows, half).astype(jnp.float32)
-            own[row, parity] = grey
-            label[row, parity] = seed
-            if row >= rows - IMG_BEFORE:
-                up[row - (rows - IMG_BEFORE), parity] = grey
-            if row >= rows - SEED_BEFORE:
-                up[IMG_BEFORE + row - (rows - SEED_BEFORE), parity] = seed
-            if row < IMG_AFTER:
-                down[row, parity] = grey
-            if row < SEED_AFTER:
-                down[IMG_AFTER + row, parity] = seed
+    for pair in copies:
+        for copy in pair:
+            copy.start()
+    for t, pair in enumerate(copies):
+        at = slice(t * LANES, (t + 1) * LANES)
+        for copy in pair:
+            copy.wait()
+        for row in range(rows):
+            for parity in range(2):
+                index = pl.ds(row + rows * parity, half, 2 * rows)
+                grey = image[t, index, :]
+                seed = seeds[t, index, :].astype(jnp.float32)
+                own[row, parity, :, at] = grey
+                label[row, parity, :, at] = seed
+                if row >= rows - IMG_BEFORE:
+                    up[row - (rows - IMG_BEFORE), parity, :, at] = grey
+                if row >= rows - SEED_BEFORE:
+                    up[IMG_BEFORE + row - (rows - SEED_BEFORE), parity, :, at] = seed
+                if row < IMG_AFTER:
+                    down[row, parity, :, at] = grey
+                if row < SEED_AFTER:
+                    down[IMG_AFTER + row, parity, :, at] = seed
 
 
 def cols_kernel(rows, half, own, label, pair, cross):

time: 44 us -> 43.6 us (level)
  no operation moved by 1% of the time
where the time goes in v6:
time: 43.6 us; the launch traced here: 43.4 us
  blocking collectives  14.2 us (33%)
  starting transfers between devices  12.7 us (29%)
  Pallas kernels  11.2 us (26%)
  waiting for transfers between devices  4.82 us (11%)
    all_to_all x1, blocking collectives, on_device(): lax.all_to_all(spread, ('gy', 'gz'), 0, 0).reshape(devices, LANES)  14.2 us
    pallas_call x6, Pallas kernels, call(): pl.pallas_call(lambda *refs: kernel(rows, half, *refs), out_shape=[jax.Sh...  11.2 us
    ppermute x2, starting transfers between devices, forward(): lax.ppermute(x, axis, [(i, i + 1) for i in range(lax.axis_size(axis) - 1)])  9 us
    ppermute x2, waiting for transfers between devices, forward(): lax.ppermute(x, axis, [(i, i + 1) for i in range(lax.axis_size(axis) - 1)])  4.81 us
    ppermute x2, starting transfers between devices, backward(): lax.ppermute(x, axis, [(i + 1, i) for i in range(lax.axis_size(axis) - 1)])  2.57 us
  transfers between devices with their start and end apart: 6, of which 1 were waited for; matrix products, arithmetic and copies ran while one was open for 1% of the time, Pallas kernels for 12%

profile of v6, /device:TPU:0, one launch (start us, length us, event | category | flops | bytes accessed | tf_op | source)
XLA Modules:
  0.0 43.4 jit_solution(3345365156069572200)
XLA Ops:
  0.0 1.7 %own_rows.1 = (f32[10,2,8,512]{3,2,1,0:T(8,128)S(1)}, f32[12,2,8,512]{3,2,1,0:T(8,128)S(1)}, f32[16,2,8,512]{3,2,1,0:T(8,128)S(1)}, f32[16,2,8,512]{3,2,1,0:T(8,128)S(1)}) custom-call(f32[256,512]{1,0:T(8,128)} %bitcast.7, s32[256,512]{1,0:T(8,128)} %bitcast.8), custom_call_target="tpu_custom_call" | custom-call | tf_op jit(solution)/shard_map/own_rows/pallas_call | solution.py:549
  1.7 0.2 own_columns.1
  1.9 0.5 %collective-permute-start.1 = (f32[2,2,8,128]{3,2,1,0:T(8,128)S(1)}, f32[2,2,8,128]{3,2,1,0:T(8,128)S(1)}, u32[]{:S(2)}, u32[]{:S(2)}) collective-permute-start(f32[2,2,8,128]{3,2,1,0:T(8,128)S(1)} %get-tuple-element.34), channel_id=1, source_target_pairs={{0,1},{1,0},{2,3},{3,2},{4,5},{5,4},{6,7},{7,6},{8,9},{9,8},{10,11... | collective-permute-start | bytes 49160 | tf_op jit(solution)/shard_map/ppermute | solution.py:591
  2.4 0.7 %collective-permute-start.2 = (f32[2,2,8,128]{3,2,1,0:T(8,128)S(1)}, f32[2,2,8,128]{3,2,1,0:T(8,128)S(1)}, u32[]{:S(2)}, u32[]{:S(2)}) collective-permute-start(f32[2,2,8,128]{3,2,1,0:T(8,128)S(1)} %get-tuple-element.35), channel_id=1, source_target_pairs={{1,2},{2,1},{5,6},{6,5},{9,10},{10,9},{13,14},{14,13},{17,18},{18,... | collective-permute-start | bytes 49160 | tf_op jit(solution)/shard_map/ppermute | solution.py:592
  3.1 4.5 %collective-permute-start.4 = (f32[10,2,8,512]{3,2,1,0:T(8,128)S(1)}, f32[10,2,8,512]{3,2,1,0:T(8,128)S(1)}, u32[]{:S(2)}, u32[]{:S(2)}) collective-permute-start(f32[10,2,8,512]{3,2,1,0:T(8,128)S(1)} %get-tuple-element.51), channel_id=1, source_target_pairs={{0,4},{4,8},{8,12},{12,16},{16,20},{20,24},{24,28},{1,5},{5,9},{9,... | collective-permute-start | bytes 983048 | tf_op jit(solution)/shard_map/ppermute | solution.py:561
  7.5 1.3 %collective-permute-start = (f32[12,2,8,512]{3,2,1,0:T(8,128)S(1)}, f32[12,2,8,512]{3,2,1,0:T(8,128)S(1)}, u32[]{:S(2)}, u32[]{:S(2)}) collective-permute-start(f32[12,2,8,512]{3,2,1,0:T(8,128)S(1)} %get-tuple-element.31), channel_id=1, source_target_pairs={{4,0},{8,4},{12,8},{16,12},{20,16},{24,20},{28,24},{5,1},{9,5},{13... | collective-permute-start | bytes 1179656 | tf_op jit(solution)/shard_map/ppermute | solution.py:564
  8.8 0.0 collective-permute-done.1
  8.8 0.0 collective-permute-done.2
  8.9 0.1 fusion
  8.9 0.1 pad_maximum_fusion.1
  9.0 4.5 %collective-permute-start.5 = (f32[2,2,8,128]{3,2,1,0:T(8,128)S(1)}, f32[2,2,8,128]{3,2,1,0:T(8,128)S(1)}, u32[]{:S(2)}, u32[]{:S(2)}) collective-permute-start(f32[2,2,8,128]{3,2,1,0:T(8,128)S(1)} %pad_maximum_fusion.1), channel_id=1, source_target_pairs={{0,4},{4,8},{8,12},{12,16},{16,20},{20,24},{24,28},{1,5},{5,9},{9,... | collective-permute-start | bytes 49160 | tf_op jit(solution)/shard_map/ppermute | solution.py:561
  13.6 0.1 pad_maximum_fusion
  13.6 1.3 %collective-permute-start.3 = (f32[2,2,8,128]{3,2,1,0:T(8,128)S(1)}, f32[2,2,8,128]{3,2,1,0:T(8,128)S(1)}, u32[]{:S(2)}, u32[]{:S(2)}) collective-permute-start(f32[2,2,8,128]{3,2,1,0:T(8,128)S(1)} %pad_maximum_fusion), channel_id=1, source_target_pairs={{4,0},{8,4},{12,8},{16,12},{20,16},{24,20},{28,24},{5,1},{9,5},{13... | collective-permute-start | bytes 49160 | tf_op jit(solution)/shard_map/ppermute | solution.py:564
  14.9 3.0 %middle.1 = (f32[16,2,8,640]{3,2,1,0:T(8,128)S(1)}, f32[2,16,2,8,640]{4,3,2,1,0:T(8,128)S(1)}, f32[12,2,8,640]{3,2,1,0:T(8,128)S(1)}, f32[11,2,8,640]{3,2,1,0:T(...) custom-call(f32[16,2,8,512]{3,2,1,0:T(8,128)S(1)} %get-tuple-element, ...), custom_call_target="tpu_custom_call" | custom-call | bytes 10485760 | tf_op jit(solution)/shard_map/middle/pallas_call | solution.py:549
  18.0 4.8 %collective-permute-done.5.refs_1_ = f32[2,2,8,128]{3,2,1,0:T(8,128)S(1)} collective-permute-done((f32[2,2,8,128]{3,2,1,0:T(8,128)S(1)}, f32[2,2,8,128]{3,2,1,0:T(8,128)S(1)}, u32[]{:S(2)}, u32[]{:S(2)}) %collective-permute-start.5) | collective-permute-done | bytes 16416 | tf_op jit(solution)/shard_map/ppermute | solution.py:561
  22.8 0.0 collective-permute-done.4.refs_0_
  22.8 2.1 %head.1 = (f32[4,2,6,2,8,512]{5,4,3,2,1,0:T(8,128)S(1)}, f32[2,8,8,128]{3,2,1,0:T(8,128)S(1)}) custom-call(f32[10,2,8,512]{3,2,1,0:T(8,128)S(1)} %collective-permute-done.4.refs_0_, f32[2,2,8,128]{3,2,1,0:T(8,128)S(1)} %collective-permute-done.5.refs_1_, f32[16,2,8,640]{3,2,1,0:T(8,128)S(1)} %get-tuple-element.36.refs_2_, ...), custom_call_target="tpu_custom_call" | custom-call | bytes 8388608 | tf_op jit(solution)/shard_map/head/pallas_call | solution.py:549
  24.9 0.0 collective-permute-done.3.refs_1_
  24.9 0.0 collective-permute-done.refs_0_
  24.9 2.5 %tail.1 = (f32[4,2,6,2,8,512]{5,4,3,2,1,0:T(8,128)S(1)}, f32[1,128]{1,0:T(1,128)S(1)}) custom-call(f32[12,2,8,512]{3,2,1,0:T(8,128)S(1)} %collective-permute-done.refs_0_, f32[2,2,8,128]{3,2,1,0:T(8,128)S(1)} %collective-permute-done.3.refs_1_, f32[16,2,8,640]{3,2,1,0:T(8,128)S(1)} %get-tuple-element.36.refs_2_, ...), custom_call_target="tpu_custom_call" | custom-call | tf_op jit(solution)/shard_map/tail/pallas_call | solution.py:549
  27.4 14.2 %all_to_all.5 = f32[32,1,128]{2,1,0:T(1,128)S(1)} all-to-all(f32[32,1,128]{2,1,0:T(1,128)S(1)} %broadcast_in_dim.9), channel_id=1, replica_groups=mesh['gy'=8,'gz'=4] {'gy','gz'}, dimensions={0} | all-to-all | bytes 32768 | tf_op jit(solution)/shard_map/all_to_all | solution.py:648
  41.6 1.8 %finish.1 = f32[512,512]{1,0:T(8,128)} custom-call(f32[32,128]{1,0:T(8,128)S(1)} %bitcast.5, f32[4,2,10,2,8,512]{5,4,3,2,1,0:T(8,128)S(1)} %get-tuple-element.54.refs_1_, f32[4,2,6,2,8,512]{5,4,3,2,1,0:T(8,128)S(1)} %get-tuple-element.55.refs_2_, f32[4,2,6,2,8,512]{5,4,3,2,1,0:T(8,128)S(1)} %get-tuple-element.56.refs_3_, ...), custom_call_target="tpu_custom_call" | custom-call | tf_op jit(solution)/shard_map/finish/pallas_call | solution.py:549
  (2 shorter events, 0.0 us)
Async XLA Ops:
  1.9 7.0 %collective-permute-start.1 = (f32[2,2,8,128]{3,2,1,0:T(8,128)S(1)}, f32[2,2,8,128]{3,2,1,0:T(8,128)S(1)}, u32[]{:S(2)}, u32[]{:S(2)}) collective-permute-start(f32[2,2,8,128]{3,2,1,0:T(8,128)S(1)} %get-tuple-element.34), channel_id=1, source_target_pairs={{0,1},{1,0},{2,3},{3,2},{4,5},{5,4},{6,7},{7,6},{8,9},{9,8},{10,11... | collective-permute-start | bytes 49160 | tf_op jit(solution)/shard_map/ppermute | solution.py:591
  2.4 6.4 %collective-permute-start.2 = (f32[2,2,8,128]{3,2,1,0:T(8,128)S(1)}, f32[2,2,8,128]{3,2,1,0:T(8,128)S(1)}, u32[]{:S(2)}, u32[]{:S(2)}) collective-permute-start(f32[2,2,8,128]{3,2,1,0:T(8,128)S(1)} %get-tuple-element.35), channel_id=1, source_target_pairs={{1,2},{2,1},{5,6},{6,5},{9,10},{10,9},{13,14},{14,13},{17,18},{18,... | collective-permute-start | bytes 49160 | tf_op jit(solution)/shard_map/ppermute | solution.py:592
  3.1 19.7 %collective-permute-start.4 = (f32[10,2,8,512]{3,2,1,0:T(8,128)S(1)}, f32[10,2,8,512]{3,2,1,0:T(8,128)S(1)}, u32[]{:S(2)}, u32[]{:S(2)}) collective-permute-start(f32[10,2,8,512]{3,2,1,0:T(8,128)S(1)} %get-tuple-element.51), channel_id=1, source_target_pairs={{0,4},{4,8},{8,12},{12,16},{16,20},{20,24},{24,28},{1,5},{5,9},{9,... | collective-permute-start | bytes 983048 | tf_op jit(solution)/shard_map/ppermute | solution.py:561
  7.5 17.3 %collective-permute-start = (f32[12,2,8,512]{3,2,1,0:T(8,128)S(1)}, f32[12,2,8,512]{3,2,1,0:T(8,128)S(1)}, u32[]{:S(2)}, u32[]{:S(2)}) collective-permute-start(f32[12,2,8,512]{3,2,1,0:T(8,128)S(1)} %get-tuple-element.31), channel_id=1, source_target_pairs={{4,0},{8,4},{12,8},{16,12},{20,16},{24,20},{28,24},{5,1},{9,5},{13... | collective-permute-start | bytes 1179656 | tf_op jit(solution)/shard_map/ppermute | solution.py:564
  9.0 13.7 %collective-permute-start.5 = (f32[2,2,8,128]{3,2,1,0:T(8,128)S(1)}, f32[2,2,8,128]{3,2,1,0:T(8,128)S(1)}, u32[]{:S(2)}, u32[]{:S(2)}) collective-permute-start(f32[2,2,8,128]{3,2,1,0:T(8,128)S(1)} %pad_maximum_fusion.1), channel_id=1, source_target_pairs={{0,4},{4,8},{8,12},{12,16},{16,20},{20,24},{24,28},{1,5},{5,9},{9,... | collective-permute-start | bytes 49160 | tf_op jit(solution)/shard_map/ppermute | solution.py:561
  13.6 11.2 %collective-permute-start.3 = (f32[2,2,8,128]{3,2,1,0:T(8,128)S(1)}, f32[2,2,8,128]{3,2,1,0:T(8,128)S(1)}, u32[]{:S(2)}, u32[]{:S(2)}) collective-permute-start(f32[2,2,8,128]{3,2,1,0:T(8,128)S(1)} %pad_maximum_fusion), channel_id=1, source_target_pairs={{4,0},{8,4},{12,8},{16,12},{20,16},{24,20},{28,24},{5,1},{9,5},{13... | collective-permute-start | bytes 49160 | tf_op jit(solution)/shard_map/ppermute | solution.py:564

commit v7 on v6

--- a/solution.py
+++ b/solution.py
@@ -153,6 +153,7 @@
     gy, gz = lax.axis_index("gy"), lax.axis_index("gz")
     last_gy, last_gz = lax.axis_size("gy") - 1, lax.axis_size("gz") - 1
     t0, t1, t2 = gauss_taps()[:3]
+    sharp = math.sqrt(EDGE_BETA / math.log(2.0))
     lane = lax.broadcasted_iota(jnp.int32, (half, LANES), 1)
     sub = lax.broadcasted_iota(jnp.int32, (half, LANES), 0)
     not_first = (sub > 0).astype(jnp.float32)
@@ -214,9 +215,9 @@
             (
                 p,
                 t,
-                t0 * (far_next(p, t) + far_prev(p, t))
-                + t1 * (near_next(p, t) + near_prev(p, t))
-                + t2 * deep(p, t),
+                sharp * t0 * (far_next(p, t) + far_prev(p, t))
+                + sharp * t1 * (near_next(p, t) + near_prev(p, t))
+                + sharp * t2 * deep(p, t),
             )
             for t, p in every
         ]
@@ -229,7 +230,7 @@
     }
 
     def weight(step):
-        return EDGE_FLOOR + jnp.exp((-EDGE_BETA * step) * step)
+        return EDGE_FLOOR + jnp.exp2(-(step * step))
 
     cut_row = {
         ITERS - 1: jnp.where(gy == 0, 0.0, 1.0),

time: 43.6 us -> 43.6 us (level)
  no operation moved by 1% of the time
where the time goes in v7:
time: 43.6 us; the launch traced here: 43.4 us
  blocking collectives  14.2 us (33%)
  starting transfers between devices  12.7 us (29%)
  Pallas kernels  11.2 us (26%)
  waiting for transfers between devices  4.87 us (11%)
    all_to_all x1, blocking collectives, on_device(): lax.all_to_all(spread, ('gy', 'gz'), 0, 0).reshape(devices, LANES)  14.2 us
    pallas_call x6, Pallas kernels, call(): pl.pallas_call(lambda *refs: kernel(rows, half, *refs), out_shape=[jax.Sh...  11.2 us
    ppermute x2, starting transfers between devices, forward(): lax.ppermute(x, axis, [(i, i + 1) for i in range(lax.axis_size(axis) - 1)])  9 us
    ppermute x2, waiting for transfers between devices, forward(): lax.ppermute(x, axis, [(i, i + 1) for i in range(lax.axis_size(axis) - 1)])  4.86 us
    ppermute x2, starting transfers between devices, backward(): lax.ppermute(x, axis, [(i + 1, i) for i in range(lax.axis_size(axis) - 1)])  2.57 us
  transfers between devices with their start and end apart: 6, of which 1 were waited for; matrix products, arithmetic and copies ran while one was open for 1% of the time, Pallas kernels for 12%

profile of v7, /device:TPU:0, one launch (start us, length us, event | category | flops | bytes accessed | tf_op | source)
XLA Modules:
  0.0 43.4 jit_solution(10087507748439739113)
XLA Ops:
  0.0 1.7 %own_rows.1 = (f32[10,2,8,512]{3,2,1,0:T(8,128)S(1)}, f32[12,2,8,512]{3,2,1,0:T(8,128)S(1)}, f32[16,2,8,512]{3,2,1,0:T(8,128)S(1)}, f32[16,2,8,512]{3,2,1,0:T(8,128)S(1)}) custom-call(f32[256,512]{1,0:T(8,128)} %bitcast.7, s32[256,512]{1,0:T(8,128)} %bitcast.8), custom_call_target="tpu_custom_call" | custom-call | tf_op jit(solution)/shard_map/own_rows/pallas_call | solution.py:550
  1.7 0.2 own_columns.1
  1.9 0.5 %collective-permute-start.1 = (f32[2,2,8,128]{3,2,1,0:T(8,128)S(1)}, f32[2,2,8,128]{3,2,1,0:T(8,128)S(1)}, u32[]{:S(2)}, u32[]{:S(2)}) collective-permute-start(f32[2,2,8,128]{3,2,1,0:T(8,128)S(1)} %get-tuple-element.34), channel_id=1, source_target_pairs={{0,1},{1,0},{2,3},{3,2},{4,5},{5,4},{6,7},{7,6},{8,9},{9,8},{10,11... | collective-permute-start | bytes 49160 | tf_op jit(solution)/shard_map/ppermute | solution.py:592
  2.4 0.7 %collective-permute-start.2 = (f32[2,2,8,128]{3,2,1,0:T(8,128)S(1)}, f32[2,2,8,128]{3,2,1,0:T(8,128)S(1)}, u32[]{:S(2)}, u32[]{:S(2)}) collective-permute-start(f32[2,2,8,128]{3,2,1,0:T(8,128)S(1)} %get-tuple-element.35), channel_id=1, source_target_pairs={{1,2},{2,1},{5,6},{6,5},{9,10},{10,9},{13,14},{14,13},{17,18},{18,... | collective-permute-start | bytes 49160 | tf_op jit(solution)/shard_map/ppermute | solution.py:593
  3.1 4.5 %collective-permute-start.4 = (f32[10,2,8,512]{3,2,1,0:T(8,128)S(1)}, f32[10,2,8,512]{3,2,1,0:T(8,128)S(1)}, u32[]{:S(2)}, u32[]{:S(2)}) collective-permute-start(f32[10,2,8,512]{3,2,1,0:T(8,128)S(1)} %get-tuple-element.51), channel_id=1, source_target_pairs={{0,4},{4,8},{8,12},{12,16},{16,20},{20,24},{24,28},{1,5},{5,9},{9,... | collective-permute-start | bytes 983048 | tf_op jit(solution)/shard_map/ppermute | solution.py:562
  7.5 1.3 %collective-permute-start = (f32[12,2,8,512]{3,2,1,0:T(8,128)S(1)}, f32[12,2,8,512]{3,2,1,0:T(8,128)S(1)}, u32[]{:S(2)}, u32[]{:S(2)}) collective-permute-start(f32[12,2,8,512]{3,2,1,0:T(8,128)S(1)} %get-tuple-element.31), channel_id=1, source_target_pairs={{4,0},{8,4},{12,8},{16,12},{20,16},{24,20},{28,24},{5,1},{9,5},{13... | collective-permute-start | bytes 1179656 | tf_op jit(solution)/shard_map/ppermute | solution.py:565
  8.8 0.0 collective-permute-done.1
  8.8 0.0 collective-permute-done.2
  8.9 0.1 fusion
  8.9 0.1 pad_maximum_fusion.1
  9.0 4.5 %collective-permute-start.5 = (f32[2,2,8,128]{3,2,1,0:T(8,128)S(1)}, f32[2,2,8,128]{3,2,1,0:T(8,128)S(1)}, u32[]{:S(2)}, u32[]{:S(2)}) collective-permute-start(f32[2,2,8,128]{3,2,1,0:T(8,128)S(1)} %pad_maximum_fusion.1), channel_id=1, source_target_pairs={{0,4},{4,8},{8,12},{12,16},{16,20},{20,24},{24,28},{1,5},{5,9},{9,... | collective-permute-start | bytes 49160 | tf_op jit(solution)/shard_map/ppermute | solution.py:562
  13.6 0.1 pad_maximum_fusion
  13.6 1.3 %collective-permute-start.3 = (f32[2,2,8,128]{3,2,1,0:T(8,128)S(1)}, f32[2,2,8,128]{3,2,1,0:T(8,128)S(1)}, u32[]{:S(2)}, u32[]{:S(2)}) collective-permute-start(f32[2,2,8,128]{3,2,1,0:T(8,128)S(1)} %pad_maximum_fusion), channel_id=1, source_target_pairs={{4,0},{8,4},{12,8},{16,12},{20,16},{24,20},{28,24},{5,1},{9,5},{13... | collective-permute-start | bytes 49160 | tf_op jit(solution)/shard_map/ppermute | solution.py:565
  14.9 3.0 %middle.1 = (f32[16,2,8,640]{3,2,1,0:T(8,128)S(1)}, f32[2,16,2,8,640]{4,3,2,1,0:T(8,128)S(1)}, f32[12,2,8,640]{3,2,1,0:T(8,128)S(1)}, f32[11,2,8,640]{3,2,1,0:T(...) custom-call(f32[16,2,8,512]{3,2,1,0:T(8,128)S(1)} %get-tuple-element, ...), custom_call_target="tpu_custom_call" | custom-call | bytes 10485760 | tf_op jit(solution)/shard_map/middle/pallas_call | solution.py:550
  17.9 4.9 %collective-permute-done.5.refs_1_ = f32[2,2,8,128]{3,2,1,0:T(8,128)S(1)} collective-permute-done((f32[2,2,8,128]{3,2,1,0:T(8,128)S(1)}, f32[2,2,8,128]{3,2,1,0:T(8,128)S(1)}, u32[]{:S(2)}, u32[]{:S(2)}) %collective-permute-start.5) | collective-permute-done | bytes 16416 | tf_op jit(solution)/shard_map/ppermute | solution.py:562
  22.8 0.0 collective-permute-done.4.refs_0_
  22.8 2.1 %head.1 = (f32[4,2,6,2,8,512]{5,4,3,2,1,0:T(8,128)S(1)}, f32[2,8,8,128]{3,2,1,0:T(8,128)S(1)}) custom-call(f32[10,2,8,512]{3,2,1,0:T(8,128)S(1)} %collective-permute-done.4.refs_0_, f32[2,2,8,128]{3,2,1,0:T(8,128)S(1)} %collective-permute-done.5.refs_1_, f32[16,2,8,640]{3,2,1,0:T(8,128)S(1)} %get-tuple-element.36.refs_2_, ...), custom_call_target="tpu_custom_call" | custom-call | bytes 8388608 | tf_op jit(solution)/shard_map/head/pallas_call | solution.py:550
  24.9 0.0 collective-permute-done.3.refs_1_
  24.9 0.0 collective-permute-done.refs_0_
  24.9 2.5 %tail.1 = (f32[4,2,6,2,8,512]{5,4,3,2,1,0:T(8,128)S(1)}, f32[1,128]{1,0:T(1,128)S(1)}) custom-call(f32[12,2,8,512]{3,2,1,0:T(8,128)S(1)} %collective-permute-done.refs_0_, f32[2,2,8,128]{3,2,1,0:T(8,128)S(1)} %collective-permute-done.3.refs_1_, f32[16,2,8,640]{3,2,1,0:T(8,128)S(1)} %get-tuple-element.36.refs_2_, ...), custom_call_target="tpu_custom_call" | custom-call | tf_op jit(solution)/shard_map/tail/pallas_call | solution.py:550
  27.4 14.2 %all_to_all.5 = f32[32,1,128]{2,1,0:T(1,128)S(1)} all-to-all(f32[32,1,128]{2,1,0:T(1,128)S(1)} %broadcast_in_dim.9), channel_id=1, replica_groups=mesh['gy'=8,'gz'=4] {'gy','gz'}, dimensions={0} | all-to-all | bytes 32768 | tf_op jit(solution)/shard_map/all_to_all | solution.py:649
  41.6 1.8 %finish.1 = f32[512,512]{1,0:T(8,128)} custom-call(f32[32,128]{1,0:T(8,128)S(1)} %bitcast.5, f32[4,2,10,2,8,512]{5,4,3,2,1,0:T(8,128)S(1)} %get-tuple-element.54.refs_1_, f32[4,2,6,2,8,512]{5,4,3,2,1,0:T(8,128)S(1)} %get-tuple-element.55.refs_2_, f32[4,2,6,2,8,512]{5,4,3,2,1,0:T(8,128)S(1)} %get-tuple-element.56.refs_3_, ...), custom_call_target="tpu_custom_call" | custom-call | tf_op jit(solution)/shard_map/finish/pallas_call | solution.py:550
  (2 shorter events, 0.0 us)
Async XLA Ops:
  1.9 7.0 %collective-permute-start.1 = (f32[2,2,8,128]{3,2,1,0:T(8,128)S(1)}, f32[2,2,8,128]{3,2,1,0:T(8,128)S(1)}, u32[]{:S(2)}, u32[]{:S(2)}) collective-permute-start(f32[2,2,8,128]{3,2,1,0:T(8,128)S(1)} %get-tuple-element.34), channel_id=1, source_target_pairs={{0,1},{1,0},{2,3},{3,2},{4,5},{5,4},{6,7},{7,6},{8,9},{9,8},{10,11... | collective-permute-start | bytes 49160 | tf_op jit(solution)/shard_map/ppermute | solution.py:592
  2.4 6.4 %collective-permute-start.2 = (f32[2,2,8,128]{3,2,1,0:T(8,128)S(1)}, f32[2,2,8,128]{3,2,1,0:T(8,128)S(1)}, u32[]{:S(2)}, u32[]{:S(2)}) collective-permute-start(f32[2,2,8,128]{3,2,1,0:T(8,128)S(1)} %get-tuple-element.35), channel_id=1, source_target_pairs={{1,2},{2,1},{5,6},{6,5},{9,10},{10,9},{13,14},{14,13},{17,18},{18,... | collective-permute-start | bytes 49160 | tf_op jit(solution)/shard_map/ppermute | solution.py:593
  3.1 19.7 %collective-permute-start.4 = (f32[10,2,8,512]{3,2,1,0:T(8,128)S(1)}, f32[10,2,8,512]{3,2,1,0:T(8,128)S(1)}, u32[]{:S(2)}, u32[]{:S(2)}) collective-permute-start(f32[10,2,8,512]{3,2,1,0:T(8,128)S(1)} %get-tuple-element.51), channel_id=1, source_target_pairs={{0,4},{4,8},{8,12},{12,16},{16,20},{20,24},{24,28},{1,5},{5,9},{9,... | collective-permute-start | bytes 983048 | tf_op jit(solution)/shard_map/ppermute | solution.py:562
  7.5 17.3 %collective-permute-start = (f32[12,2,8,512]{3,2,1,0:T(8,128)S(1)}, f32[12,2,8,512]{3,2,1,0:T(8,128)S(1)}, u32[]{:S(2)}, u32[]{:S(2)}) collective-permute-start(f32[12,2,8,512]{3,2,1,0:T(8,128)S(1)} %get-tuple-element.31), channel_id=1, source_target_pairs={{4,0},{8,4},{12,8},{16,12},{20,16},{24,20},{28,24},{5,1},{9,5},{13... | collective-permute-start | bytes 1179656 | tf_op jit(solution)/shard_map/ppermute | solution.py:565
  9.0 13.7 %collective-permute-start.5 = (f32[2,2,8,128]{3,2,1,0:T(8,128)S(1)}, f32[2,2,8,128]{3,2,1,0:T(8,128)S(1)}, u32[]{:S(2)}, u32[]{:S(2)}) collective-permute-start(f32[2,2,8,128]{3,2,1,0:T(8,128)S(1)} %pad_maximum_fusion.1), channel_id=1, source_target_pairs={{0,4},{4,8},{8,12},{12,16},{16,20},{20,24},{24,28},{1,5},{5,9},{9,... | collective-permute-start | bytes 49160 | tf_op jit(solution)/shard_map/ppermute | solution.py:562
  13.6 11.2 %collective-permute-start.3 = (f32[2,2,8,128]{3,2,1,0:T(8,128)S(1)}, f32[2,2,8,128]{3,2,1,0:T(8,128)S(1)}, u32[]{:S(2)}, u32[]{:S(2)}) collective-permute-start(f32[2,2,8,128]{3,2,1,0:T(8,128)S(1)} %pad_maximum_fusion), channel_id=1, source_target_pairs={{4,0},{8,4},{12,8},{16,12},{20,16},{24,20},{28,24},{5,1},{9,5},{13... | collective-permute-start | bytes 49160 | tf_op jit(solution)/shard_map/ppermute | solution.py:565
